TPU v7x, 32 devices: a whole 2x2x4 slice. The times are simulated.
32 devices in a mesh: dp: 8 (over z, x), tensor: 4 (over y, core).
Axes of the slice: x: 2, y: 2, z: 4, core: 2. Of those that a mesh axis runs over, the one named last changes fastest.
Arguments:
- tokens: bfloat16 [8, 1024, 768], P('dp', 'tensor'), may hold values from -6 to 6
- row_lengths: int32 [8], P('dp'), may hold values from 769 to 1024, as said below
- instruction_mask: int32 [8, 1024], P('dp', 'tensor'), may hold values from 0 to 1, as said below
- task_groups: int32 [8], replicated, may hold values from 0 to 3
- rel_buckets: int32 [2047], replicated, may hold values from 0 to 31
- gain_attn: float32 [768], replicated, may hold values from 0.5 to 1.5
- w_query: bfloat16 [768, 768], P(None, 'tensor'), may hold values from -0.109375 to 0.109375
- w_key: bfloat16 [768, 768], P(None, 'tensor'), may hold values from -0.109375 to 0.109375
- w_value: bfloat16 [768, 768], P(None, 'tensor'), may hold values from -0.21875 to 0.21875
- rel_table: float32 [32, 12], P(None, 'tensor'), may hold values from -4 to 4
- w_out: bfloat16 [768, 768], P('tensor'), may hold values from -0.875 to 0.875
- gain_ffn: float32 [768], replicated, may hold values from 0.5 to 1.5
- w_in: bfloat16 [768, 3072], P(None, 'tensor'), may hold values from -0.21875 to 0.21875
- w_back: bfloat16 [3072, 768], P('tensor'), may hold values from -0.15625 to 0.15625
- out_grad: bfloat16 [8, 1024, 768], P('dp', 'tensor'), may hold values from -6 to 6
Outputs:
- mixed: bfloat16 [8, 1024, 768], P('dp', 'tensor')
- grad_tokens: float32 [8, 1024, 768], P('dp', 'tensor')
- grad_gain_attn: float32 [768], replicated
- grad_query: float32 [768, 768], P(None, 'tensor')
- grad_key: float32 [768, 768], P(None, 'tensor')
- grad_value: float32 [768, 768], P(None, 'tensor')
- grad_table: float32 [32, 12], P(None, 'tensor')
- grad_out: float32 [768, 768], P('tensor')
- grad_gain_ffn: float32 [768], replicated
- grad_in: float32 [768, 3072], P(None, 'tensor')
- grad_back: float32 [3072, 768], P('tensor')
Inputs may be any that keep to these rules, and one draw needn't show every extreme that they name: `row_lengths`: in each aligned block of 1 row one row is longer than 768; some row has length 1024. `instruction_mask`: the ones of each row form a prefix of 1 to 128 positions.
All inputs are finite; a program needn't handle non-finite values.
Results may differ from a plain program's by a relative error of at most 0.017.
Values may be sent and summed in bfloat16 or wider, within the bound.
No kernel may reach another device: no remote copies, remote signals or barrier semaphores. Data moves between devices by JAX's collectives and lax.ppermute only.
A program may use at most 192 MiB of HBM per device.

v0:
```python
import functools

import jax
import jax.numpy as jnp
from jax import lax
from jax.experimental import pallas as pl
from jax.experimental.pallas import tpu as pltpu
from jax.sharding import PartitionSpec as P

NORM_EPS = 1e-06
MASK_FILL = -1000000000.0
F32 = jnp.float32
BF16 = jnp.bfloat16
LANES = 128
FREE = jax.ShapeDtypeStruct
FAR = pltpu.HBM
HEAVY = pl.CostEstimate(flops=10**11, bytes_accessed=1024, transcendentals=0)
LIGHT = pl.CostEstimate(flops=1024, bytes_accessed=1024, transcendentals=0)
GELU_SCALE = 0.7978845608028654
GELU_CUBE = 0.044715


def dot_nn(left, right):
    return jnp.dot(left, right, preferred_element_type=F32)


def dot_nt(left, right):
    return lax.dot_general(left, right, (((1,), (1,)), ((), ())), preferred_element_type=F32)


def dot_tn(left, right):
    return lax.dot_general(left, right, (((0,), (0,)), ((), ())), preferred_element_type=F32)


def vmem_whole(shape):
    return pl.BlockSpec(shape, lambda i: (0,) * len(shape))


class Came:
    def __init__(self, array):
        self.array = array


def local_call(kernel, *, out_shape, grid, in_specs, out_specs, scratch_shapes=(), prefetch=0, mib, name, cost=LIGHT):
    def place(value, spec):
        if isinstance(value, Came):
            return value.array
        if value.ndim < 2 or spec.memory_space is pltpu.SMEM:
            return value
        return pltpu.with_memory_space_constraint(value, pltpu.HBM)

    def run(*args):
        given = [place(value, spec) for value, spec in zip(args[prefetch:], in_specs, strict=True)]
        return call(*args[:prefetch], *given)

    call = pl.pallas_call(
        kernel,
        grid_spec=pltpu.PrefetchScalarGridSpec(
            num_scalar_prefetch=prefetch,
            grid=grid,
            in_specs=in_specs,
            out_specs=out_specs,
            scratch_shapes=scratch_shapes,
        ),
        out_shape=out_shape,
        compiler_params=pltpu.CompilerParams(vmem_limit_bytes=mib << 20),
        cost_estimate=cost,
        name=name,
    )
    return run


class Turn:
    def __init__(self):
        self.last = None

    def __call__(self, value):
        if self.last is None:
            return value
        return lax.optimization_barrier((value, self.last))[0]

    def done(self, value):
        self.last = value[0] if isinstance(value, (list, tuple)) else value
        return value


def block_order(count):
    order = [0]
    bit = count // 2
    while bit:
        order = order + [slot | bit for slot in order]
        bit //= 2
    return order


def tensor_bits(count):
    bits = []
    bit = count // 2
    while bit:
        bits.append(bit)
        bit //= 2
    return bits


def swap_tensor(value, bit):
    size = lax.axis_size("tensor")
    return lax.ppermute(value, "tensor", [(i, i ^ bit) for i in range(size)])


def gather_tensor(value, count, ready=()):
    slots = [value]
    for bit in tensor_bits(count):
        came = [swap_tensor(piece, bit) for piece in slots]
        if ready:
            came, ready = lax.optimization_barrier((came, ready))
        slots = slots + came
    return slots, ready


def scatter_tensor(value, count, bits=None):
    for bit in reversed(tensor_bits(count) if bits is None else bits):
        half = value.shape[0] // 2
        came = swap_tensor(value[half:], bit)
        value = (value[:half].astype(F32) + came.astype(F32)).astype(BF16)
    return value


def dp_steps(count):
    bits = []
    bit = 1
    while bit < count:
        bits.append(bit)
        bit *= 2
    return list(zip(bits, bits[1::-1] + bits[2:], strict=True))


def swap_dp(value, pair):
    rows, cols = lax.axis_size("dp"), lax.axis_size("tensor")
    route = []
    for row in range(rows):
        for col in range(cols):
            route.append((row * cols + col, (row ^ pair[col % 2]) * cols + col))
    return lax.ppermute(value, ("dp", "tensor"), route)


def side_of(pair):
    row, col = lax.axis_index("dp"), lax.axis_index("tensor")
    bit = jnp.where(col % 2 == 1, pair[1], pair[0])
    return ((row & bit) != 0).astype(jnp.int32)[None]


def add_kernel(left_ref, right_ref, out_ref):
    total = left_ref[...].astype(F32) + right_ref[...].astype(F32)
    out_ref[...] = total.astype(out_ref.dtype)


def add(left, right, cost=LIGHT):
    return local_call(
        add_kernel,
        grid=(1,),
        in_specs=[vmem_whole(left.shape)] * 2,
        out_specs=vmem_whole(left.shape),
        out_shape=FAR(left.shape, left.dtype),
        mib=8,
        name="add",
        cost=cost,
    )(left, Came(right))


def add_pieces_kernel(count, *refs):
    step = pl.program_id(0)
    for k in range(count):

        @pl.when(step == k)
        def _():
            total = refs[0][...].astype(F32) + refs[1][...].astype(F32)
            refs[2 + k][...] = total.astype(BF16)


def add_pieces(left, right, count):
    rows, cols = left.shape
    part = pl.BlockSpec((rows // count, cols), lambda i: (i, 0))
    return local_call(
        functools.partial(add_pieces_kernel, count),
        grid=(count,),
        in_specs=[part, part],
        out_specs=[vmem_whole((rows // count, cols))] * count,
        out_shape=[FAR((rows // count, cols), BF16)] * count,
        mib=10,
        name="add_pieces",
    )(left, Came(right))


def add_swap_kernel(left_ref, right_ref, plain_ref, swapped_ref):
    total = (left_ref[...].astype(F32) + right_ref[...].astype(F32)).astype(BF16)
    plain_ref[...] = total
    swapped_ref[...] = total


def add_swap(left, right, count, flip):
    rows, cols = left.shape
    part = pl.BlockSpec((rows // count, cols), lambda i: (i, 0))
    return local_call(
        add_swap_kernel,
        grid=(count,),
        in_specs=[part, part],
        out_specs=[part, pl.BlockSpec((rows // count, cols), lambda i: (i ^ flip, 0))],
        out_shape=[FAR((rows, cols), BF16), FREE((rows, cols), BF16)],
        mib=10,
        name="add_swap",
    )(left, Came(right))


def fold_kernel(side_ref, kept_ref, came_ref, send_ref, keep_ref):
    total = (kept_ref[...].astype(F32) + came_ref[...].astype(F32)).astype(BF16)

    @pl.when(pl.program_id(0) == 0)
    def _():
        send_ref[...] = total

    @pl.when(pl.program_id(0) == 1)
    def _():
        keep_ref[...] = total


def fold(side, kept, came, cost=LIGHT):
    rows, cols = kept.shape
    half = rows // 2
    if half % 16:
        total = (kept.astype(F32) + came.astype(F32)).astype(BF16)
        return [lax.dynamic_slice_in_dim(total, k * half, half) for k in (1 - side[0], side[0])]
    place = pl.BlockSpec((half, cols), lambda i, side: (jnp.where(i == 0, 1 - side[0], side[0]), 0))
    whole = pl.BlockSpec((half, cols), lambda i, side: (0, 0))
    return local_call(
        fold_kernel,
        grid=(2,),
        in_specs=[place, place],
        out_specs=[whole, whole],
        out_shape=[FREE((half, cols), BF16), FAR((half, cols), BF16)],
        prefetch=1,
        mib=8,
        name="fold",
        cost=cost,
    )(side, kept, Came(came))


def join_kernel(steps, side_ref, own_ref, came_ref, out_ref):
    upper = pl.program_id(0) // steps
    mine = upper == side_ref[0]

    @pl.when(mine)
    def _():
        out_ref[...] = own_ref[...].astype(out_ref.dtype)

    @pl.when(jnp.logical_not(mine))
    def _():
        out_ref[...] = came_ref[...].astype(out_ref.dtype)


def join(side, own, came, cost=LIGHT):
    rows, cols = own.shape
    if rows % 16:
        mine = side[0] != 0
        pair = (jnp.where(mine, came, own), jnp.where(mine, own, came))
        return jnp.concatenate(pair)
    steps = 1
    part = rows // steps
    half = pl.BlockSpec((part, cols), lambda i, side: (i % steps, 0))
    return local_call(
        functools.partial(join_kernel, steps),
        grid=(2 * steps,),
        in_specs=[half, half],
        out_specs=pl.BlockSpec((part, cols), lambda i, side: (i, 0)),
        out_shape=FAR((2 * rows, cols), BF16),
        prefetch=1,
        mib=10,
        name="join",
        cost=cost,
    )(side, own, Came(came))


SMALL = 16


def split_small(value):
    coarse = value.astype(BF16)
    return jnp.concatenate((coarse, (value - coarse.astype(F32)).astype(BF16)), axis=0)


def read_small(rows):
    return rows[:SMALL].astype(F32) + rows[SMALL:].astype(F32)


def fold_small_kernel(side_ref, kept_ref, came_ref, small_came_ref, small_ref, send_ref, keep_ref, small_out_ref):
    total = (kept_ref[...].astype(F32) + came_ref[...].astype(F32)).astype(BF16)
    half = keep_ref.shape[0]

    @pl.when(pl.program_id(0) == 0)
    def _():
        small = split_small(read_small(small_ref) + read_small(small_came_ref))
        send_ref[:half] = total
        send_ref[half:] = small
        small_out_ref[...] = small

    @pl.when(pl.program_id(0) == 1)
    def _():
        keep_ref[...] = total


def fold_small(side, kept, came, small, cost=LIGHT):
    rows, cols = kept.shape
    half = rows // 2
    extra = 2 * SMALL
    if half % extra:
        send, keep = fold(side, kept, came[:rows])
        small = split_small(read_small(small) + read_small(came[rows:]))
        return jnp.concatenate((send, small)), keep, small
    place = pl.BlockSpec((half, cols), lambda i, side: (jnp.where(i == 0, 1 - side[0], side[0]), 0))

    def whole(count):
        return pl.BlockSpec((count, cols), lambda i, side: (0, 0))

    return local_call(
        fold_small_kernel,
        grid=(2,),
        in_specs=[place, place, pl.BlockSpec((extra, cols), lambda i, side: (rows // extra, 0)), whole(extra)],
        out_specs=[whole(half + extra), whole(half), whole(extra)],
        out_shape=[FREE((half + extra, cols), BF16), FAR((half, cols), BF16), FAR((extra, cols), BF16)],
        prefetch=1,
        mib=10,
        name="fold_small",
        cost=cost,
    )(side, kept, Came(came), Came(came), small)


def add_small_kernel(kept_ref, came_ref, small_ref, out_ref, small_out_ref):
    rows = kept_ref.shape[0]
    out_ref[...] = (kept_ref[...].astype(F32) + came_ref[:rows].astype(F32)).astype(BF16)
    small_out_ref[...] = read_small(small_ref) + read_small(came_ref[rows:])


def add_small(kept, came, small, cost=LIGHT):
    rows, cols = kept.shape
    if rows % (2 * SMALL):
        return add(kept, came[:rows]), read_small(small) + read_small(came[rows:])
    return local_call(
        add_small_kernel,
        grid=(1,),
        in_specs=[vmem_whole(kept.shape), vmem_whole(came.shape), vmem_whole(small.shape)],
        out_specs=[vmem_whole(kept.shape), vmem_whole((SMALL, cols))],
        out_shape=[FAR(kept.shape, BF16), FAR((SMALL, cols), F32)],
        mib=8,
        name="add_small",
        cost=cost,
    )(kept, Came(came), small)


class DpSum:
    def __init__(self, turn, send, keep, finish, small=None):
        self.turn, self.finish, self.small = turn, finish, small
        self.pairs = dp_steps(lax.axis_size("dp"))
        self.at = 0
        self.keep = keep
        self.came = swap_dp(send, self.pairs[0])

    def step(self, cost=LIGHT):
        turn, last = self.turn, len(self.pairs) - 1
        came = turn(self.came)
        if self.at < last:
            after = self.pairs[self.at + 1]
            if self.small is None:
                send, self.keep = turn.done(fold(side_of(after), self.keep, came, cost))
            else:
                results = turn.done(fold_small(side_of(after), self.keep, came, self.small, cost))
                send, self.keep, self.small = results
            self.came = swap_dp(send, after)
        elif self.at == last:
            if self.small is None:
                self.keep = turn.done(add(self.keep, came, cost))
            else:
                self.keep, self.small = turn.done(add_small(self.keep, came, self.small, cost))
            self.came = swap_dp(self.keep, self.pairs[last])
        else:
            place = 2 * last + 1 - self.at
            side = side_of(self.pairs[place])
            if place == 0:
                self.result = turn.done(self.finish(side, self.keep, came))
            else:
                self.keep = turn.done(join(side, self.keep, came, cost))
                self.came = swap_dp(self.keep, self.pairs[place - 1])
        self.at += 1

    def rest(self):
        while self.at < 2 * len(self.pairs):
            self.step()
        return self.result


def finish_feed_kernel(side_ref, own_ref, came_ref, back_ref, in_ref):
    step = pl.program_id(0)
    many = back_ref.shape[0]

    def put(source):
        back_ref[...] = source[:many].astype(F32)
        in_ref[...] = source[many:].astype(F32)

    @pl.when(step == side_ref[0])
    def _():
        put(own_ref)

    @pl.when(step != side_ref[0])
    def _():
        put(came_ref)


def finish_feed(side, own, came):
    rows, cols = own.shape
    whole = pl.BlockSpec((rows, cols), lambda i, side: (0, 0))
    return local_call(
        finish_feed_kernel,
        grid=(2,),
        in_specs=[whole, whole],
        out_specs=[pl.BlockSpec((rows // 2, cols), lambda i, side: (i, 0))] * 2,
        out_shape=[FREE((rows, cols), F32)] * 2,
        prefetch=1,
        mib=20,
        name="finish_feed",
    )(side, own, Came(came))


def finish_heads_kernel(side_ref, own_ref, came_ref, q_ref, k_ref, v_ref, out_ref):
    step = pl.program_id(0)
    cols = q_ref.shape[0]
    for half, refs in enumerate(((q_ref, k_ref), (v_ref, out_ref))):
        for source, is_own in ((own_ref, True), (came_ref, False)):

            @pl.when((step == half) & ((side_ref[0] == half) == is_own))
            def _():
                refs[0][...] = source[:cols].astype(F32)
                refs[1][...] = source[cols:].astype(F32)


def finish_heads(side, own, came):
    rows, cols = own.shape
    each = rows // 2
    whole = pl.BlockSpec((rows, cols), lambda i, side: (0, 0))
    return local_call(
        finish_heads_kernel,
        grid=(2,),
        in_specs=[whole, whole],
        out_specs=[pl.BlockSpec((each, cols), lambda i, side: (0, 0))] * 4,
        out_shape=[FREE((each, cols), F32)] * 4,
        prefetch=1,
        mib=12,
        name="finish_heads",
    )(side, own, Came(came))


def norm_rows(values):
    return lax.rsqrt(jnp.mean(values * values, axis=-1, keepdims=True) + NORM_EPS)


def norm_back(dnormed, unit, spread, gain):
    scaled = gain * dnormed
    inner = jnp.mean(scaled * unit, axis=-1, keepdims=True)
    return spread * (scaled - unit * inner), dnormed * unit


def bias_lanes(seq, first_row, first_col):
    start = seq - LANES - first_row + first_col
    return pl.multiple_of(start, LANES)


def attend_kernel(
    heads, count, length_ref, starts_ref, table_ref, buckets_ref, gain_ref, wq_ref, wk_ref, wv_ref, *refs
):
    tok_refs = refs[:count]
    (ctx_ref, exps_ref, linv_ref, normed_ref, tok_all_ref, q_ref, v_ref, k_turned_ref) = refs[count : count + 8]
    k_ref, v_turned_ref, bias_ref, all_normed, scores_ref = refs[count + 8 :]
    step = pl.program_id(0)
    blk = ctx_ref.shape[0]
    seq = blk * count
    head_cols = wq_ref.shape[0]
    width = head_cols // heads
    wide = 2 * seq

    @pl.when(step == 0)
    def _():
        which = buckets_ref[...]
        for h in range(heads):
            rel = jnp.zeros((8, wide), F32)
            for b in range(table_ref.shape[0]):
                rel = jnp.where(which == b, table_ref[b, h], rel)
            full = jnp.broadcast_to(rel[0:1], (LANES, wide))
            bias_ref[h] = pltpu.roll(full, wide - (LANES - 1), 1, stride=1, stride_axis=0)
        lane = lax.broadcasted_iota(jnp.int32, (blk, LANES - width), 1)
        row = lax.broadcasted_iota(jnp.int32, (blk, LANES - width), 0)
        first = lane == 0
        ones_q = jnp.where(first, 1.0, 0.0)
        ones_v = jnp.where(lane < 2, 1.0, 0.0)
        for b in range(count):
            values = tok_refs[b][...].astype(F32)
            normed = (values * norm_rows(values) * gain_ref[...]).astype(BF16)
            rows = slice(b * blk, (b + 1) * blk)
            all_normed[rows] = normed
            masked = first & (row + starts_ref[b] >= length_ref[0])
            fill = jnp.where(masked, MASK_FILL, 0.0)
            query = dot_nt(normed, wq_ref[...])
            keys = dot_nt(normed, wk_ref[...])
            values = dot_nt(normed, wv_ref[...])
            for h in range(heads):
                cols = slice(h * width, (h + 1) * width)
                q_ref[h, rows] = jnp.concatenate((query[:, cols], ones_q), axis=1).astype(BF16)
                own_k = jnp.concatenate((keys[:, cols], fill), axis=1)
                own_v = jnp.concatenate((values[:, cols], ones_v), axis=1)
                k_ref[h, rows] = own_k.astype(BF16)
                v_ref[h, rows] = own_v.astype(BF16)
                k_turned_ref[h, :, rows] = own_k.T.astype(BF16)
                v_turned_ref[h, :, rows] = own_v.T.astype(BF16)

    row0 = pl.multiple_of(step * blk, blk)
    first_query = starts_ref[step]
    normed_ref[...] = all_normed[pl.ds(row0, blk)]
    for b in range(count):

        @pl.when(step == b)
        def _():
            tok_all_ref[...] = tok_refs[b][...]

    outs = []
    linv = jnp.zeros((blk, LANES), F32)
    stat_lane = lax.broadcasted_iota(jnp.int32, (blk, LANES), 1)
    for h in range(heads):
        query = q_ref[h, pl.ds(row0, blk)]
        top = jnp.full((8, blk), -3.0e38, F32)
        for b in range(count):
            for a in range(blk // LANES):
                rows = slice(b * blk + a * LANES, b * blk + (a + 1) * LANES)
                start = bias_lanes(seq, starts_ref[b] + a * LANES, first_query)
                scores = dot_nt(k_ref[h, rows], query) + bias_ref[h, :, pl.ds(start, blk)]
                scores_ref[rows] = scores
                top = jnp.maximum(top, jnp.max(scores.reshape(LANES // 8, 8, blk), axis=0))
        top = jnp.max(top, axis=0, keepdims=True)
        for c in range(seq // LANES):
            rows = slice(c * LANES, (c + 1) * LANES)
            exps_ref[h, rows] = jnp.exp(scores_ref[rows] - top).astype(BF16)
        mixed = dot_nn(v_turned_ref[h], exps_ref[h]).T
        inverse = 1.0 / mixed[:, width : width + 1]
        outs.append(mixed[:, :width] * inverse)
        linv = jnp.where(stat_lane == h, inverse, linv)
    ctx_ref[...] = jnp.concatenate(outs, axis=1).astype(BF16)
    linv_ref[...] = linv


def attend(length, starts, table, buckets, gain, w_query, w_key, w_value, tok):
    count = len(tok)
    blk, model = tok[0].shape
    seq = blk * count
    heads = table.shape[1]
    head_cols = w_query.shape[0]
    smem = pl.BlockSpec(memory_space=pltpu.SMEM)
    flops = 2 * seq * (3 * model * head_cols + 2 * seq * head_cols)
    return local_call(
        functools.partial(attend_kernel, heads, count),
        grid=(count,),
        in_specs=[smem, smem, smem, vmem_whole((8, 2 * seq)), vmem_whole((1, model))]
        + [vmem_whole((head_cols, model))] * 3
        + [vmem_whole((blk, model))] * count,
        out_specs=[
            pl.BlockSpec((blk, head_cols), lambda i: (i, 0)),
            pl.BlockSpec((heads, seq, blk), lambda i: (0, 0, i)),
            pl.BlockSpec((blk, LANES), lambda i: (i, 0)),
            pl.BlockSpec((blk, model), lambda i: (i, 0)),
            pl.BlockSpec((blk, model), lambda i: (i, 0)),
            vmem_whole((heads, seq, LANES)),
            vmem_whole((heads, seq, LANES)),
            vmem_whole((heads, LANES, seq)),
        ],
        out_shape=[
            FAR((seq, head_cols), BF16),
            FAR((heads, seq, seq), BF16),
            FAR((seq, LANES), F32),
            FAR((seq, model), BF16),
            FAR((seq, model), BF16),
            FAR((heads, seq, LANES), BF16),
            FAR((heads, seq, LANES), BF16),
            FAR((heads, LANES, seq), BF16),
        ],
        scratch_shapes=[
            pltpu.VMEM((heads, seq, LANES), BF16),
            pltpu.VMEM((heads, LANES, seq), BF16),
            pltpu.VMEM((heads, LANES, 2 * seq), F32),
            pltpu.VMEM((seq, model), BF16),
            pltpu.VMEM((seq, blk), F32),
        ],
        mib=28,
        name="attend",
        cost=HEAVY,
    )(length, starts, table, buckets, gain, w_query, w_key, w_value, tok[0], *tok[1:])


def feed_kernel(count, side_ref, scale_ref, gain_ref, *refs):
    tok_far, ctx_far, refs = refs[0], refs[1 : 1 + count], refs[1 + count :]
    w_in_far, w_back_far, joined_far, refs = refs[0], refs[1], refs[2 : 2 + count], refs[2 + count :]
    hidden_ref, unit_ref, spread_ref, dn_low_ref, dn_high_ref, out_low_ref, out_high_ref, send_far, keep_far = refs[:9]
    tok_all, ctx_all, w_in_ref, w_back_ref, w_out_ref, grad_all, active_now, dup_all, active_turned = refs[9:18]
    normed_turned, hidden_now, halves, sems, out_sems = refs[18:]
    step = pl.program_id(0)
    blk = hidden_ref.shape[0]
    units = w_in_ref.shape[1]
    head_cols = ctx_all.shape[2]
    many, fewer = units // 2, normed_turned.shape[0] // 2

    def copy(far, near, sem):
        return pltpu.make_async_copy(far, near, sems.at[sem])

    def block_copies(b):
        rows = pl.ds(b * blk, blk)
        found = [copy(tok_far.at[rows], tok_all.at[rows], b)]
        for k in range(count):
            found.append(copy(ctx_far[k].at[pl.ds((b ^ k) * blk, blk)], ctx_all.at[k, rows], count * (1 + k) + b))
        return found

    first_sem = count * (1 + count)
    out_copies, grad_copies = [], []
    for k in range(count):
        place = w_out_ref.at[pl.ds(k * head_cols, head_cols)]
        out_copies.append(copy(joined_far[k].at[pl.ds(blk, head_cols)], place, first_sem + k))
        place = grad_all.at[pl.ds(k * blk, blk)]
        grad_copies.append(copy(joined_far[k].at[pl.ds(0, blk)], place, first_sem + count + k))
    in_copy = copy(w_in_far, w_in_ref, first_sem + 2 * count)
    back_copy = copy(w_back_far, w_back_ref, first_sem + 2 * count + 1)

    @pl.when(step == 0)
    def _():
        for one in [*block_copies(0), *out_copies, in_copy, grad_copies[0], back_copy]:
            one.start()
        for b in range(1, count):
            for one in [*block_copies(b), grad_copies[b]]:
                one.start()
        for one in out_copies:
            one.wait()

    for b in range(count):

        @pl.when(step == b)
        def _():
            for one in block_copies(b):
                one.wait()

    rows = pl.ds(pl.multiple_of(step * blk, blk), blk)
    hidden = tok_all[rows].astype(F32)
    for slot in range(count):
        hidden = hidden + dot_nn(ctx_all[slot, rows], w_out_ref[slot * head_cols : (slot + 1) * head_cols])
    hidden_now[...] = hidden
    strip = 32 if blk % 32 == 0 else blk
    for r in range(0, blk, strip):
        some = slice(r, r + strip)
        hidden = hidden_now[some]
        spread = norm_rows(hidden)
        unit = hidden * spread
        unit_ref[some] = unit.astype(BF16)
        spread_ref[some] = jnp.broadcast_to(spread, (strip, LANES))
        active_now[some, : unit.shape[1]] = (unit * gain_ref[...]).astype(BF16)
    normed = active_now[:, : hidden.shape[1]]
    normed_turned[:, rows] = normed.T

    @pl.when(step == 0)
    def _():
        hidden_ref[...] = hidden_now[...]
        in_copy.wait()
        back_copy.wait()

    for b in range(count):

        @pl.when(step == b)
        def _():
            grad_copies[b].wait()

    grad = grad_all[rows]
    scale = scale_ref[0]
    part = 256 if units % 256 == 0 else units
    normed = normed_turned[:, rows].T
    for c in range(units // part):
        cols = slice(c * part, (c + 1) * part)
        up = dot_nn(normed, w_in_ref[:, cols])
        dactive = dot_nt(grad, w_back_ref[cols])
        square = up * up
        bend = jnp.tanh(up * (GELU_SCALE + GELU_SCALE * GELU_CUBE * square))
        half = 0.5 + 0.5 * bend
        active = (up * half).astype(BF16)
        steep = GELU_SCALE + 3.0 * GELU_SCALE * GELU_CUBE * square
        slope = (half + (0.5 * up) * (1.0 - bend * bend) * steep) * scale
        active_now[:, cols] = active
        active_turned[cols, rows] = active.T
        dup_all[rows, cols] = (dactive * slope).astype(BF16)
    dnormed = dot_nt(dup_all[rows], w_in_ref[...]).astype(BF16)
    out = dot_nn(active_now[:, :units], w_back_ref[...]).astype(BF16)

    @pl.when(step < count // 2)
    def _():
        dn_low_ref[...] = dnormed
        out_low_ref[...] = out

    @pl.when(step >= count // 2)
    def _():
        dn_high_ref[...] = dnormed
        out_high_ref[...] = out

    @pl.when(step == count - 1)
    def _():
        going = []
        for k, (far, side) in enumerate(((send_far, 1 - side_ref[0]), (keep_far, side_ref[0]))):
            back = dot_nn(active_turned[pl.ds(side * many, many)], grad_all[...]) * scale
            halves[k, :many] = back.astype(BF16)
            halves[k, many:] = dot_nn(normed_turned[pl.ds(side * fewer, fewer)], dup_all[...]).astype(BF16)
            going.append(pltpu.make_async_copy(halves.at[k], far, out_sems.at[k]))
            going[-1].start()
        for one in going:
            one.wait()


def feed(side, scale, gain, w_in, w_back, tok, ctx, joined):
    count = len(ctx)
    rows, model = tok.shape
    blk = rows // count
    units = w_in.shape[1]
    head_cols = ctx[0].shape[1]
    half = count // 2

    by_row = pl.BlockSpec((blk, model), lambda i, side: (i, 0))
    low = pl.BlockSpec((blk, model), lambda i, side: (jnp.minimum(i, half - 1), 0))
    high = pl.BlockSpec((blk, model), lambda i, side: (jnp.maximum(i - half, 0), 0))
    anywhere = pl.BlockSpec(memory_space=pl.ANY)

    def whole(shape):
        return pl.BlockSpec(shape, lambda i, side: (0, 0))

    part_rows = FAR((rows // 2, model), BF16)
    grads = ((units + model) // 2, model)
    return local_call(
        functools.partial(feed_kernel, count),
        grid=(count,),
        in_specs=[pl.BlockSpec(memory_space=pltpu.SMEM), whole((1, model))] + [anywhere] * (3 + 2 * count),
        out_specs=[
            whole((blk, model)),
            by_row,
            pl.BlockSpec((blk, LANES), lambda i, side: (i, 0)),
            low,
            high,
            low,
            high,
            anywhere,
            anywhere,
        ],
        out_shape=[FAR((blk, model), F32), FAR((rows, model), BF16), FAR((rows, LANES), F32)]
        + [part_rows] * 4
        + [FAR(grads, BF16)] * 2,
        scratch_shapes=[
            pltpu.VMEM((rows, model), BF16),
            pltpu.VMEM((count, rows, head_cols), BF16),
            pltpu.VMEM((model, units), BF16),
            pltpu.VMEM((units, model), BF16),
            pltpu.VMEM((count * head_cols, model), BF16),
            pltpu.VMEM((rows, model), BF16),
            pltpu.VMEM((blk, max(units, model)), BF16),
            pltpu.VMEM((rows, units), BF16),
            pltpu.VMEM((units, rows), BF16),
            pltpu.VMEM((model, rows), BF16),
            pltpu.VMEM((blk, model), F32),
            pltpu.VMEM((2, *grads), BF16),
            pltpu.SemaphoreType.DMA((count * (3 + count) + 2,)),
            pltpu.SemaphoreType.DMA((2,)),
        ],
        prefetch=1,
        mib=44,
        name="feed",
        cost=HEAVY,
    )(side, scale, gain, tok, *ctx, w_in, w_back, *joined)


def finish_mixed_kernel(hidden_ref, own_ref, came_ref, out_ref):
    total = own_ref[...].astype(F32) + came_ref[...].astype(F32)
    out_ref[...] = (hidden_ref[...] + total).astype(BF16)


def finish_mixed(hidden, own, came):
    blk, model = own.shape
    place = pl.BlockSpec((blk, model), lambda i: (0, 0))
    return local_call(
        finish_mixed_kernel,
        grid=(1,),
        in_specs=[place] * 3,
        out_specs=place,
        out_shape=jax.ShapeDtypeStruct((blk, model), BF16),
        mib=10,
        name="finish_mixed",
    )(hidden, own, Came(came))


def finish_tokens_kernel(gain_ref, tok_ref, own_ref, came_ref, dh_ref, out_ref):
    dnormed = own_ref[...].astype(F32) + came_ref[...].astype(F32)
    values = tok_ref[...].astype(F32)
    spread = norm_rows(values)
    out_ref[...] = dh_ref[...].astype(F32) + norm_back(dnormed, values * spread, spread, gain_ref[...])[0]


def finish_tokens(gain, tok, own, came, dh_own):
    blk, model = own.shape
    steps = 2 if blk % 32 == 0 else 1
    place = pl.BlockSpec((blk // steps, model), lambda i: (i, 0))
    return local_call(
        finish_tokens_kernel,
        grid=(steps,),
        in_specs=[vmem_whole((1, model))] + [place] * 4,
        out_specs=place,
        out_shape=jax.ShapeDtypeStruct((blk, model), F32),
        mib=10,
        name="finish_tokens",
    )(gain, tok, own, Came(came), dh_own)


def attend_back_kernel(heads, count, bucket_count, side_ref, starts_ref, scale_ref, gain_ref, buckets_ref, *refs):
    dn_refs, refs = refs[:count], refs[count:]
    (unit_ref, spread_ref, ctx_ref, linv_ref, exps_ref), refs = refs[:5], refs[5:]
    far_refs, refs = refs[: 9 + count], refs[9 + count :]
    (dh_own_ref, small_ref, send_ref, keep_ref, in_low_ref, in_high_ref), refs = refs[:6], refs[6:]
    near_refs, refs = refs[:10], refs[10:]
    w_out_ref, q_ref, v_ref, k_turned_ref, normed_ref, wq_ref, wk_ref, wv_ref, tok_ref, grad_all = near_refs
    dk_ref, dv_ref, acc_ref, ds_ref, given_ref, dh_all, ctx_all, dn_now, dj_ref, sums_ref, sems = refs
    block, h = pl.program_id(0), pl.program_id(1)
    blk = dn_now.shape[0]
    seq = blk * count
    head_cols = ctx_ref.shape[1]
    width = head_cols // heads
    wide = acc_ref.shape[2]
    copies = [pltpu.make_async_copy(far_refs[k], near_refs[k], sems.at[k]) for k in range(9)]
    for k in range(count):
        place = grad_all.at[pl.ds(k * blk, blk)]
        copies.append(pltpu.make_async_copy(far_refs[9 + k].at[pl.ds(0, blk)], place, sems.at[9 + k]))
    soon, later, last = [*copies[9:], copies[0]], copies[1:4], copies[4:9]
    strip = 32 if blk % 32 == 0 else blk

    @pl.when((block == 0) & (h == 0))
    def _():
        for copy in [*soon, *later, *last]:
            copy.start()
        dk_ref[...] = jnp.zeros_like(dk_ref)
        dv_ref[...] = jnp.zeros_like(dv_ref)
        acc_ref[...] = jnp.zeros_like(acc_ref)
        for copy in soon:
            copy.wait()

    row0 = pl.multiple_of(block * blk, blk)
    now = pl.ds(row0, blk)

    @pl.when(h == 0)
    def _():
        for b in range(count):

            @pl.when(block == b)
            def _():
                dn_now[...] = dn_refs[b][...]

        for r in range(0, blk, strip):
            some = slice(r, r + strip)
            there = pl.ds(pl.multiple_of(row0 + r, strip), strip)
            unit = unit_ref[some].astype(F32)
            scaled = gain_ref[...] * dn_now[some].astype(F32)
            inner = jnp.mean(scaled * unit, axis=-1, keepdims=True)
            dhidden = spread_ref[some, 0:1] * (scaled - unit * inner)
            dh_all[there] = (dhidden + grad_all[there].astype(F32) * scale_ref[0]).astype(BF16)

        @pl.when(block == 0)
        def _():
            total = jnp.zeros((1, dn_now.shape[1]), F32)
            for r in range(0, blk, strip):
                some = slice(r, r + strip)
                product = unit_ref[some].astype(F32) * dn_now[some].astype(F32)
                total += jnp.sum(product, axis=0, keepdims=True)
            sums_ref[...] = jnp.zeros_like(sums_ref)
            sums_ref[12:16] = jnp.broadcast_to(total, (4, total.shape[1]))
            dh_own_ref[...] = dh_all[0:blk]

        ctx_all[now] = ctx_ref[...]
        dctx = dot_nt(dh_all[now], w_out_ref[...])
        product = dctx * ctx_ref[...].astype(F32)
        lane = lax.broadcasted_iota(jnp.int32, (blk, LANES - width), 1)
        for k in range(heads):
            cols = slice(k * width, (k + 1) * width)
            inverse = linv_ref[:, k : k + 1]
            inner = -jnp.sum(product[:, cols], axis=1, keepdims=True) * inverse
            coarse = inner.astype(BF16).astype(F32)
            extra = jnp.where(lane == 0, coarse, jnp.where(lane == 1, inner - coarse, 0.0))
            given_ref[k] = jnp.concatenate((dctx[:, cols] * inverse, extra), axis=1).astype(BF16)

    @pl.when((block == 0) & (h == 0))
    def _():
        for copy in later:
            copy.wait()

    given = given_ref[h]
    first_query = starts_ref[block]
    for b in range(count):
        for a in range(blk // LANES):
            rows = slice(b * blk + a * LANES, b * blk + (a + 1) * LANES)
            dscores = exps_ref[0, rows].astype(F32) * dot_nt(v_ref[h, rows], given)
            ds_ref[rows] = dscores.astype(BF16)
            start = bias_lanes(seq, starts_ref[b] + a * LANES, first_query)
            acc_ref[h, :, pl.ds(start, blk)] += dscores
    dk_ref[h] += dot_nn(ds_ref[...], q_ref[h, now])
    dv_ref[h] += dot_nn(exps_ref[0], given)
    dquery = dot_nn(k_turned_ref[h], ds_ref[...]).T[:, :width].astype(BF16)
    for k in range(heads):

        @pl.when(h == k)
        def _():
            dj_ref[0, now, k * width : (k + 1) * width] = dquery

    @pl.when((block == count - 1) & (h == heads - 1))
    def _():
        dj_ref[1] = jnp.concatenate([dk_ref[k][:, :width] for k in range(heads)], axis=1).astype(BF16)
        dj_ref[2] = jnp.concatenate([dv_ref[k][:, :width] for k in range(heads)], axis=1).astype(BF16)
        for copy in last:
            copy.wait()
        gain_total = jnp.zeros((1, tok_ref.shape[1]), F32)
        for b in range(count):
            rows = slice(b * blk, (b + 1) * blk)
            dnormed = dot_nn(dj_ref[0, rows], wq_ref[...])
            dnormed = dnormed + dot_nn(dj_ref[1, rows], wk_ref[...])
            dnormed = dnormed + dot_nn(dj_ref[2, rows], wv_ref[...])
            out = (in_low_ref, in_high_ref)[b // (count // 2)]
            base = (b % (count // 2)) * blk
            for r in range(0, blk, strip):
                some = slice(r, r + strip)
                values = tok_ref[b * blk + r : b * blk + r + strip].astype(F32)
                gain_total += jnp.sum(dnormed[some] * (values * norm_rows(values)), axis=0, keepdims=True)
                out[base + r : base + r + strip] = dnormed[some].astype(BF16)
        sums_ref[8:12] = jnp.broadcast_to(gain_total, (4, gain_total.shape[1]))

        which = buckets_ref[...]
        drel = []
        for k in range(heads):
            part = acc_ref[k]
            rows = LANES
            while rows > 1:
                rows //= 2
                part = part[:rows] + pltpu.roll(part[rows:], wide - rows, 1)
            drel.append(pltpu.roll(part, LANES - 1, 1))
        drel = jnp.concatenate(drel + [jnp.zeros((8 - heads, wide), F32)], axis=0)
        bucket = lax.broadcasted_iota(jnp.int32, (LANES, wide), 0)
        onehot = jnp.where(bucket == jnp.broadcast_to(which[0:1], (LANES, wide)), 1.0, 0.0).astype(BF16)
        table = jnp.zeros((8, LANES), F32)
        for _ in range(3):
            coarse = drel.astype(BF16)
            table = table + dot_nt(jnp.concatenate((coarse, jnp.zeros_like(coarse)), axis=0), onehot)[:8]
            drel = drel - coarse.astype(F32)
        sums_ref[0:8, 0:LANES] = table
        small = split_small(sums_ref[...])
        small_ref[...] = small
        for side in range(2):

            @pl.when(side_ref[0] == side)
            def _():
                near, other = (keep_ref, send_ref) if side == 0 else (send_ref, keep_ref)
                near[:head_cols] = dot_tn(dj_ref[0], normed_ref[...]).astype(BF16)
                near[head_cols : 2 * head_cols] = dot_tn(dj_ref[1], normed_ref[...]).astype(BF16)
                other[:head_cols] = dot_tn(dj_ref[2], normed_ref[...]).astype(BF16)
                other[head_cols : 2 * head_cols] = dot_tn(ctx_all[...], dh_all[...]).astype(BF16)

        send_ref[2 * head_cols :] = small


def attend_back(bucket_count, side, starts, scale, gain, w_out, buckets, dn, unit, spread, joined, ctx, linv, exps, q, v, k_turned, normed, weights, tok):
    head_cols, model = w_out.shape
    count = starts.shape[0]
    heads, seq = exps.shape[:2]
    assert bucket_count <= LANES and heads <= 8
    blk = seq // count

    def block(cols):
        return pl.BlockSpec((blk, cols), lambda i, h, side: (i, 0))

    def whole(shape):
        return pl.BlockSpec(shape, lambda i, h, side: (0,) * len(shape))

    near = [w_out, q, v, k_turned, normed, *weights, tok]
    smem = pl.BlockSpec(memory_space=pltpu.SMEM)
    extra = 2 * SMALL
    outs = [(blk, model), (extra, model), (2 * head_cols + extra, model), (2 * head_cols, model), (seq // 2, model), (seq // 2, model)]
    return local_call(
        functools.partial(attend_back_kernel, heads, count, bucket_count),
        grid=(count, heads),
        in_specs=[
            smem,
            smem,
            whole((1, model)),
            whole((8, 2 * seq)),
            *[whole((blk, model))] * count,
            block(model),
            block(LANES),
            block(head_cols),
            block(LANES),
            pl.BlockSpec((1, seq, blk), lambda i, h, side: (h, 0, i)),
            *[pl.BlockSpec(memory_space=pl.ANY)] * (len(near) + count),
        ],
        out_specs=[whole(shape) for shape in outs],
        out_shape=[FAR(shape, BF16) for shape in outs],
        scratch_shapes=[pltpu.VMEM(a.shape, a.dtype) for a in near]
        + [
            pltpu.VMEM((seq, model), BF16),
            pltpu.VMEM((heads, seq, LANES), F32),
            pltpu.VMEM((heads, seq, LANES), F32),
            pltpu.VMEM((heads, LANES, 2 * seq), F32),
            pltpu.VMEM((seq, blk), BF16),
            pltpu.VMEM((heads, blk, LANES), BF16),
            pltpu.VMEM((seq, model), BF16),
            pltpu.VMEM((seq, head_cols), BF16),
            pltpu.VMEM((blk, model), BF16),
            pltpu.VMEM((3, seq, head_cols), BF16),
            pltpu.VMEM((SMALL, model), F32),
            pltpu.SemaphoreType.DMA((len(near) + count,)),
        ],
        prefetch=1,
        mib=52,
        name="attend_back",
    )(side, starts, scale, gain, buckets, *dn, unit, spread, ctx, linv, exps, *near, *joined)


def shards(
    tokens,
    row_lengths,
    instruction_mask,
    task_groups,
    rel_buckets,
    gain_attn,
    w_query,
    w_key,
    w_value,
    rel_table,
    w_out,
    gain_ffn,
    w_in,
    w_back,
    out_grad,
):
    blk, model = tokens.shape[1:]
    count = lax.axis_size("tensor")
    head_cols = w_query.shape[1]
    bucket_count, heads = rel_table.shape
    width = head_cols // heads
    seq = blk * count
    half = count // 2
    bits = tensor_bits(count)
    here = lax.axis_index("tensor")
    starts = (here ^ jnp.array(block_order(count), jnp.int32)) * blk
    weights = (w_query.T, w_key.T, w_value.T)
    gain_attn = gain_attn[None, :]
    gain_ffn = gain_ffn[None, :]
    turned = jnp.pad(rel_buckets[::-1], (0, 1), constant_values=-1)
    buckets = jnp.broadcast_to(turned[None], (8, 2 * seq))
    first_side = side_of(dp_steps(lax.axis_size("dp"))[0])

    own_group = lax.dynamic_slice_in_dim(task_groups, lax.axis_index("dp"), 1)
    scale = lax.rsqrt(jnp.sum((own_group == task_groups).astype(F32)))[None]
    positions = here * blk + jnp.arange(blk, dtype=jnp.int32)
    keep = (positions < row_lengths[0]) & (instruction_mask[0] == 0)
    masked_grad = jnp.where(keep[:, None], out_grad[0], 0).astype(BF16)

    turn = Turn()
    low_bits = bits[:-1]

    def across(pieces):
        while len(pieces) > 1:
            bit = low_bits[len(low_bits) - len(pieces).bit_length() + 1]
            near = len(pieces) // 2
            others = [swap_tensor(piece, bit) for piece in pieces[near:]]
            pieces = list(zip(pieces[:near], others, strict=True))
            if near > 1:
                pieces = [turn.done(add(a, turn(b))) for a, b in pieces]
        return pieces[0]

    own_tok = tokens[0]
    joined = jnp.concatenate((masked_grad, w_out))
    ready = (joined, starts, scale, buckets, gain_attn, gain_ffn, rel_table)
    tok, ready = gather_tensor(own_tok, count, ready)
    joined, starts, scale, buckets, gain_attn, gain_ffn, rel_table = ready
    joined = [joined]
    for bit in low_bits:
        joined = joined + [swap_tensor(piece, bit) for piece in joined]
    ctx, exps, linv, normed, tok_all, q, v, k_turned = turn.done(
        attend(row_lengths, starts, rel_table, buckets, gain_attn, *weights, tok)
    )
    contexts, _ = gather_tensor(ctx, count)
    joined = [turn(piece) for piece in joined]
    joined = joined + [swap_tensor(piece, bits[-1]) for piece in joined]
    hidden, unit, spread, dn_low, dn_high, out_low, out_high, feed_send, feed_keep = turn.done(
        feed(first_side, scale, gain_ffn, w_in, w_back, tok_all, contexts, joined)
    )
    dn_came = swap_tensor(dn_high, bits[-1])
    out_came = swap_tensor(out_high, bits[-1])
    sum_feed = DpSum(turn, feed_send, feed_keep, finish_feed)

    assert half == 2 and len(low_bits) == 1
    flip = block_order(count).index(low_bits[0])
    dn_low, dn_sent = turn.done(add_swap(dn_low, turn(dn_came), half, flip))
    dn_came = swap_tensor(dn_sent, low_bits[0])
    out_own = turn.done(add_pieces(out_low, turn(out_came), half))
    sum_feed.step(HEAVY)
    dn_low = turn.done(add_pieces(dn_low, turn(dn_came), half))
    dn_high = [swap_tensor(piece, bits[-1]) for piece in dn_low]
    dh_own, small, heads_send, heads_keep, dn_low, dn_high = turn.done(
        attend_back(
            bucket_count,
            first_side,
            starts,
            scale,
            gain_ffn,
            w_out,
            buckets,
            [*dn_low, *[turn(piece) for piece in dn_high]],
            unit,
            spread,
            joined,
            ctx,
            linv,
            exps,
            q,
            v,
            k_turned,
            normed,
            weights,
            tok_all,
        )
    )
    sum_heads = DpSum(turn, heads_send, heads_keep, finish_heads, small)
    dn_came = swap_tensor(dn_high, bits[-1])
    out_own, out_came = across([turn(piece) for piece in out_own])
    sum_feed.step(HEAVY)
    dn_own = turn.done(add_pieces(dn_low, turn(dn_came), half))
    dn_own, dn_came = across(dn_own)
    sum_heads.step(HEAVY)
    mixed = turn.done(finish_mixed(hidden, out_own, turn(out_came)))[None]
    sum_feed.step(HEAVY)
    grad_tokens = turn.done(finish_tokens(gain_attn, own_tok, dn_own, turn(dn_came), dh_own))[None]
    sum_heads.step(HEAVY)
    sum_feed.step()
    sum_heads.step(HEAVY)
    while sum_heads.at < len(sum_heads.pairs):
        sum_heads.step(HEAVY)
    gains = sum_heads.small[SMALL // 2 :]
    gains_came = swap_tensor(gains, bits[-1])
    sum_heads.step()
    gains = turn.done(add(gains, turn(gains_came)))
    for bit in reversed(low_bits):
        gains_came = swap_tensor(gains, bit)
    sum_feed.step()
    sum_heads.step(HEAVY)
    gains = turn.done(add(gains, turn(gains_came)))
    dtable = sum_heads.small
    grad_back, grad_in = sum_feed.rest()
    grad_query, grad_key, grad_value, grad_out = sum_heads.rest()
    return (
        mixed,
        grad_tokens,
        gains[0],
        grad_query.T,
        grad_key.T,
        grad_value.T,
        dtable[:heads, :bucket_count].T,
        grad_out,
        gains[4],
        grad_in,
        grad_back,
    )


def solution(mesh):
    return jax.shard_map(
        shards,
        mesh=mesh,
        in_specs=(
            P("dp", "tensor", None),
            P("dp"),
            P("dp", "tensor"),
            P(),
            P(),
            P(),
            P(None, "tensor"),
            P(None, "tensor"),
            P(None, "tensor"),
            P(None, "tensor"),
            P("tensor", None),
            P(),
            P(None, "tensor"),
            P("tensor", None),
            P("dp", "tensor", None),
        ),
        out_specs=(
            P("dp", "tensor", None),
            P("dp", "tensor", None),
            P(),
            P(None, "tensor"),
            P(None, "tensor"),
            P(None, "tensor"),
            P(None, "tensor"),
            P("tensor", None),
            P(),
            P(None, "tensor"),
            P("tensor", None),
        ),
        check_vma=False,
    )
```

profile of v0, /device:TPU:0, one launch (start us, length us, event | category | flops | bytes accessed | tf_op | source)
XLA Modules:
  0.0 221.1 jit_solution(12344975531437057295)
XLA Ops:
  0.7 3.0 %collective-permute-start.1 = (bf16[256,768]{1,0:T(8,128)(2,1)}, bf16[256,768]{1,0:T(8,128)(2,1)S(1)}, u32[]{:S(2)}, u32[]{:S(2)}) collective-permute-start(bf16[256,768]{1,0:T(8,128)(2,1)} %bitcast.22), channel_id=1, source_target_pairs={{0,2},{1,3},{2,0},{3,1},{4,6},{5,7},{6,4},{7,5},{8,10},{9,11},{10,... | collective-permute-start | bytes 1179656 | tf_op jit(solution)/shard_map/ppermute | solution.py:107
  5.1 1.2 dynamic_slice.3
  6.3 1.1 bitcast_select_fusion
  7.4 1.9 fusion
  10.0 1.3 broadcast_in_dim.63.gain_ref
  11.3 1.3 broadcast_in_dim.64.gain_ref
  12.5 0.8 reverse
  13.4 1.0 pad_maximum_fusion.refs_7_.refs_18_
  15.7 1.3 collective-permute-done.2.refs_3_
  17.8 16.2 %attend.1 = (bf16[1024,192]{1,0:T(8,128)(2,1)}, bf16[3,1024,1024]{2,1,0:T(8,128)(2,1)}, f32[1024,128]{1,0:T(8,128)}, bf16[1024,768]{1,0:T(8,128)(2,1)}, bf16[102...) custom-call(s32[1]{0:T(128)} %copy.28.length_ref, ...), custom_call_target="tpu_custom_call" | custom-call | flops 99999997952 | bytes 1024 | tf_op jit(solution)/shard_map/attend/pallas_call | solution.py:54
  34.0 1.5 collective-permute-start.3
  36.1 12.4 %collective-permute-done.3.refs_2_ = bf16[1024,192]{1,0:T(8,128)(2,1)S(1)} collective-permute-done((bf16[1024,192]{1,0:T(8,128)(2,1)}, bf16[1024,192]{1,0:T(8,128)(2,1)S(1)}, u32[]{:S(2)}, u32[]{:S(2)}) %collective-permute-start.3) | collective-permute-done | bytes 393248 | tf_op jit(solution)/shard_map/ppermute | solution.py:107
  48.5 2.0 collective-permute-done.5.refs_4_
  50.6 0.8 copy-done.5
  51.4 19.6 %feed.1 = (f32[256,768]{1,0:T(8,128)}, bf16[1024,768]{1,0:T(8,128)(2,1)}, f32[1024,128]{1,0:T(8,128)}, bf16[512,768]{1,0:T(8,128)(2,1)}, bf16[512,768]{1,0:T(8,1...) custom-call(s32[1]{0:T(128)} %bitcast.side_ref, ...), custom_call_target="tpu_custom_call" | custom-call | flops 99999997952 | bytes 1024 | tf_op jit(solution)/shard_map/feed/pallas_call | solution.py:54
  71.0 1.6 collective-permute-start.12
  73.1 2.0 collective-permute-done.10.right_ref
  75.1 2.0 add_swap.1
  77.1 1.1 collective-permute-start.11
  78.2 2.1 add_pieces.3
  80.3 7.2 %collective-permute-done.12.came_ref = bf16[768,768]{1,0:T(8,128)(2,1)S(1)} collective-permute-done((bf16[768,768]{1,0:T(8,128)(2,1)}, bf16[768,768]{1,0:T(8,128)(2,1)S(1)}, u32[]{:S(2)}, u32[]{:S(2)}) %collective-permute-start.12) | collective-permute-done | bytes 1179680 | tf_op jit(solution)/shard_map/ppermute | solution.py:143
  87.5 2.5 %fold.2 = (bf16[384,768]{1,0:T(8,128)(2,1)S(1)}, bf16[384,768]{1,0:T(8,128)(2,1)}) custom-call(s32[1]{0:T(128)} %bitcast.9.side_ref, bf16[768,768]{1,0:T(8,128)(2,1)} %get-tuple-element.134.kept_ref, bf16[768,768]{1,0:T(8,128)(2,1)S(1)} %collective-permute-done.12.came_ref), custom_call_target="tpu_custom_call" | custom-call | flops 99999997952 | bytes 1024 | tf_op jit(solution)/shard_map/fold/pallas_call | solution.py:54
  90.0 1.6 collective-permute-start.18
  91.6 5.1 %collective-permute-done.11.refs_1_ = bf16[512,768]{1,0:T(8,128)(2,1)S(1)} collective-permute-done((bf16[512,768]{1,0:T(8,128)(2,1)S(1)}, bf16[512,768]{1,0:T(8,128)(2,1)S(1)}, u32[]{:S(2)}, u32[]{:S(2)}) %collective-permute-start.11) | collective-permute-done | bytes 786464 | tf_op jit(solution)/shard_map/ppermute | solution.py:107
  96.7 2.1 add_pieces.4
  99.3 1.4 collective-permute-done.14.refs_3_
  102.0 27.2 %attend_back.1 = (bf16[256,768]{1,0:T(8,128)(2,1)}, bf16[32,768]{1,0:T(8,128)(2,1)}, bf16[416,768]{1,0:T(8,128)(2,1)}, bf16[384,768]{1,0:T(8,128)(2,1)}, bf16[51...) custom-call(s32[1]{0:T(128)} %bitcast.side_ref, s32[4]{0:T(128)S(1)} %copy-done.1, f32[1]{0:T(128)} %bitcast.5.scale_ref, ...), custom_call_target="tpu_custom_call" | custom-call | flops 1024 | bytes 1024 | tf_op jit(solution)/shard_map/attend_back/pallas_call | solution.py:54
  129.2 1.2 collective-permute-start.15
  130.4 1.3 collective-permute-start.16
  131.7 2.0 fold.3
  133.6 2.6 %collective-permute-start.20 = (bf16[192,768]{1,0:T(8,128)(2,1)S(1)}, bf16[192,768]{1,0:T(8,128)(2,1)S(1)}, u32[]{:S(2)}, u32[]{:S(2)}) collective-permute-start(bf16[192,768]{1,0:T(8,128)(2,1)S(1)} %get-tuple-element.161), channel_id=1, source_target_pairs={{0,16},{1,17},{2,18},{3,19},{4,20},{5,21},{6,22},{7,23},{8,24},{9,... | collective-permute-start | bytes 884744 | tf_op jit(solution)/shard_map/ppermute | solution.py:143
  136.2 2.1 add_pieces.5
  138.3 2.7 %collective-permute-done.16.came_ref.small_came_ref = bf16[416,768]{1,0:T(8,128)(2,1)S(1)} collective-permute-done((bf16[416,768]{1,0:T(8,128)(2,1)}, bf16[416,768]{1,0:T(8,128)(2,1)S(1)}, u32[]{:S(2)}, u32[]{:S(2)}) %collective-permute-start.16) | collective-permute-done | bytes 639008 | tf_op jit(solution)/shard_map/ppermute | solution.py:143
  141.0 2.0 fold_small.2
  143.0 1.6 collective-permute-start.21
  144.6 2.2 %finish_mixed.1 = bf16[256,768]{1,0:T(8,128)(2,1)} custom-call(f32[256,768]{1,0:T(8,128)} %get-tuple-element.124.hidden_ref, bf16[256,768]{1,0:T(8,128)(2,1)} %get-tuple-element.152.own_ref, bf16[256,768]{1,0:T(8,128)(2,1)} %collective-permute-done.15.came_ref), custom_call_target="tpu_custom_call" | custom-call | flops 1024 | bytes 1024 | tf_op jit(solution)/shard_map/finish_mixed/pallas_call | solution.py:54
  146.8 3.6 %collective-permute-done.20.right_ref = bf16[192,768]{1,0:T(8,128)(2,1)S(1)} collective-permute-done((bf16[192,768]{1,0:T(8,128)(2,1)S(1)}, bf16[192,768]{1,0:T(8,128)(2,1)S(1)}, u32[]{:S(2)}, u32[]{:S(2)}) %collective-permute-start.20) | collective-permute-done | bytes 294944 | tf_op jit(solution)/shard_map/ppermute | solution.py:143
  150.4 0.9 collective-permute-start.19
  151.3 1.7 add.41.own_ref
  153.0 8.0 %collective-permute-done.19.came_ref = bf16[256,768]{1,0:T(8,128)(2,1)S(1)} collective-permute-done((bf16[256,768]{1,0:T(8,128)(2,1)S(1)}, bf16[256,768]{1,0:T(8,128)(2,1)S(1)}, u32[]{:S(2)}, u32[]{:S(2)}) %collective-permute-start.19) | collective-permute-done | bytes 393248 | tf_op jit(solution)/shard_map/ppermute | solution.py:107
  161.1 2.4 %finish_tokens.1 = f32[256,768]{1,0:T(8,128)} custom-call(f32[1,768]{1,0:T(1,128)} %broadcast_in_dim.63.gain_ref, bf16[256,768]{1,0:T(8,128)(2,1)} %bitcast.25, bf16[256,768]{1,0:T(8,128)(2,1)} %get-tuple-element.163.own_ref, bf16[256,768]{1,0:T(8,128)(2,1)S(1)} %collective-permute-done.19.came_ref, bf16[256,768]{1,0:T(8,128)(2,1)} %get-tuple-element.151.dh_ref), custom_call_target="tpu_custom_call" | custom-call | flops 1024 | bytes 1024 | tf_op jit(solution)/shard_map/finish_tokens/pallas_call | solution.py:54
  163.5 1.7 fold_small.3
  165.8 7.5 %collective-permute-done.23.came_ref = bf16[192,768]{1,0:T(8,128)(2,1)S(1)} collective-permute-done((bf16[192,768]{1,0:T(8,128)(2,1)}, bf16[192,768]{1,0:T(8,128)(2,1)S(1)}, u32[]{:S(2)}, u32[]{:S(2)}) %collective-permute-start.23) | collective-permute-done | bytes 294944 | tf_op jit(solution)/shard_map/ppermute | solution.py:143
  173.3 1.8 join.4.own_ref
  175.1 2.1 collective-permute-done.22.came_ref
  177.2 1.6 add_small.1
  178.9 9.5 %collective-permute-done.25.came_ref = bf16[96,768]{1,0:T(8,128)(2,1)S(1)} collective-permute-done((bf16[96,768]{1,0:T(8,128)(2,1)}, bf16[96,768]{1,0:T(8,128)(2,1)S(1)}, u32[]{:S(2)}, u32[]{:S(2)}) %collective-permute-start.25) | collective-permute-done | bytes 147488 | tf_op jit(solution)/shard_map/ppermute | solution.py:143
  188.4 1.6 join.5.own_ref
  190.3 0.7 slice.12.left_ref
  191.0 1.2 collective-permute-done.24.right_ref
  192.2 1.3 add.42.left_ref
  193.6 2.2 join.6.own_ref
  195.7 0.9 collective-permute-start.30
  197.0 1.8 join.7.own_ref
  198.8 0.8 collective-permute-start.29
  199.6 1.1 collective-permute-start.26
  200.7 1.3 slice_bitcast_fusion
  201.9 1.4 collective-permute-done.26.right_ref
  203.4 1.4 add.43
  204.7 1.4 slice_reduce_fusion
  206.2 6.0 %collective-permute-done.30.came_ref = bf16[768,768]{1,0:T(8,128)(2,1)S(1)} collective-permute-done((bf16[768,768]{1,0:T(8,128)(2,1)}, bf16[768,768]{1,0:T(8,128)(2,1)S(1)}, u32[]{:S(2)}, u32[]{:S(2)}) %collective-permute-start.30) | collective-permute-done | bytes 1179680 | tf_op jit(solution)/shard_map/ppermute | solution.py:143
  212.1 3.6 %finish_feed.1 = (f32[768,768]{1,0:T(8,128)}, f32[768,768]{1,0:T(8,128)}) custom-call(s32[1]{0:T(128)} %bitcast.side_ref, bf16[768,768]{1,0:T(8,128)(2,1)} %join.6.own_ref, bf16[768,768]{1,0:T(8,128)(2,1)S(1)} %collective-permute-done.30.came_ref), custom_call_target="tpu_custom_call" | custom-call | flops 1024 | bytes 1024 | tf_op jit(solution)/shard_map/finish_feed/pallas_call | solution.py:54
  215.7 2.7 %collective-permute-done.29.came_ref = bf16[384,768]{1,0:T(8,128)(2,1)S(1)} collective-permute-done((bf16[384,768]{1,0:T(8,128)(2,1)}, bf16[384,768]{1,0:T(8,128)(2,1)S(1)}, u32[]{:S(2)}, u32[]{:S(2)}) %collective-permute-start.29) | collective-permute-done | bytes 589856 | tf_op jit(solution)/shard_map/ppermute | solution.py:143
  218.5 2.7 %finish_heads.1 = (f32[192,768]{1,0:T(8,128)}, f32[192,768]{1,0:T(8,128)}, f32[192,768]{1,0:T(8,128)}, f32[192,768]{1,0:T(8,128)}) custom-call(s32[1]{0:T(128)} %bitcast.side_ref, bf16[384,768]{1,0:T(8,128)(2,1)} %join.7.own_ref, bf16[384,768]{1,0:T(8,128)(2,1)S(1)} %collective-permute-done.29.came_ref), custom_call_target="tpu_custom_call" | custom-call | flops 1024 | bytes 1024 | tf_op jit(solution)/shard_map/finish_heads/pallas_call | solution.py:54
  (72 shorter events, 7.0 us)
Async XLA Ops:
  0.6 13.8 %copy-start.16 = (s32[4]{0:T(128)S(1)}, s32[4]{0:T(128)}, u32[]{:S(2)}) copy-start(s32[4]{0:T(128)} %constant.60.clone) | copy-start | bytes 52
  0.7 16.4 %copy-start.10 = (f32[32,3]{0,1:T(4,128)S(1)}, f32[32,3]{0,1:T(4,128)}, u32[]{:S(2)}) copy-start(f32[32,3]{0,1:T(4,128)} %param.25) | copy-start | bytes 1156
  0.7 13.8 %collective-permute-start.1 = (bf16[256,768]{1,0:T(8,128)(2,1)}, bf16[256,768]{1,0:T(8,128)(2,1)S(1)}, u32[]{:S(2)}, u32[]{:S(2)}) collective-permute-start(bf16[256,768]{1,0:T(8,128)(2,1)} %bitcast.22), channel_id=1, source_target_pairs={{0,2},{1,3},{2,0},{3,1},{4,6},{5,7},{6,4},{7,5},{8,10},{9,11},{10,... | collective-permute-start | bytes 1179656 | tf_op jit(solution)/shard_map/ppermute | solution.py:107
  3.7 12.0 %collective-permute-start = (bf16[256,768]{1,0:T(8,128)(2,1)}, bf16[256,768]{1,0:T(8,128)(2,1)S(1)}, u32[]{:S(2)}, u32[]{:S(2)}) collective-permute-start(bf16[256,768]{1,0:T(8,128)(2,1)} %bitcast.23), channel_id=1, source_target_pairs={{0,1},{1,0},{2,3},{3,2},{4,5},{5,4},{6,7},{7,6},{8,9},{9,8},{10,11... | collective-permute-start | bytes 1179656 | tf_op jit(solution)/shard_map/ppermute | solution.py:107
  14.4 21.1 %copy-start.2 = (bf16[448,768]{1,0:T(8,128)(2,1)}, bf16[448,768]{1,0:T(8,128)(2,1)S(1)}, u32[]{:S(2)}) copy-start(bf16[448,768]{1,0:T(8,128)(2,1)S(1)} %pad_maximum_fusion.refs_7_.refs_18_) | copy-start | bytes 2064388
  14.4 19.6 %copy-start = (s32[4]{0:T(128)}, s32[4]{0:T(128)S(1)}, u32[]{:S(2)}) copy-start(s32[4]{0:T(128)S(1)} %xor_multiply_fusion.starts_ref) | copy-start | bytes 52
  14.5 2.8 %copy-start.12 = (bf16[256,768]{1,0:T(8,128)(2,1)}, bf16[256,768]{1,0:T(8,128)(2,1)S(1)}, u32[]{:S(2)}) copy-start(bf16[256,768]{1,0:T(8,128)(2,1)S(1)} %collective-permute-done.1.refs_1_) | copy-start | bytes 1179652
  15.2 1.9 collective-permute-start.2
  15.7 1.5 copy-start.13
  17.0 0.7 copy-start.15
  17.1 18.4 %collective-permute-start.6 = (bf16[448,768]{1,0:T(8,128)(2,1)S(1)}, bf16[448,768]{1,0:T(8,128)(2,1)S(1)}, u32[]{:S(2)}, u32[]{:S(2)}) collective-permute-start(bf16[448,768]{1,0:T(8,128)(2,1)S(1)} %pad_maximum_fusion.refs_7_.refs_18_), channel_id=1, source_target_pairs={{0,2},{1,3},{2,0},{3,1},{4,6},{5,7},{6,4},{7,5},{8,10},{9,11},{10,... | collective-permute-start | bytes 2064392 | tf_op jit(solution)/shard_map/ppermute | solution.py:107
  34.0 14.5 %collective-permute-start.3 = (bf16[1024,192]{1,0:T(8,128)(2,1)}, bf16[1024,192]{1,0:T(8,128)(2,1)S(1)}, u32[]{:S(2)}, u32[]{:S(2)}) collective-permute-start(bf16[1024,192]{1,0:T(8,128)(2,1)} %get-tuple-element.120.refs_1_.refs_6_), channel_id=1, source_target_pairs={{0,2},{1,3},{2,0},{3,1},{4,6},{5,7},{6,4},{7,5},{8,10},{9,11},{10,... | collective-permute-start | bytes 1179656 | tf_op jit(solution)/shard_map/ppermute | solution.py:107
  35.5 13.0 %collective-permute-start.7 = (bf16[448,768]{1,0:T(8,128)(2,1)S(1)}, bf16[448,768]{1,0:T(8,128)(2,1)S(1)}, u32[]{:S(2)}, u32[]{:S(2)}) collective-permute-start(bf16[448,768]{1,0:T(8,128)(2,1)S(1)} %pad_maximum_fusion.refs_7_.refs_18_), channel_id=1, source_target_pairs={{0,1},{1,0},{2,3},{3,2},{4,5},{5,4},{6,7},{7,6},{8,9},{9,8},{10,11... | collective-permute-start | bytes 2064392 | tf_op jit(solution)/shard_map/ppermute | solution.py:107
  35.5 15.0 %copy-start.3 = (bf16[448,768]{1,0:T(8,128)(2,1)}, bf16[448,768]{1,0:T(8,128)(2,1)S(1)}, u32[]{:S(2)}) copy-start(bf16[448,768]{1,0:T(8,128)(2,1)S(1)} %collective-permute-done.6.refs_8_.refs_19_) | copy-start | bytes 2064388
  35.6 15.0 %collective-permute-start.8 = (bf16[448,768]{1,0:T(8,128)(2,1)S(1)}, bf16[448,768]{1,0:T(8,128)(2,1)S(1)}, u32[]{:S(2)}, u32[]{:S(2)}) collective-permute-start(bf16[448,768]{1,0:T(8,128)(2,1)S(1)} %collective-permute-done.6.refs_8_.refs_19_), channel_id=1, source_target_pairs={{0,1},{1,0},{2,3},{3,2},{4,5},{5,4},{6,7},{7,6},{8,9},{9,8},{10,11... | collective-permute-start | bytes 2064392 | tf_op jit(solution)/shard_map/ppermute | solution.py:107
  36.0 12.5 %collective-permute-start.4 = (bf16[1024,192]{1,0:T(8,128)(2,1)}, bf16[1024,192]{1,0:T(8,128)(2,1)}, u32[]{:S(2)}, u32[]{:S(2)}) collective-permute-start(bf16[1024,192]{1,0:T(8,128)(2,1)} %get-tuple-element.120.refs_1_.refs_6_), channel_id=1, source_target_pairs={{0,1},{1,0},{2,3},{3,2},{4,5},{5,4},{6,7},{7,6},{8,9},{9,8},{10,11... | collective-permute-start | bytes 1179656 | tf_op jit(solution)/shard_map/ppermute | solution.py:107
  48.5 2.1 copy-start.11
  48.5 2.0 collective-permute-start.5
  48.5 2.0 copy-start.4
  50.6 0.8 copy-start.5
  71.0 16.5 %collective-permute-start.12 = (bf16[768,768]{1,0:T(8,128)(2,1)}, bf16[768,768]{1,0:T(8,128)(2,1)S(1)}, u32[]{:S(2)}, u32[]{:S(2)}) collective-permute-start(bf16[768,768]{1,0:T(8,128)(2,1)} %get-tuple-element.135), channel_id=1, source_target_pairs={{0,4},{1,9},{2,6},{3,11},{4,0},{5,13},{6,2},{7,15},{8,12},{9,1},{1... | collective-permute-start | bytes 3538952 | tf_op jit(solution)/shard_map/ppermute | solution.py:143
  72.6 2.5 %collective-permute-start.10 = (bf16[512,768]{1,0:T(8,128)(2,1)}, bf16[512,768]{1,0:T(8,128)(2,1)S(1)}, u32[]{:S(2)}, u32[]{:S(2)}) collective-permute-start(bf16[512,768]{1,0:T(8,128)(2,1)} %get-tuple-element.128), channel_id=1, source_target_pairs={{0,1},{1,0},{2,3},{3,2},{4,5},{5,4},{6,7},{7,6},{8,9},{9,8},{10,11... | collective-permute-start | bytes 2359304 | tf_op jit(solution)/shard_map/ppermute | solution.py:107
  72.6 4.5 %collective-permute-start.9 = (bf16[512,768]{1,0:T(8,128)(2,1)}, bf16[512,768]{1,0:T(8,128)(2,1)S(1)}, u32[]{:S(2)}, u32[]{:S(2)}) collective-permute-start(bf16[512,768]{1,0:T(8,128)(2,1)} %get-tuple-element.126), channel_id=1, source_target_pairs={{0,1},{1,0},{2,3},{3,2},{4,5},{5,4},{6,7},{7,6},{8,9},{9,8},{10,11... | collective-permute-start | bytes 2359304 | tf_op jit(solution)/shard_map/ppermute | solution.py:107
  77.1 19.6 %collective-permute-start.11 = (bf16[512,768]{1,0:T(8,128)(2,1)S(1)}, bf16[512,768]{1,0:T(8,128)(2,1)S(1)}, u32[]{:S(2)}, u32[]{:S(2)}) collective-permute-start(bf16[512,768]{1,0:T(8,128)(2,1)S(1)} %get-tuple-element.133), channel_id=1, source_target_pairs={{0,2},{1,3},{2,0},{3,1},{4,6},{5,7},{6,4},{7,5},{8,10},{9,11},{10,... | collective-permute-start | bytes 2359304 | tf_op jit(solution)/shard_map/ppermute | solution.py:107
  90.0 12.0 %copy-start.1 = (s32[4]{0:T(128)S(1)}, s32[4]{0:T(128)}, u32[]{:S(2)}) copy-start(s32[4]{0:T(128)} %copy-done) | copy-start | bytes 52
  90.0 40.4 %collective-permute-start.18 = (bf16[384,768]{1,0:T(8,128)(2,1)S(1)}, bf16[384,768]{1,0:T(8,128)(2,1)S(1)}, u32[]{:S(2)}, u32[]{:S(2)}) collective-permute-start(bf16[384,768]{1,0:T(8,128)(2,1)S(1)} %get-tuple-element.137), channel_id=1, source_target_pairs={{0,8},{1,5},{2,10},{3,7},{4,12},{5,1},{6,14},{7,3},{8,0},{9,13},{1... | collective-permute-start | bytes 1769480 | tf_op jit(solution)/shard_map/ppermute | solution.py:143
  98.8 1.9 collective-permute-start.14
  98.8 2.5 %collective-permute-start.13 = (bf16[256,768]{1,0:T(8,128)(2,1)}, bf16[256,768]{1,0:T(8,128)(2,1)S(1)}, u32[]{:S(2)}, u32[]{:S(2)}) collective-permute-start(bf16[256,768]{1,0:T(8,128)(2,1)} %get-tuple-element.139.refs_0_), channel_id=1, source_target_pairs={{0,1},{1,0},{2,3},{3,2},{4,5},{5,4},{6,7},{7,6},{8,9},{9,8},{10,11... | collective-permute-start | bytes 1179656 | tf_op jit(solution)/shard_map/ppermute | solution.py:107
  100.7 0.8 copy-start.6
  101.3 0.7 copy-start.7
  129.2 15.4 %collective-permute-start.15 = (bf16[256,768]{1,0:T(8,128)(2,1)}, bf16[256,768]{1,0:T(8,128)(2,1)}, u32[]{:S(2)}, u32[]{:S(2)}) collective-permute-start(bf16[256,768]{1,0:T(8,128)(2,1)} %get-tuple-element.154), channel_id=1, source_target_pairs={{0,2},{1,3},{2,0},{3,1},{4,6},{5,7},{6,4},{7,5},{8,10},{9,11},{10,... | collective-permute-start | bytes 1179656 | tf_op jit(solution)/shard_map/ppermute | solution.py:107
  130.4 10.6 %collective-permute-start.16 = (bf16[416,768]{1,0:T(8,128)(2,1)}, bf16[416,768]{1,0:T(8,128)(2,1)S(1)}, u32[]{:S(2)}, u32[]{:S(2)}) collective-permute-start(bf16[416,768]{1,0:T(8,128)(2,1)} %get-tuple-element.156), channel_id=1, source_target_pairs={{0,4},{1,9},{2,6},{3,11},{4,0},{5,13},{6,2},{7,15},{8,12},{9,1},{1... | collective-permute-start | bytes 1916936 | tf_op jit(solution)/shard_map/ppermute | solution.py:143
  131.7 4.6 %collective-permute-start.17 = (bf16[512,768]{1,0:T(8,128)(2,1)}, bf16[512,768]{1,0:T(8,128)(2,1)S(1)}, u32[]{:S(2)}, u32[]{:S(2)}) collective-permute-start(bf16[512,768]{1,0:T(8,128)(2,1)} %get-tuple-element.158), channel_id=1, source_target_pairs={{0,1},{1,0},{2,3},{3,2},{4,5},{5,4},{6,7},{7,6},{8,9},{9,8},{10,11... | collective-permute-start | bytes 2359304 | tf_op jit(solution)/shard_map/ppermute | solution.py:107
  133.6 16.7 %collective-permute-start.20 = (bf16[192,768]{1,0:T(8,128)(2,1)S(1)}, bf16[192,768]{1,0:T(8,128)(2,1)S(1)}, u32[]{:S(2)}, u32[]{:S(2)}) collective-permute-start(bf16[192,768]{1,0:T(8,128)(2,1)S(1)} %get-tuple-element.161), channel_id=1, source_target_pairs={{0,16},{1,17},{2,18},{3,19},{4,20},{5,21},{6,22},{7,23},{8,24},{9,... | collective-permute-start | bytes 884744 | tf_op jit(solution)/shard_map/ppermute | solution.py:143
  143.0 7.4 %copy-start.14 = (bf16[256,768]{1,0:T(8,128)(2,1)S(1)}, bf16[256,768]{1,0:T(8,128)(2,1)}, u32[]{:S(2)}) copy-start(bf16[256,768]{1,0:T(8,128)(2,1)} %get-tuple-element.168) | copy-start | bytes 1179652
  143.0 20.5 %collective-permute-start.21 = (bf16[224,768]{1,0:T(8,128)(2,1)S(1)}, bf16[224,768]{1,0:T(8,128)(2,1)S(1)}, u32[]{:S(2)}, u32[]{:S(2)}) collective-permute-start(bf16[224,768]{1,0:T(8,128)(2,1)S(1)} %get-tuple-element.166), channel_id=1, source_target_pairs={{0,8},{1,5},{2,10},{3,7},{4,12},{5,1},{6,14},{7,3},{8,0},{9,13},{1... | collective-permute-start | bytes 1032200 | tf_op jit(solution)/shard_map/ppermute | solution.py:143
  150.4 10.7 %collective-permute-start.19 = (bf16[256,768]{1,0:T(8,128)(2,1)S(1)}, bf16[256,768]{1,0:T(8,128)(2,1)S(1)}, u32[]{:S(2)}, u32[]{:S(2)}) collective-permute-start(bf16[256,768]{1,0:T(8,128)(2,1)S(1)} %copy-done.14), channel_id=1, source_target_pairs={{0,2},{1,3},{2,0},{3,1},{4,6},{5,7},{6,4},{7,5},{8,10},{9,11},{10,... | collective-permute-start | bytes 1179656 | tf_op jit(solution)/shard_map/ppermute | solution.py:107
  153.0 20.3 %collective-permute-start.23 = (bf16[192,768]{1,0:T(8,128)(2,1)}, bf16[192,768]{1,0:T(8,128)(2,1)S(1)}, u32[]{:S(2)}, u32[]{:S(2)}) collective-permute-start(bf16[192,768]{1,0:T(8,128)(2,1)} %add.41.own_ref), channel_id=1, source_target_pairs={{0,16},{1,17},{2,18},{3,19},{4,20},{5,21},{6,22},{7,23},{8,24},{9,... | collective-permute-start | bytes 884744 | tf_op jit(solution)/shard_map/ppermute | solution.py:143
  165.2 12.0 %collective-permute-start.22 = (bf16[128,768]{1,0:T(8,128)(2,1)S(1)}, bf16[128,768]{1,0:T(8,128)(2,1)S(1)}, u32[]{:S(2)}, u32[]{:S(2)}) collective-permute-start(bf16[128,768]{1,0:T(8,128)(2,1)S(1)} %get-tuple-element.176), channel_id=1, source_target_pairs={{0,16},{1,17},{2,18},{3,19},{4,20},{5,21},{6,22},{7,23},{8,24},{9,... | collective-permute-start | bytes 589832 | tf_op jit(solution)/shard_map/ppermute | solution.py:143
  175.1 18.4 %collective-permute-start.28 = (bf16[384,768]{1,0:T(8,128)(2,1)}, bf16[384,768]{1,0:T(8,128)(2,1)S(1)}, u32[]{:S(2)}, u32[]{:S(2)}) collective-permute-start(bf16[384,768]{1,0:T(8,128)(2,1)} %join.4.own_ref), channel_id=1, source_target_pairs={{0,8},{1,5},{2,10},{3,7},{4,12},{5,1},{6,14},{7,3},{8,0},{9,13},{1... | collective-permute-start | bytes 1769480 | tf_op jit(solution)/shard_map/ppermute | solution.py:143
  178.8 9.6 %collective-permute-start.25 = (bf16[96,768]{1,0:T(8,128)(2,1)}, bf16[96,768]{1,0:T(8,128)(2,1)S(1)}, u32[]{:S(2)}, u32[]{:S(2)}) collective-permute-start(bf16[96,768]{1,0:T(8,128)(2,1)} %get-tuple-element.181.own_ref), channel_id=1, source_target_pairs={{0,16},{1,17},{2,18},{3,19},{4,20},{5,21},{6,22},{7,23},{8,24},{9,... | collective-permute-start | bytes 442376 | tf_op jit(solution)/shard_map/ppermute | solution.py:143
  190.1 6.9 %collective-permute-start.27 = (bf16[192,768]{1,0:T(8,128)(2,1)}, bf16[192,768]{1,0:T(8,128)(2,1)S(1)}, u32[]{:S(2)}, u32[]{:S(2)}) collective-permute-start(bf16[192,768]{1,0:T(8,128)(2,1)} %join.5.own_ref), channel_id=1, source_target_pairs={{0,8},{1,5},{2,10},{3,7},{4,12},{5,1},{6,14},{7,3},{8,0},{9,13},{1... | collective-permute-start | bytes 884744 | tf_op jit(solution)/shard_map/ppermute | solution.py:143
  191.0 1.2 copy-start.8
  191.0 1.2 collective-permute-start.24
  195.7 3.8 %copy-start.9 = (f32[8,768]{1,0:T(8,128)S(1)}, f32[8,768]{1,0:T(8,128)}, u32[]{:S(2)}) copy-start(f32[8,768]{1,0:T(8,128)} %add.42.left_ref) | copy-start | bytes 73732
  195.7 16.4 %collective-permute-start.30 = (bf16[768,768]{1,0:T(8,128)(2,1)}, bf16[768,768]{1,0:T(8,128)(2,1)S(1)}, u32[]{:S(2)}, u32[]{:S(2)}) collective-permute-start(bf16[768,768]{1,0:T(8,128)(2,1)} %join.6.own_ref), channel_id=1, source_target_pairs={{0,4},{1,9},{2,6},{3,11},{4,0},{5,13},{6,2},{7,15},{8,12},{9,1},{1... | collective-permute-start | bytes 3538952 | tf_op jit(solution)/shard_map/ppermute | solution.py:143
  198.8 19.7 %collective-permute-start.29 = (bf16[384,768]{1,0:T(8,128)(2,1)}, bf16[384,768]{1,0:T(8,128)(2,1)S(1)}, u32[]{:S(2)}, u32[]{:S(2)}) collective-permute-start(bf16[384,768]{1,0:T(8,128)(2,1)} %join.7.own_ref), channel_id=1, source_target_pairs={{0,4},{1,9},{2,6},{3,11},{4,0},{5,13},{6,2},{7,15},{8,12},{9,1},{1... | collective-permute-start | bytes 1769480 | tf_op jit(solution)/shard_map/ppermute | solution.py:143
  199.6 3.8 %collective-permute-start.26 = (f32[8,768]{1,0:T(8,128)S(1)}, f32[8,768]{1,0:T(8,128)S(1)}, u32[]{:S(2)}, u32[]{:S(2)}) collective-permute-start(f32[8,768]{1,0:T(8,128)S(1)} %copy-done.9), channel_id=1, source_target_pairs={{0,2},{1,3},{2,0},{3,1},{4,6},{5,7},{6,4},{7,5},{8,10},{9,11},{10,... | collective-permute-start | bytes 73736 | tf_op jit(solution)/shard_map/ppermute | solution.py:107
where the time goes:
time: 223 us; the launch traced here: 221 us
  Pallas kernels  104 us (47%)
  waiting for transfers between devices  77.1 us (35%)
  starting transfers between devices  22.3 us (10%)
  local copies, waits for them, and re-layouts  11 us (5%)
  other arithmetic  4.73 us (2%)
    pallas_call x23, Pallas kernels, run(): return call(*args[:prefetch], *given)  104 us
    ppermute x12, waiting for transfers between devices, swap_dp(): return lax.ppermute(value, ('dp', 'tensor'), route)  41.6 us
    ppermute x19, waiting for transfers between devices, swap_tensor(): return lax.ppermute(value, 'tensor', [(i, i ^ bit) for i in range(size)])  35.5 us
    ppermute x12, starting transfers between devices, swap_dp(): return lax.ppermute(value, ('dp', 'tensor'), route)  11.2 us
    ppermute x19, starting transfers between devices, swap_tensor(): return lax.ppermute(value, 'tensor', [(i, i ^ bit) for i in range(size)])  11 us
  transfers between devices with their start and end apart: 31, of which 19 were waited for; matrix products, arithmetic and copies ran while one was open for 6% of the time, Pallas kernels for 37%

commit v1 on v0

--- a/solution.py
+++ b/solution.py
@@ -16,6 +16,19 @@
 FAR = pltpu.HBM
 HEAVY = pl.CostEstimate(flops=10**11, bytes_accessed=1024, transcendentals=0)
 LIGHT = pl.CostEstimate(flops=1024, bytes_accessed=1024, transcendentals=0)
+ORDER = (
+    "swap_dn", "feed1", "sum_dn", "feed2", "back", "feed3",
+    "swap_out", "swap_in", "two1", "feed4", "two2", "go_mixed",
+    "feed5", "two3", "end_tokens", "gains_a", "two4", "end_mixed",
+    "gains_b", "two5", "end_feed", "end_heads",
+)
+LONG = (
+    "feed", "end_heads", "end_tokens", "feed4", "swap_out", "two2",
+)
+
+
+def cost_of(name):
+    return HEAVY if name in LONG else LIGHT
 GELU_SCALE = 0.7978845608028654
 GELU_CUBE = 0.044715
 
@@ -177,7 +190,7 @@
             refs[2 + k][...] = total.astype(BF16)
 
 
-def add_pieces(left, right, count):
+def add_pieces(left, right, count, cost=LIGHT):
     rows, cols = left.shape
     part = pl.BlockSpec((rows // count, cols), lambda i: (i, 0))
     return local_call(
@@ -188,6 +201,7 @@
         out_shape=[FAR((rows // count, cols), BF16)] * count,
         mib=10,
         name="add_pieces",
+        cost=cost,
     )(left, Came(right))
 
 
@@ -197,7 +211,7 @@
     swapped_ref[...] = total
 
 
-def add_swap(left, right, count, flip):
+def add_swap(left, right, count, flip, cost=LIGHT):
     rows, cols = left.shape
     part = pl.BlockSpec((rows // count, cols), lambda i: (i, 0))
     return local_call(
@@ -208,6 +222,7 @@
         out_shape=[FAR((rows, cols), BF16), FREE((rows, cols), BF16)],
         mib=10,
         name="add_swap",
+        cost=cost,
     )(left, Came(right))
 
 
@@ -456,6 +471,14 @@
     )(side, own, Came(came))
 
 
+def group_scale(groups_ref, own_ref):
+    own = groups_ref[own_ref[0]]
+    alike = jnp.int32(0)
+    for row in range(groups_ref.shape[0]):
+        alike += (groups_ref[row] == own).astype(jnp.int32)
+    return lax.rsqrt(jnp.full((1, LANES), alike.astype(F32)))[:, 0:1]
+
+
 def norm_rows(values):
     return lax.rsqrt(jnp.mean(values * values, axis=-1, keepdims=True) + NORM_EPS)
 
@@ -475,8 +498,8 @@
     heads, count, length_ref, starts_ref, table_ref, buckets_ref, gain_ref, wq_ref, wk_ref, wv_ref, *refs
 ):
     tok_refs = refs[:count]
-    (ctx_ref, exps_ref, linv_ref, normed_ref, tok_all_ref, q_ref, v_ref, k_turned_ref) = refs[count : count + 8]
-    k_ref, v_turned_ref, bias_ref, all_normed, scores_ref = refs[count + 8 :]
+    (ctx_ref, packed_ref, exps_ref, linv_ref, normed_ref, tok_all_ref) = refs[count : count + 6]
+    (q_ref, v_ref, k_turned_ref, k_ref, v_turned_ref, bias_ref, all_normed, scores_ref) = refs[count + 6 :]
     step = pl.program_id(0)
     blk = ctx_ref.shape[0]
     seq = blk * count
@@ -500,7 +523,7 @@
         ones_v = jnp.where(lane < 2, 1.0, 0.0)
         for b in range(count):
             values = tok_refs[b][...].astype(F32)
-            normed = (values * norm_rows(values) * gain_ref[...]).astype(BF16)
+            normed = (values * norm_rows(values) * gain_ref[0:1]).astype(BF16)
             rows = slice(b * blk, (b + 1) * blk)
             all_normed[rows] = normed
             masked = first & (row + starts_ref[b] >= length_ref[0])
@@ -548,8 +571,18 @@
         inverse = 1.0 / mixed[:, width : width + 1]
         outs.append(mixed[:, :width] * inverse)
         linv = jnp.where(stat_lane == h, inverse, linv)
-    ctx_ref[...] = jnp.concatenate(outs, axis=1).astype(BF16)
+    ctx = jnp.concatenate(outs, axis=1).astype(BF16)
+    ctx_ref[...] = ctx
     linv_ref[...] = linv
+    packed_ref[pl.ds(row0, blk)] = ctx[:, :LANES]
+    rest = head_cols - LANES
+    for k in range(count):
+
+        @pl.when(step == k)
+        def _():
+            place = seq + (k % (count // 2)) * blk
+            lanes = (k // (count // 2)) * rest
+            packed_ref[place : place + blk, lanes : lanes + rest] = ctx[:, LANES:]
 
 
 def attend(length, starts, table, buckets, gain, w_query, w_key, w_value, tok):
@@ -559,15 +592,16 @@
     heads = table.shape[1]
     head_cols = w_query.shape[0]
     smem = pl.BlockSpec(memory_space=pltpu.SMEM)
-    flops = 2 * seq * (3 * model * head_cols + 2 * seq * head_cols)
+    assert 2 * (head_cols - LANES) == LANES
     return local_call(
         functools.partial(attend_kernel, heads, count),
         grid=(count,),
-        in_specs=[smem, smem, smem, vmem_whole((8, 2 * seq)), vmem_whole((1, model))]
+        in_specs=[smem, smem, smem, vmem_whole((8, 2 * seq)), vmem_whole((2, model))]
         + [vmem_whole((head_cols, model))] * 3
         + [vmem_whole((blk, model))] * count,
         out_specs=[
             pl.BlockSpec((blk, head_cols), lambda i: (i, 0)),
+            vmem_whole((seq * 3 // 2, LANES)),
             pl.BlockSpec((heads, seq, blk), lambda i: (0, 0, i)),
             pl.BlockSpec((blk, LANES), lambda i: (i, 0)),
             pl.BlockSpec((blk, model), lambda i: (i, 0)),
@@ -578,6 +612,7 @@
         ],
         out_shape=[
             FAR((seq, head_cols), BF16),
+            FAR((seq * 3 // 2, LANES), BF16),
             FAR((heads, seq, seq), BF16),
             FAR((seq, LANES), F32),
             FAR((seq, model), BF16),
@@ -599,7 +634,7 @@
     )(length, starts, table, buckets, gain, w_query, w_key, w_value, tok[0], *tok[1:])
 
 
-def feed_kernel(count, side_ref, scale_ref, gain_ref, *refs):
+def feed_kernel(count, side_ref, groups_ref, own_ref, gain_ref, *refs):
     tok_far, ctx_far, refs = refs[0], refs[1 : 1 + count], refs[1 + count :]
     w_in_far, w_back_far, joined_far, refs = refs[0], refs[1], refs[2 : 2 + count], refs[2 + count :]
     hidden_ref, unit_ref, spread_ref, dn_low_ref, dn_high_ref, out_low_ref, out_high_ref, send_far, keep_far = refs[:9]
@@ -607,108 +642,122 @@
     normed_turned, hidden_now, halves, sems, out_sems = refs[18:]
     step = pl.program_id(0)
     blk = hidden_ref.shape[0]
-    units = w_in_ref.shape[1]
-    head_cols = ctx_all.shape[2]
-    many, fewer = units // 2, normed_turned.shape[0] // 2
-
-    def copy(far, near, sem):
-        return pltpu.make_async_copy(far, near, sems.at[sem])
-
-    def block_copies(b):
+    half = count // 2
+    span = blk * half
+    units, model = w_back_ref.shape
+    rest = LANES // 2
+    many, fewer = units // 2, model // 2
+    used = 0
+
+    def copy(far, near):
+        nonlocal used
+        used += 1
+        return pltpu.make_async_copy(far, near, sems.at[used - 1])
+
+    row_copies, out_copies, grad_copies = [], [], []
+    for b in range(count):
         rows = pl.ds(b * blk, blk)
-        found = [copy(tok_far.at[rows], tok_all.at[rows], b)]
+        found = [copy(tok_far.at[rows], tok_all.at[rows])]
         for k in range(count):
-            found.append(copy(ctx_far[k].at[pl.ds((b ^ k) * blk, blk)], ctx_all.at[k, rows], count * (1 + k) + b))
-        return found
-
-    first_sem = count * (1 + count)
-    out_copies, grad_copies = [], []
+            c = b ^ k
+            found.append(copy(ctx_far[k].at[pl.ds(c * blk, blk)], ctx_all.at[k, rows, pl.ds(0, LANES)]))
+            place = pl.ds(count * blk + (c % half) * blk, blk)
+            found.append(copy(ctx_far[k].at[place], ctx_all.at[k, rows, pl.ds(LANES, LANES)]))
+        row_copies.append(found)
+        grad_copies.append(copy(joined_far[b].at[pl.ds(0, blk)], grad_all.at[rows]))
     for k in range(count):
-        place = w_out_ref.at[pl.ds(k * head_cols, head_cols)]
-        out_copies.append(copy(joined_far[k].at[pl.ds(blk, head_cols)], place, first_sem + k))
-        place = grad_all.at[pl.ds(k * blk, blk)]
-        grad_copies.append(copy(joined_far[k].at[pl.ds(0, blk)], place, first_sem + count + k))
-    in_copy = copy(w_in_far, w_in_ref, first_sem + 2 * count)
-    back_copy = copy(w_back_far, w_back_ref, first_sem + 2 * count + 1)
+        for side in range(2):
+            place = w_out_ref.at[side, k, pl.ds(0, LANES)]
+            out_copies.append(copy(joined_far[k].at[pl.ds(blk, LANES)], place))
+            place = w_out_ref.at[side, k, pl.ds(LANES + side * rest, rest)]
+            out_copies.append(copy(joined_far[k].at[pl.ds(blk + LANES, rest)], place))
+    in_copy = copy(w_in_far, w_in_ref)
+    back_copy = copy(w_back_far, w_back_ref)
 
     @pl.when(step == 0)
     def _():
-        for one in [*block_copies(0), *out_copies, in_copy, grad_copies[0], back_copy]:
+        early = [one for b in range(half) for one in row_copies[b]]
+        late = [one for b in range(half, count) for one in row_copies[b]]
+        for one in [*out_copies, *early, in_copy, *grad_copies[:half], back_copy, *late, *grad_copies[half:]]:
             one.start()
-        for b in range(1, count):
-            for one in [*block_copies(b), grad_copies[b]]:
-                one.start()
+        for side in range(2):
+            for k in range(count):
+                other = LANES + (1 - side) * rest
+                w_out_ref[side, k, other : other + rest] = jnp.zeros((rest, model), BF16)
         for one in out_copies:
             one.wait()
 
-    for b in range(count):
-
-        @pl.when(step == b)
+    for part in range(2):
+
+        @pl.when(step == part)
         def _():
-            for one in block_copies(b):
-                one.wait()
-
-    rows = pl.ds(pl.multiple_of(step * blk, blk), blk)
-    hidden = tok_all[rows].astype(F32)
-    for slot in range(count):
-        hidden = hidden + dot_nn(ctx_all[slot, rows], w_out_ref[slot * head_cols : (slot + 1) * head_cols])
-    hidden_now[...] = hidden
+            for b in range(part * half, (part + 1) * half):
+                for one in row_copies[b]:
+                    one.wait()
+
+    rows = pl.ds(pl.multiple_of(step * span, span), span)
+    for b in range(half):
+        now = slice(b * blk, (b + 1) * blk)
+        block = step * half + b
+        there = pl.ds(pl.multiple_of(block * blk, blk), blk)
+        hidden = tok_all[there].astype(F32)
+        for k in range(count):
+            side = (block ^ k) // half
+            hidden = hidden + dot_nn(ctx_all[k, there], w_out_ref[side, k])
+        hidden_now[now] = hidden
     strip = 32 if blk % 32 == 0 else blk
-    for r in range(0, blk, strip):
+    for r in range(0, span, strip):
         some = slice(r, r + strip)
         hidden = hidden_now[some]
         spread = norm_rows(hidden)
         unit = hidden * spread
         unit_ref[some] = unit.astype(BF16)
         spread_ref[some] = jnp.broadcast_to(spread, (strip, LANES))
-        active_now[some, : unit.shape[1]] = (unit * gain_ref[...]).astype(BF16)
-    normed = active_now[:, : hidden.shape[1]]
+        active_now[some, :model] = (unit * gain_ref[1:2]).astype(BF16)
+    normed = active_now[:, :model]
     normed_turned[:, rows] = normed.T
 
     @pl.when(step == 0)
     def _():
-        hidden_ref[...] = hidden_now[...]
+        hidden_ref[...] = hidden_now[0:blk]
         in_copy.wait()
         back_copy.wait()
 
-    for b in range(count):
-
-        @pl.when(step == b)
+    for part in range(2):
+
+        @pl.when(step == part)
         def _():
-            grad_copies[b].wait()
+            for b in range(part * half, (part + 1) * half):
+                grad_copies[b].wait()
 
     grad = grad_all[rows]
-    scale = scale_ref[0]
+    scale = group_scale(groups_ref, own_ref)
     part = 256 if units % 256 == 0 else units
-    normed = normed_turned[:, rows].T
-    for c in range(units // part):
-        cols = slice(c * part, (c + 1) * part)
-        up = dot_nn(normed, w_in_ref[:, cols])
+    ups = [dot_nn(normed, w_in_ref[:, c : c + part]) for c in range(0, units, part)]
+    for c, up in zip(range(0, units, part), ups, strict=True):
+        cols = slice(c, c + part)
         dactive = dot_nt(grad, w_back_ref[cols])
         square = up * up
         bend = jnp.tanh(up * (GELU_SCALE + GELU_SCALE * GELU_CUBE * square))
-        half = 0.5 + 0.5 * bend
-        active = (up * half).astype(BF16)
+        bell = 0.5 + 0.5 * bend
+        active = (up * bell).astype(BF16)
         steep = GELU_SCALE + 3.0 * GELU_SCALE * GELU_CUBE * square
-        slope = (half + (0.5 * up) * (1.0 - bend * bend) * steep) * scale
+        slope = (bell + (0.5 * up) * (1.0 - bend * bend) * steep) * scale
         active_now[:, cols] = active
         active_turned[cols, rows] = active.T
         dup_all[rows, cols] = (dactive * slope).astype(BF16)
     dnormed = dot_nt(dup_all[rows], w_in_ref[...]).astype(BF16)
     out = dot_nn(active_now[:, :units], w_back_ref[...]).astype(BF16)
 
-    @pl.when(step < count // 2)
+    @pl.when(step == 0)
     def _():
         dn_low_ref[...] = dnormed
         out_low_ref[...] = out
 
-    @pl.when(step >= count // 2)
+    @pl.when(step == 1)
     def _():
         dn_high_ref[...] = dnormed
         out_high_ref[...] = out
-
-    @pl.when(step == count - 1)
-    def _():
         going = []
         for k, (far, side) in enumerate(((send_far, 1 - side_ref[0]), (keep_far, side_ref[0]))):
             back = dot_nn(active_turned[pl.ds(side * many, many)], grad_all[...]) * scale
@@ -720,63 +769,57 @@
             one.wait()
 
 
-def feed(side, scale, gain, w_in, w_back, tok, ctx, joined):
+def feed(side, groups, own, gain, w_in, w_back, tok, ctx, joined):
     count = len(ctx)
     rows, model = tok.shape
     blk = rows // count
     units = w_in.shape[1]
-    head_cols = ctx[0].shape[1]
-    half = count // 2
-
-    by_row = pl.BlockSpec((blk, model), lambda i, side: (i, 0))
-    low = pl.BlockSpec((blk, model), lambda i, side: (jnp.minimum(i, half - 1), 0))
-    high = pl.BlockSpec((blk, model), lambda i, side: (jnp.maximum(i - half, 0), 0))
+    span = rows // 2
+    by_row = pl.BlockSpec((span, model), lambda i, side: (i, 0))
     anywhere = pl.BlockSpec(memory_space=pl.ANY)
+    smem = pl.BlockSpec(memory_space=pltpu.SMEM)
 
     def whole(shape):
         return pl.BlockSpec(shape, lambda i, side: (0, 0))
 
-    part_rows = FAR((rows // 2, model), BF16)
     grads = ((units + model) // 2, model)
+    copies = count * (4 + 2 * count) + 2 + 2 * count
     return local_call(
         functools.partial(feed_kernel, count),
-        grid=(count,),
-        in_specs=[pl.BlockSpec(memory_space=pltpu.SMEM), whole((1, model))] + [anywhere] * (3 + 2 * count),
+        grid=(2,),
+        in_specs=[smem, smem, whole((2, model))] + [anywhere] * (3 + 2 * count),
         out_specs=[
             whole((blk, model)),
             by_row,
-            pl.BlockSpec((blk, LANES), lambda i, side: (i, 0)),
-            low,
-            high,
-            low,
-            high,
+            pl.BlockSpec((span, LANES), lambda i, side: (i, 0)),
+            *[whole((span, model))] * 4,
             anywhere,
             anywhere,
         ],
         out_shape=[FAR((blk, model), F32), FAR((rows, model), BF16), FAR((rows, LANES), F32)]
-        + [part_rows] * 4
+        + [FAR((span, model), BF16)] * 4
         + [FAR(grads, BF16)] * 2,
         scratch_shapes=[
             pltpu.VMEM((rows, model), BF16),
-            pltpu.VMEM((count, rows, head_cols), BF16),
+            pltpu.VMEM((count, rows, 2 * LANES), BF16),
             pltpu.VMEM((model, units), BF16),
             pltpu.VMEM((units, model), BF16),
-            pltpu.VMEM((count * head_cols, model), BF16),
+            pltpu.VMEM((2, count, 2 * LANES, model), BF16),
             pltpu.VMEM((rows, model), BF16),
-            pltpu.VMEM((blk, max(units, model)), BF16),
+            pltpu.VMEM((span, max(units, model)), BF16),
             pltpu.VMEM((rows, units), BF16),
             pltpu.VMEM((units, rows), BF16),
             pltpu.VMEM((model, rows), BF16),
-            pltpu.VMEM((blk, model), F32),
+            pltpu.VMEM((span, model), F32),
             pltpu.VMEM((2, *grads), BF16),
-            pltpu.SemaphoreType.DMA((count * (3 + count) + 2,)),
+            pltpu.SemaphoreType.DMA((copies,)),
             pltpu.SemaphoreType.DMA((2,)),
         ],
         prefetch=1,
-        mib=44,
+        mib=52,
         name="feed",
-        cost=HEAVY,
-    )(side, scale, gain, tok, *ctx, w_in, w_back, *joined)
+        cost=cost_of("feed"),
+    )(side, groups, own, gain, tok, *ctx, w_in, w_back, *joined)
 
 
 def finish_mixed_kernel(hidden_ref, own_ref, came_ref, out_ref):
@@ -784,7 +827,7 @@
     out_ref[...] = (hidden_ref[...] + total).astype(BF16)
 
 
-def finish_mixed(hidden, own, came):
+def finish_mixed(hidden, own, came, cost=LIGHT):
     blk, model = own.shape
     place = pl.BlockSpec((blk, model), lambda i: (0, 0))
     return local_call(
@@ -795,6 +838,7 @@
         out_shape=jax.ShapeDtypeStruct((blk, model), BF16),
         mib=10,
         name="finish_mixed",
+        cost=cost,
     )(hidden, own, Came(came))
 
 
@@ -802,146 +846,174 @@
     dnormed = own_ref[...].astype(F32) + came_ref[...].astype(F32)
     values = tok_ref[...].astype(F32)
     spread = norm_rows(values)
-    out_ref[...] = dh_ref[...].astype(F32) + norm_back(dnormed, values * spread, spread, gain_ref[...])[0]
-
-
-def finish_tokens(gain, tok, own, came, dh_own):
+    out_ref[...] = dh_ref[...].astype(F32) + norm_back(dnormed, values * spread, spread, gain_ref[0:1])[0]
+
+
+def finish_tokens(gain, tok, own, came, dh_own, cost=LIGHT):
     blk, model = own.shape
     steps = 2 if blk % 32 == 0 else 1
     place = pl.BlockSpec((blk // steps, model), lambda i: (i, 0))
     return local_call(
         finish_tokens_kernel,
         grid=(steps,),
-        in_specs=[vmem_whole((1, model))] + [place] * 4,
+        in_specs=[vmem_whole((2, model))] + [place] * 4,
         out_specs=place,
         out_shape=jax.ShapeDtypeStruct((blk, model), F32),
         mib=10,
         name="finish_tokens",
+        cost=cost,
     )(gain, tok, own, Came(came), dh_own)
 
 
-def attend_back_kernel(heads, count, bucket_count, side_ref, starts_ref, scale_ref, gain_ref, buckets_ref, *refs):
-    dn_refs, refs = refs[:count], refs[count:]
-    (unit_ref, spread_ref, ctx_ref, linv_ref, exps_ref), refs = refs[:5], refs[5:]
-    far_refs, refs = refs[: 9 + count], refs[9 + count :]
-    (dh_own_ref, small_ref, send_ref, keep_ref, in_low_ref, in_high_ref), refs = refs[:6], refs[6:]
-    near_refs, refs = refs[:10], refs[10:]
-    w_out_ref, q_ref, v_ref, k_turned_ref, normed_ref, wq_ref, wk_ref, wv_ref, tok_ref, grad_all = near_refs
-    dk_ref, dv_ref, acc_ref, ds_ref, given_ref, dh_all, ctx_all, dn_now, dj_ref, sums_ref, sems = refs
-    block, h = pl.program_id(0), pl.program_id(1)
-    blk = dn_now.shape[0]
-    seq = blk * count
-    head_cols = ctx_ref.shape[1]
+def attend_back_kernel(heads, count, side_ref, starts_ref, groups_ref, own_ref, gain_ref, buckets_ref, *refs):
+    dn_far, joined_far, refs = refs[:count], refs[count : 2 * count], refs[2 * count :]
+    unit_far, spread_far, ctx_far, linv_far, exps_far, w_out_far, refs = *refs[:6], refs[6:]
+    late_far, refs = refs[:8], refs[8:]
+    dh_own_far, small_far, send_far, keep_far, in_low_far, in_high_far, refs = *refs[:6], refs[6:]
+    dn_all, grad_all, unit_all, spread_all, ctx_all, linv_all, exps_all, w_out_ref, refs = *refs[:8], refs[8:]
+    late_near, refs = refs[:8], refs[8:]
+    v_ref, q_ref, k_turned_ref, normed_ref, tok_ref, wq_ref, wk_ref, wv_ref = late_near
+    dk_ref, dv_ref, acc_ref, ds_ref, given_ref, dh_all, dj_ref, sums_ref, in_all, halves, sems, out_sems = refs
+    block = pl.program_id(0)
+    seq, model = dh_all.shape
+    blk = seq // count
+    head_cols = ctx_all.shape[1]
     width = head_cols // heads
     wide = acc_ref.shape[2]
-    copies = [pltpu.make_async_copy(far_refs[k], near_refs[k], sems.at[k]) for k in range(9)]
-    for k in range(count):
-        place = grad_all.at[pl.ds(k * blk, blk)]
-        copies.append(pltpu.make_async_copy(far_refs[9 + k].at[pl.ds(0, blk)], place, sems.at[9 + k]))
-    soon, later, last = [*copies[9:], copies[0]], copies[1:4], copies[4:9]
+    half_cols = 2 * head_cols
     strip = 32 if blk % 32 == 0 else blk
 
-    @pl.when((block == 0) & (h == 0))
-    def _():
-        for copy in [*soon, *later, *last]:
+    def first_copies(b):
+        rows = pl.ds(b * blk, blk)
+        pairs = [
+            (dn_far[b], dn_all.at[rows]),
+            (unit_far.at[rows], unit_all.at[rows]),
+            (spread_far.at[rows], spread_all.at[rows]),
+            (joined_far[b].at[pl.ds(0, blk)], grad_all.at[rows]),
+            (ctx_far.at[rows], ctx_all.at[rows]),
+            (linv_far.at[rows], linv_all.at[rows]),
+        ]
+        return [pltpu.make_async_copy(far, near, sems.at[7 * b + k]) for k, (far, near) in enumerate(pairs)]
+
+    def exps_copy(b):
+        cols = pl.ds(b * blk, blk)
+        return pltpu.make_async_copy(exps_far.at[:, :, cols], exps_all.at[b % 2], sems.at[7 * b + 6])
+
+    out_copy = pltpu.make_async_copy(w_out_far, w_out_ref, sems.at[7 * count])
+    late = [pltpu.make_async_copy(late_far[k], late_near[k], sems.at[7 * count + 1 + k]) for k in range(8)]
+
+    @pl.when(block == 0)
+    def _():
+        for copy in [*first_copies(0), out_copy, late[0], exps_copy(0), late[1], late[2], *first_copies(1)]:
             copy.start()
         dk_ref[...] = jnp.zeros_like(dk_ref)
         dv_ref[...] = jnp.zeros_like(dv_ref)
         acc_ref[...] = jnp.zeros_like(acc_ref)
-        for copy in soon:
-            copy.wait()
+
+    for b in range(count):
+
+        @pl.when(block == b)
+        def _():
+            if b + 1 < count:
+                exps_copy(b + 1).start()
+            if b == 0:
+                for k in range(2, count):
+                    for copy in first_copies(k):
+                        copy.start()
+                for copy in late[3:]:
+                    copy.start()
+            for copy in first_copies(b):
+                copy.wait()
+            if b == 0:
+                out_copy.wait()
 
     row0 = pl.multiple_of(block * blk, blk)
     now = pl.ds(row0, blk)
-
-    @pl.when(h == 0)
-    def _():
+    scale = group_scale(groups_ref, own_ref)
+    for r in range(0, blk, strip):
+        there = pl.ds(pl.multiple_of(row0 + r, strip), strip)
+        unit = unit_all[there].astype(F32)
+        scaled = gain_ref[1:2] * dn_all[there].astype(F32)
+        inner = jnp.mean(scaled * unit, axis=-1, keepdims=True)
+        dhidden = spread_all[there, 0:1] * (scaled - unit * inner)
+        dh_all[there] = (dhidden + grad_all[there].astype(F32) * scale).astype(BF16)
+
+    dctx = dot_nt(dh_all[now], w_out_ref[...])
+    product = dctx * ctx_all[now].astype(F32)
+    lane = lax.broadcasted_iota(jnp.int32, (blk, LANES - width), 1)
+    for h in range(heads):
+        cols = slice(h * width, (h + 1) * width)
+        inverse = linv_all[now, h : h + 1]
+        inner = -jnp.sum(product[:, cols], axis=1, keepdims=True) * inverse
+        coarse = inner.astype(BF16).astype(F32)
+        extra = jnp.where(lane == 0, coarse, jnp.where(lane == 1, inner - coarse, 0.0))
+        given_ref[h] = jnp.concatenate((dctx[:, cols] * inverse, extra), axis=1).astype(BF16)
+
+    @pl.when(block == 0)
+    def _():
+        total = jnp.zeros((1, model), F32)
+        for r in range(0, blk, strip):
+            product = unit_all[r : r + strip].astype(F32) * dn_all[r : r + strip].astype(F32)
+            total += jnp.sum(product, axis=0, keepdims=True)
+        sums_ref[...] = jnp.zeros_like(sums_ref)
+        sums_ref[12:16] = jnp.broadcast_to(total, (4, model))
+        pltpu.make_async_copy(dh_all.at[pl.ds(0, blk)], dh_own_far, out_sems.at[0]).start()
+        for copy in late[:3]:
+            copy.wait()
+
+    for b in range(count):
+
+        @pl.when(block == b)
+        def _():
+            exps_copy(b).wait()
+
+    slot = lax.rem(block, 2)
+    first_query = starts_ref[block]
+    dquery = []
+    for h in range(heads):
+        given = given_ref[h]
         for b in range(count):
-
-            @pl.when(block == b)
-            def _():
-                dn_now[...] = dn_refs[b][...]
-
-        for r in range(0, blk, strip):
-            some = slice(r, r + strip)
-            there = pl.ds(pl.multiple_of(row0 + r, strip), strip)
-            unit = unit_ref[some].astype(F32)
-            scaled = gain_ref[...] * dn_now[some].astype(F32)
-            inner = jnp.mean(scaled * unit, axis=-1, keepdims=True)
-            dhidden = spread_ref[some, 0:1] * (scaled - unit * inner)
-            dh_all[there] = (dhidden + grad_all[there].astype(F32) * scale_ref[0]).astype(BF16)
-
-        @pl.when(block == 0)
-        def _():
-            total = jnp.zeros((1, dn_now.shape[1]), F32)
-            for r in range(0, blk, strip):
-                some = slice(r, r + strip)
-                product = unit_ref[some].astype(F32) * dn_now[some].astype(F32)
-                total += jnp.sum(product, axis=0, keepdims=True)
-            sums_ref[...] = jnp.zeros_like(sums_ref)
-            sums_ref[12:16] = jnp.broadcast_to(total, (4, total.shape[1]))
-            dh_own_ref[...] = dh_all[0:blk]
-
-        ctx_all[now] = ctx_ref[...]
-        dctx = dot_nt(dh_all[now], w_out_ref[...])
-        product = dctx * ctx_ref[...].astype(F32)
-        lane = lax.broadcasted_iota(jnp.int32, (blk, LANES - width), 1)
-        for k in range(heads):
-            cols = slice(k * width, (k + 1) * width)
-            inverse = linv_ref[:, k : k + 1]
-            inner = -jnp.sum(product[:, cols], axis=1, keepdims=True) * inverse
-            coarse = inner.astype(BF16).astype(F32)
-            extra = jnp.where(lane == 0, coarse, jnp.where(lane == 1, inner - coarse, 0.0))
-            given_ref[k] = jnp.concatenate((dctx[:, cols] * inverse, extra), axis=1).astype(BF16)
-
-    @pl.when((block == 0) & (h == 0))
-    def _():
-        for copy in later:
+            for a in range(blk // LANES):
+                rows = slice(b * blk + a * LANES, b * blk + (a + 1) * LANES)
+                dscores = exps_all[slot, h, rows].astype(F32) * dot_nt(v_ref[h, rows], given)
+                ds_ref[h, rows] = dscores.astype(BF16)
+                start = bias_lanes(seq, starts_ref[b] + a * LANES, first_query)
+                acc_ref[h, :, pl.ds(start, blk)] += dscores
+        dk_ref[h] += dot_nn(ds_ref[h], q_ref[h, now])
+        dv_ref[h] += dot_nn(exps_all[slot, h], given)
+        dquery.append(dot_nn(k_turned_ref[h], ds_ref[h]).T[:, :width])
+    dj_ref[0, now] = jnp.concatenate(dquery, axis=1).astype(BF16)
+
+    @pl.when(block == count - 1)
+    def _():
+        dj_ref[1] = jnp.concatenate([dk_ref[h][:, :width] for h in range(heads)], axis=1).astype(BF16)
+        dj_ref[2] = jnp.concatenate([dv_ref[h][:, :width] for h in range(heads)], axis=1).astype(BF16)
+        going = [pltpu.make_async_copy(dh_all.at[pl.ds(0, blk)], dh_own_far, out_sems.at[0])]
+
+        def send_out(near, far):
+            going.append(pltpu.make_async_copy(near, far, out_sems.at[len(going)]))
+            going[-1].start()
+
+        for copy in late[3:]:
             copy.wait()
-
-    given = given_ref[h]
-    first_query = starts_ref[block]
-    for b in range(count):
-        for a in range(blk // LANES):
-            rows = slice(b * blk + a * LANES, b * blk + (a + 1) * LANES)
-            dscores = exps_ref[0, rows].astype(F32) * dot_nt(v_ref[h, rows], given)
-            ds_ref[rows] = dscores.astype(BF16)
-            start = bias_lanes(seq, starts_ref[b] + a * LANES, first_query)
-            acc_ref[h, :, pl.ds(start, blk)] += dscores
-    dk_ref[h] += dot_nn(ds_ref[...], q_ref[h, now])
-    dv_ref[h] += dot_nn(exps_ref[0], given)
-    dquery = dot_nn(k_turned_ref[h], ds_ref[...]).T[:, :width].astype(BF16)
-    for k in range(heads):
-
-        @pl.when(h == k)
-        def _():
-            dj_ref[0, now, k * width : (k + 1) * width] = dquery
-
-    @pl.when((block == count - 1) & (h == heads - 1))
-    def _():
-        dj_ref[1] = jnp.concatenate([dk_ref[k][:, :width] for k in range(heads)], axis=1).astype(BF16)
-        dj_ref[2] = jnp.concatenate([dv_ref[k][:, :width] for k in range(heads)], axis=1).astype(BF16)
-        for copy in last:
-            copy.wait()
-        gain_total = jnp.zeros((1, tok_ref.shape[1]), F32)
+        gain_total = jnp.zeros((1, model), F32)
         for b in range(count):
             rows = slice(b * blk, (b + 1) * blk)
             dnormed = dot_nn(dj_ref[0, rows], wq_ref[...])
             dnormed = dnormed + dot_nn(dj_ref[1, rows], wk_ref[...])
             dnormed = dnormed + dot_nn(dj_ref[2, rows], wv_ref[...])
-            out = (in_low_ref, in_high_ref)[b // (count // 2)]
-            base = (b % (count // 2)) * blk
+            in_all[rows] = dnormed.astype(BF16)
             for r in range(0, blk, strip):
-                some = slice(r, r + strip)
                 values = tok_ref[b * blk + r : b * blk + r + strip].astype(F32)
-                gain_total += jnp.sum(dnormed[some] * (values * norm_rows(values)), axis=0, keepdims=True)
-                out[base + r : base + r + strip] = dnormed[some].astype(BF16)
-        sums_ref[8:12] = jnp.broadcast_to(gain_total, (4, gain_total.shape[1]))
-
-        which = buckets_ref[...]
+                product = dnormed[r : r + strip] * (values * norm_rows(values))
+                gain_total += jnp.sum(product, axis=0, keepdims=True)
+        send_out(in_all.at[pl.ds(0, seq // 2)], in_low_far)
+        send_out(in_all.at[pl.ds(seq // 2, seq // 2)], in_high_far)
+        sums_ref[8:12] = jnp.broadcast_to(gain_total, (4, model))
+
         drel = []
-        for k in range(heads):
-            part = acc_ref[k]
+        for h in range(heads):
+            part = acc_ref[h]
             rows = LANES
             while rows > 1:
                 rows //= 2
@@ -949,82 +1021,84 @@
             drel.append(pltpu.roll(part, LANES - 1, 1))
         drel = jnp.concatenate(drel + [jnp.zeros((8 - heads, wide), F32)], axis=0)
         bucket = lax.broadcasted_iota(jnp.int32, (LANES, wide), 0)
-        onehot = jnp.where(bucket == jnp.broadcast_to(which[0:1], (LANES, wide)), 1.0, 0.0).astype(BF16)
+        onehot = jnp.where(bucket == jnp.broadcast_to(buckets_ref[0:1], (LANES, wide)), 1.0, 0.0).astype(BF16)
         table = jnp.zeros((8, LANES), F32)
         for _ in range(3):
             coarse = drel.astype(BF16)
             table = table + dot_nt(jnp.concatenate((coarse, jnp.zeros_like(coarse)), axis=0), onehot)[:8]
             drel = drel - coarse.astype(F32)
         sums_ref[0:8, 0:LANES] = table
-        small = split_small(sums_ref[...])
-        small_ref[...] = small
-        for side in range(2):
-
-            @pl.when(side_ref[0] == side)
+        halves[0, half_cols:] = split_small(sums_ref[...])
+        send_out(halves.at[0, pl.ds(half_cols, 2 * SMALL)], small_far)
+        side = side_ref[0]
+        for k in range(2):
+
+            @pl.when((side == 0) == (k == 1))
             def _():
-                near, other = (keep_ref, send_ref) if side == 0 else (send_ref, keep_ref)
-                near[:head_cols] = dot_tn(dj_ref[0], normed_ref[...]).astype(BF16)
-                near[head_cols : 2 * head_cols] = dot_tn(dj_ref[1], normed_ref[...]).astype(BF16)
-                other[:head_cols] = dot_tn(dj_ref[2], normed_ref[...]).astype(BF16)
-                other[head_cols : 2 * head_cols] = dot_tn(ctx_all[...], dh_all[...]).astype(BF16)
-
-        send_ref[2 * head_cols :] = small
-
-
-def attend_back(bucket_count, side, starts, scale, gain, w_out, buckets, dn, unit, spread, joined, ctx, linv, exps, q, v, k_turned, normed, weights, tok):
+                halves[k, :head_cols] = dot_tn(dj_ref[0], normed_ref[...]).astype(BF16)
+                halves[k, head_cols:half_cols] = dot_tn(dj_ref[1], normed_ref[...]).astype(BF16)
+
+            @pl.when((side == 0) == (k == 0))
+            def _():
+                halves[k, :head_cols] = dot_tn(dj_ref[2], normed_ref[...]).astype(BF16)
+                halves[k, head_cols:half_cols] = dot_tn(ctx_all[...], dh_all[...]).astype(BF16)
+
+            if k == 0:
+                send_out(halves.at[0], send_far)
+            else:
+                send_out(halves.at[1, pl.ds(0, half_cols)], keep_far)
+        for copy in going:
+            copy.wait()
+
+
+def attend_back(cost, bucket_count, side, starts, groups, own, gain, w_out, buckets, dn, unit, spread, joined, ctx, linv, exps, q, v, k_turned, normed, weights, tok):
     head_cols, model = w_out.shape
     count = starts.shape[0]
     heads, seq = exps.shape[:2]
     assert bucket_count <= LANES and heads <= 8
     blk = seq // count
 
-    def block(cols):
-        return pl.BlockSpec((blk, cols), lambda i, h, side: (i, 0))
-
     def whole(shape):
-        return pl.BlockSpec(shape, lambda i, h, side: (0,) * len(shape))
-
-    near = [w_out, q, v, k_turned, normed, *weights, tok]
+        return pl.BlockSpec(shape, lambda i, side: (0,) * len(shape))
+
+    def room(value):
+        return pltpu.VMEM(value.shape, value.dtype)
+
+    first = [unit, spread, ctx, linv]
+    late = [v, q, k_turned, normed, tok, *weights]
     smem = pl.BlockSpec(memory_space=pltpu.SMEM)
+    anywhere = pl.BlockSpec(memory_space=pl.ANY)
     extra = 2 * SMALL
     outs = [(blk, model), (extra, model), (2 * head_cols + extra, model), (2 * head_cols, model), (seq // 2, model), (seq // 2, model)]
     return local_call(
-        functools.partial(attend_back_kernel, heads, count, bucket_count),
-        grid=(count, heads),
-        in_specs=[
-            smem,
-            smem,
-            whole((1, model)),
-            whole((8, 2 * seq)),
-            *[whole((blk, model))] * count,
-            block(model),
-            block(LANES),
-            block(head_cols),
-            block(LANES),
-            pl.BlockSpec((1, seq, blk), lambda i, h, side: (h, 0, i)),
-            *[pl.BlockSpec(memory_space=pl.ANY)] * (len(near) + count),
-        ],
-        out_specs=[whole(shape) for shape in outs],
+        functools.partial(attend_back_kernel, heads, count),
+        grid=(count,),
+        in_specs=[smem, smem, smem, whole((2, model)), whole((8, 2 * seq))] + [anywhere] * (2 * count + 6 + len(late)),
+        out_specs=[anywhere] * len(outs),
         out_shape=[FAR(shape, BF16) for shape in outs],
-        scratch_shapes=[pltpu.VMEM(a.shape, a.dtype) for a in near]
+        scratch_shapes=[pltpu.VMEM((seq, model), BF16), pltpu.VMEM((seq, model), BF16)]
+        + [room(a) for a in first]
+        + [pltpu.VMEM((2, heads, seq, blk), BF16), room(w_out)]
+        + [room(a) for a in late]
         + [
-            pltpu.VMEM((seq, model), BF16),
             pltpu.VMEM((heads, seq, LANES), F32),
             pltpu.VMEM((heads, seq, LANES), F32),
             pltpu.VMEM((heads, LANES, 2 * seq), F32),
-            pltpu.VMEM((seq, blk), BF16),
+            pltpu.VMEM((heads, seq, blk), BF16),
             pltpu.VMEM((heads, blk, LANES), BF16),
             pltpu.VMEM((seq, model), BF16),
-            pltpu.VMEM((seq, head_cols), BF16),
-            pltpu.VMEM((blk, model), BF16),
             pltpu.VMEM((3, seq, head_cols), BF16),
             pltpu.VMEM((SMALL, model), F32),
-            pltpu.SemaphoreType.DMA((len(near) + count,)),
+            pltpu.VMEM((seq, model), BF16),
+            pltpu.VMEM((2, 2 * head_cols + extra, model), BF16),
+            pltpu.SemaphoreType.DMA((7 * count + 1 + len(late),)),
+            pltpu.SemaphoreType.DMA((6,)),
         ],
         prefetch=1,
         mib=52,
         name="attend_back",
-    )(side, starts, scale, gain, buckets, *dn, unit, spread, ctx, linv, exps, *near, *joined)
+        cost=cost,
+    )(side, starts, groups, own, gain, buckets, *dn, *joined, *first, exps, w_out, *late)
 
 
 def shards(
@@ -1055,14 +1129,12 @@
     here = lax.axis_index("tensor")
     starts = (here ^ jnp.array(block_order(count), jnp.int32)) * blk
     weights = (w_query.T, w_key.T, w_value.T)
-    gain_attn = gain_attn[None, :]
-    gain_ffn = gain_ffn[None, :]
+    gains = jnp.stack((gain_attn, gain_ffn))
+    own_row = lax.axis_index("dp")[None]
     turned = jnp.pad(rel_buckets[::-1], (0, 1), constant_values=-1)
     buckets = jnp.broadcast_to(turned[None], (8, 2 * seq))
     first_side = side_of(dp_steps(lax.axis_size("dp"))[0])
 
-    own_group = lax.dynamic_slice_in_dim(task_groups, lax.axis_index("dp"), 1)
-    scale = lax.rsqrt(jnp.sum((own_group == task_groups).astype(F32)))[None]
     positions = here * blk + jnp.arange(blk, dtype=jnp.int32)
     keep = (positions < row_lengths[0]) & (instruction_mask[0] == 0)
     masked_grad = jnp.where(keep[:, None], out_grad[0], 0).astype(BF16)
@@ -1082,43 +1154,49 @@
 
     own_tok = tokens[0]
     joined = jnp.concatenate((masked_grad, w_out))
-    ready = (joined, starts, scale, buckets, gain_attn, gain_ffn, rel_table)
+    ready = (joined, starts, buckets, gains, own_row, rel_table)
     tok, ready = gather_tensor(own_tok, count, ready)
-    joined, starts, scale, buckets, gain_attn, gain_ffn, rel_table = ready
+    joined, starts, buckets, both_gains, own_row, rel_table = ready
     joined = [joined]
     for bit in low_bits:
         joined = joined + [swap_tensor(piece, bit) for piece in joined]
-    ctx, exps, linv, normed, tok_all, q, v, k_turned = turn.done(
-        attend(row_lengths, starts, rel_table, buckets, gain_attn, *weights, tok)
+    ctx, packed, exps, linv, normed, tok_all, q, v, k_turned = turn.done(
+        attend(row_lengths, starts, rel_table, buckets, both_gains, *weights, tok)
     )
-    contexts, _ = gather_tensor(ctx, count)
+    contexts, _ = gather_tensor(packed, count)
     joined = [turn(piece) for piece in joined]
     joined = joined + [swap_tensor(piece, bits[-1]) for piece in joined]
     hidden, unit, spread, dn_low, dn_high, out_low, out_high, feed_send, feed_keep = turn.done(
-        feed(first_side, scale, gain_ffn, w_in, w_back, tok_all, contexts, joined)
+        feed(first_side, task_groups, own_row, both_gains, w_in, w_back, tok_all, contexts, joined)
     )
     dn_came = swap_tensor(dn_high, bits[-1])
     out_came = swap_tensor(out_high, bits[-1])
     sum_feed = DpSum(turn, feed_send, feed_keep, finish_feed)
-
     assert half == 2 and len(low_bits) == 1
     flip = block_order(count).index(low_bits[0])
-    dn_low, dn_sent = turn.done(add_swap(dn_low, turn(dn_came), half, flip))
-    dn_came = swap_tensor(dn_sent, low_bits[0])
-    out_own = turn.done(add_pieces(out_low, turn(out_came), half))
-    sum_feed.step(HEAVY)
-    dn_low = turn.done(add_pieces(dn_low, turn(dn_came), half))
-    dn_high = [swap_tensor(piece, bits[-1]) for piece in dn_low]
-    dh_own, small, heads_send, heads_keep, dn_low, dn_high = turn.done(
-        attend_back(
+    got = {}
+
+    def swap_dn(cost):
+        got["dn"], sent = turn.done(add_swap(dn_low, turn(dn_came), half, flip, cost))
+        got["dn_came"] = swap_tensor(sent, low_bits[0])
+
+    def sum_dn(cost):
+        got["dn"] = turn.done(add_pieces(got["dn"], turn(got["dn_came"]), half, cost))
+        got["dn_far"] = [swap_tensor(piece, bits[-1]) for piece in got["dn"]]
+
+    def back(cost):
+        dn = [*got["dn"], *[turn(piece) for piece in got["dn_far"]]]
+        results = attend_back(
+            cost,
             bucket_count,
             first_side,
             starts,
-            scale,
-            gain_ffn,
+            task_groups,
+            own_row,
+            both_gains,
             w_out,
             buckets,
-            [*dn_low, *[turn(piece) for piece in dn_high]],
+            dn,
             unit,
             spread,
             joined,
@@ -1132,44 +1210,76 @@
             weights,
             tok_all,
         )
+        got["dh"], small, send, keep, got["in_low"], in_high = turn.done(results)
+        got["two"] = DpSum(turn, send, keep, finish_heads, small)
+        got["in_came"] = swap_tensor(in_high, bits[-1])
+
+    def swap_in(cost):
+        own, other = turn.done(add_pieces(got["in_low"], turn(got["in_came"]), half, cost))
+        got["in_own"], got["in_came"] = own, swap_tensor(other, low_bits[0])
+
+    def end_tokens(cost):
+        args = (both_gains, own_tok, got["in_own"], turn(got["in_came"]), got["dh"], cost)
+        got["tokens"] = turn.done(finish_tokens(*args))[None]
+
+    def swap_out(cost):
+        got["out_own"], got["out_other"] = turn.done(add_pieces(out_low, turn(out_came), half, cost))
+
+    def go_mixed(cost):
+        got["out_came"] = swap_tensor(turn(got["out_other"]), low_bits[0])
+
+    def end_mixed(cost):
+        got["mixed"] = turn.done(finish_mixed(hidden, got["out_own"], turn(got["out_came"]), cost))[None]
+
+    def start_gains():
+        while got["two"].at < len(got["two"].pairs):
+            got["two"].step()
+        got["gains"] = got["two"].small[SMALL // 2 :]
+        got["gains_came"] = swap_tensor(got["gains"], bits[-1])
+
+    def gains_a(cost):
+        got["gains"] = turn.done(add(got["gains"], turn(got["gains_came"]), cost))
+        got["gains_came"] = swap_tensor(got["gains"], low_bits[0])
+
+    def gains_b(cost):
+        got["gains"] = turn.done(add(got["gains"], turn(got["gains_came"]), cost))
+
+    stages = dict(
+        swap_dn=swap_dn,
+        sum_dn=sum_dn,
+        back=back,
+        swap_in=swap_in,
+        end_tokens=end_tokens,
+        swap_out=swap_out,
+        go_mixed=go_mixed,
+        end_mixed=end_mixed,
+        gains_a=gains_a,
+        gains_b=gains_b,
+        end_heads=lambda cost: got["two"].rest(),
+        end_feed=lambda cost: sum_feed.rest(),
     )
-    sum_heads = DpSum(turn, heads_send, heads_keep, finish_heads, small)
-    dn_came = swap_tensor(dn_high, bits[-1])
-    out_own, out_came = across([turn(piece) for piece in out_own])
-    sum_feed.step(HEAVY)
-    dn_own = turn.done(add_pieces(dn_low, turn(dn_came), half))
-    dn_own, dn_came = across(dn_own)
-    sum_heads.step(HEAVY)
-    mixed = turn.done(finish_mixed(hidden, out_own, turn(out_came)))[None]
-    sum_feed.step(HEAVY)
-    grad_tokens = turn.done(finish_tokens(gain_attn, own_tok, dn_own, turn(dn_came), dh_own))[None]
-    sum_heads.step(HEAVY)
-    sum_feed.step()
-    sum_heads.step(HEAVY)
-    while sum_heads.at < len(sum_heads.pairs):
-        sum_heads.step(HEAVY)
-    gains = sum_heads.small[SMALL // 2 :]
-    gains_came = swap_tensor(gains, bits[-1])
-    sum_heads.step()
-    gains = turn.done(add(gains, turn(gains_came)))
-    for bit in reversed(low_bits):
-        gains_came = swap_tensor(gains, bit)
-    sum_feed.step()
-    sum_heads.step(HEAVY)
-    gains = turn.done(add(gains, turn(gains_came)))
-    dtable = sum_heads.small
-    grad_back, grad_in = sum_feed.rest()
-    grad_query, grad_key, grad_value, grad_out = sum_heads.rest()
+    for name in ORDER:
+        cost = cost_of(name)
+        if name in stages:
+            stages[name](cost)
+        elif name.startswith("feed"):
+            sum_feed.step(cost)
+        else:
+            got["two"].step(cost)
+            if name == "two3":
+                start_gains()
+    grad_query, grad_key, grad_value, grad_out = got["two"].result
+    grad_back, grad_in = sum_feed.result
     return (
-        mixed,
-        grad_tokens,
-        gains[0],
+        got["mixed"],
+        got["tokens"],
+        got["gains"][0],
         grad_query.T,
         grad_key.T,
         grad_value.T,
-        dtable[:heads, :bucket_count].T,
+        got["two"].small[:heads, :bucket_count].T,
         grad_out,
-        gains[4],
+        got["gains"][4],
         grad_in,
         grad_back,
     )

time: 223 us -> 197 us (0.88)
  waiting for transfers between devices: 77.1 us -> 61.1 us
  Pallas kernels: 104 us -> 101 us
  local copies, waits for them, and re-layouts: 11 us -> 8.13 us
    ppermute x19, waiting for transfers between devices: 35.5 us -> 25.1 us  [swap_tensor(): return lax.ppermute(value, 'tensor', [(i, i ^ bit) for i in range(size)])]
    ppermute x12, waiting for transfers between devices: 41.6 us -> 36 us  [swap_dp(): return lax.ppermute(value, ('dp', 'tensor'), route)]
    pallas_call x23, Pallas kernels: 104 us -> 101 us  [run(): return call(*args[:prefetch], *given)]
    broadcast_in_dim x2 -> x0, local copies, waits for them, and re-layouts: 2.54 us -> none  [the longest x1 1.27 us: shards(): gain_attn = gain_attn[None, :]]
  transfers between devices with their start and end apart: 31 -> 31, of which waited for: 19 -> 16; matrix products, arithmetic and copies ran while one was open for 6% -> 5% of each run, Pallas kernels for 37% -> 40%
where the time goes in v1:
time: 197 us; the launch traced here: 196 us
  Pallas kernels  101 us (51%)
  waiting for transfers between devices  61.1 us (31%)
  starting transfers between devices  21.5 us (11%)
  local copies, waits for them, and re-layouts  8.13 us (4%)
  other arithmetic  3.42 us (2%)
    pallas_call x23, Pallas kernels, run(): return call(*args[:prefetch], *given)  101 us
    ppermute x12, waiting for transfers between devices, swap_dp(): return lax.ppermute(value, ('dp', 'tensor'), route)  36 us
    ppermute x19, waiting for transfers between devices, swap_tensor(): return lax.ppermute(value, 'tensor', [(i, i ^ bit) for i in range(size)])  25.1 us
    ppermute x12, starting transfers between devices, swap_dp(): return lax.ppermute(value, ('dp', 'tensor'), route)  11.3 us
    ppermute x19, starting transfers between devices, swap_tensor(): return lax.ppermute(value, 'tensor', [(i, i ^ bit) for i in range(size)])  10.2 us
  transfers between devices with their start and end apart: 31, of which 16 were waited for; matrix products, arithmetic and copies ran while one was open for 5% of the time, Pallas kernels for 40%

profile of v1, /device:TPU:0, one launch (start us, length us, event | category | flops | bytes accessed | tf_op | source)
XLA Modules:
  0.0 196.3 jit_solution(8573447605916222889)
XLA Ops:
  0.7 3.0 %collective-permute-start.1 = (bf16[256,768]{1,0:T(8,128)(2,1)}, bf16[256,768]{1,0:T(8,128)(2,1)S(1)}, u32[]{:S(2)}, u32[]{:S(2)}) collective-permute-start(bf16[256,768]{1,0:T(8,128)(2,1)} %bitcast.31), channel_id=1, source_target_pairs={{0,2},{1,3},{2,0},{3,1},{4,6},{5,7},{6,4},{7,5},{8,10},{9,11},{10,... | collective-permute-start | bytes 1179656 | tf_op jit(solution)/shard_map/ppermute | solution.py:120
  4.4 0.7 compare_reduce_fusion
  5.1 0.7 stack.10
  5.7 0.7 stack.9
  6.4 1.1 bitcast_select_fusion
  8.1 0.8 reverse
  9.0 1.0 pad_maximum_fusion.refs_7_.refs_4_
  10.0 3.0 %collective-permute-done.1.refs_1_ = bf16[256,768]{1,0:T(8,128)(2,1)S(1)} collective-permute-done((bf16[256,768]{1,0:T(8,128)(2,1)}, bf16[256,768]{1,0:T(8,128)(2,1)S(1)}, u32[]{:S(2)}, u32[]{:S(2)}) %collective-permute-start.1) | collective-permute-done | bytes 393248 | tf_op jit(solution)/shard_map/ppermute | solution.py:120
  13.0 0.7 broadcast_in_dim.55.buckets_ref
  13.7 1.7 collective-permute-done.2.refs_3_
  15.5 1.7 collective-permute-start.6
  17.3 17.2 %attend.1 = (bf16[1024,192]{1,0:T(8,128)(2,1)}, bf16[1536,128]{1,0:T(8,128)(2,1)}, bf16[3,1024,1024]{2,1,0:T(8,128)(2,1)}, f32[1024,128]{1,0:T(8,128)}, bf16[102...) custom-call(s32[1]{0:T(128)} %copy.28.length_ref, ...), custom_call_target="tpu_custom_call" | custom-call | flops 99999997952 | bytes 1024 | tf_op jit(solution)/shard_map/attend/pallas_call | solution.py:67
  34.4 0.7 collective-permute-start.3
  35.7 9.9 %collective-permute-done.3.refs_2_ = bf16[1536,128]{1,0:T(8,128)(2,1)S(1)} collective-permute-done((bf16[1536,128]{1,0:T(8,128)(2,1)}, bf16[1536,128]{1,0:T(8,128)(2,1)S(1)}, u32[]{:S(2)}, u32[]{:S(2)}) %collective-permute-start.3) | collective-permute-done | bytes 393248 | tf_op jit(solution)/shard_map/ppermute | solution.py:120
  45.6 1.8 collective-permute-done.5.refs_4_
  47.5 0.8 copy-done.4
  48.3 19.4 %feed.1 = (f32[256,768]{1,0:T(8,128)}, bf16[1024,768]{1,0:T(8,128)(2,1)}, f32[1024,128]{1,0:T(8,128)}, bf16[512,768]{1,0:T(8,128)(2,1)}, bf16[512,768]{1,0:T(8,1...) custom-call(s32[1]{0:T(128)} %bitcast.side_ref, ...), custom_call_target="tpu_custom_call" | custom-call | flops 99999997952 | bytes 1024 | tf_op jit(solution)/shard_map/feed/pallas_call | solution.py:67
  67.7 1.6 collective-permute-start.10
  69.3 2.5 %collective-permute-done.11.right_ref = bf16[512,768]{1,0:T(8,128)(2,1)S(1)} collective-permute-done((bf16[512,768]{1,0:T(8,128)(2,1)}, bf16[512,768]{1,0:T(8,128)(2,1)S(1)}, u32[]{:S(2)}, u32[]{:S(2)}) %collective-permute-start.11) | collective-permute-done | bytes 786464 | tf_op jit(solution)/shard_map/ppermute | solution.py:120
  71.7 2.0 %add_swap.1 = (bf16[512,768]{1,0:T(8,128)(2,1)}, bf16[512,768]{1,0:T(8,128)(2,1)S(1)}) custom-call(bf16[512,768]{1,0:T(8,128)(2,1)} %get-tuple-element.126.left_ref, bf16[512,768]{1,0:T(8,128)(2,1)S(1)} %collective-permute-done.11.right_ref), custom_call_target="tpu_custom_call" | custom-call | flops 1024 | bytes 1024 | tf_op jit(solution)/shard_map/add_swap/pallas_call | solution.py:67
  73.7 0.9 collective-permute-start.13
  74.6 9.5 %collective-permute-done.10.came_ref = bf16[768,768]{1,0:T(8,128)(2,1)S(1)} collective-permute-done((bf16[768,768]{1,0:T(8,128)(2,1)}, bf16[768,768]{1,0:T(8,128)(2,1)S(1)}, u32[]{:S(2)}, u32[]{:S(2)}) %collective-permute-start.10) | collective-permute-done | bytes 1179680 | tf_op jit(solution)/shard_map/ppermute | solution.py:156
  84.2 2.7 %fold.2 = (bf16[384,768]{1,0:T(8,128)(2,1)}, bf16[384,768]{1,0:T(8,128)(2,1)}) custom-call(s32[1]{0:T(128)} %bitcast.9.side_ref, bf16[768,768]{1,0:T(8,128)(2,1)} %get-tuple-element.124.kept_ref, bf16[768,768]{1,0:T(8,128)(2,1)S(1)} %collective-permute-done.10.came_ref), custom_call_target="tpu_custom_call" | custom-call | flops 1024 | bytes 1024 | tf_op jit(solution)/shard_map/fold/pallas_call | solution.py:67
  86.9 1.6 collective-permute-start.12
  88.4 4.9 %collective-permute-done.13.refs_1_ = bf16[512,768]{1,0:T(8,128)(2,1)S(1)} collective-permute-done((bf16[512,768]{1,0:T(8,128)(2,1)S(1)}, bf16[512,768]{1,0:T(8,128)(2,1)S(1)}, u32[]{:S(2)}, u32[]{:S(2)}) %collective-permute-start.13) | collective-permute-done | bytes 786464 | tf_op jit(solution)/shard_map/ppermute | solution.py:120
  93.3 2.1 %add_pieces.3 = (bf16[256,768]{1,0:T(8,128)(2,1)}, bf16[256,768]{1,0:T(8,128)(2,1)}) custom-call(bf16[512,768]{1,0:T(8,128)(2,1)} %get-tuple-element.129.refs_0_, bf16[512,768]{1,0:T(8,128)(2,1)S(1)} %collective-permute-done.13.refs_1_), custom_call_target="tpu_custom_call" | custom-call | flops 1024 | bytes 1024 | tf_op jit(solution)/shard_map/add_pieces/pallas_call | solution.py:67
  95.9 1.0 collective-permute-done.12.came_ref
  97.0 2.0 %fold.3 = (bf16[192,768]{1,0:T(8,128)(2,1)S(1)}, bf16[192,768]{1,0:T(8,128)(2,1)}) custom-call(s32[1]{0:T(128)} %bitcast.8.side_ref, bf16[384,768]{1,0:T(8,128)(2,1)} %get-tuple-element.131.kept_ref, bf16[384,768]{1,0:T(8,128)(2,1)S(1)} %collective-permute-done.12.came_ref), custom_call_target="tpu_custom_call" | custom-call | flops 1024 | bytes 1024 | tf_op jit(solution)/shard_map/fold/pallas_call | solution.py:67
  98.9 2.6 %collective-permute-start.14 = (bf16[192,768]{1,0:T(8,128)(2,1)S(1)}, bf16[192,768]{1,0:T(8,128)(2,1)S(1)}, u32[]{:S(2)}, u32[]{:S(2)}) collective-permute-start(bf16[192,768]{1,0:T(8,128)(2,1)S(1)} %get-tuple-element.138), channel_id=1, source_target_pairs={{0,16},{1,17},{2,18},{3,19},{4,20},{5,21},{6,22},{7,23},{8,24},{9,... | collective-permute-start | bytes 884744 | tf_op jit(solution)/shard_map/ppermute | solution.py:156
  101.5 0.7 copy-done.5
  102.4 23.1 %attend_back.1 = (bf16[256,768]{1,0:T(8,128)(2,1)}, bf16[32,768]{1,0:T(8,128)(2,1)}, bf16[416,768]{1,0:T(8,128)(2,1)}, bf16[384,768]{1,0:T(8,128)(2,1)}, bf16[51...) custom-call(s32[1]{0:T(128)} %bitcast.side_ref, s32[4]{0:T(128)S(1)} %xor_multiply_fusion.starts_ref, s32[8]{0:T(128)S(1)} %copy-done, ...), custom_call_target="tpu_custom_call" | custom-call | flops 1024 | bytes 1024 | tf_op jit(solution)/shard_map/attend_back/pallas_call | solution.py:67
  125.6 1.6 collective-permute-start.17
  127.2 1.7 add.37.own_ref
  129.3 2.1 %add_pieces.4 = (bf16[256,768]{1,0:T(8,128)(2,1)}, bf16[256,768]{1,0:T(8,128)(2,1)}) custom-call(bf16[512,768]{1,0:T(8,128)(2,1)} %get-tuple-element.122.refs_0_, bf16[512,768]{1,0:T(8,128)(2,1)S(1)} %collective-permute-done.9.refs_1_), custom_call_target="tpu_custom_call" | custom-call | flops 99999997952 | bytes 1024 | tf_op jit(solution)/shard_map/add_pieces/pallas_call | solution.py:67
  131.3 2.1 %add_pieces.5 = (bf16[256,768]{1,0:T(8,128)(2,1)}, bf16[256,768]{1,0:T(8,128)(2,1)}) custom-call(bf16[512,768]{1,0:T(8,128)(2,1)} %get-tuple-element.157.refs_0_, bf16[512,768]{1,0:T(8,128)(2,1)S(1)} %collective-permute-done.18.refs_1_), custom_call_target="tpu_custom_call" | custom-call | flops 1024 | bytes 1024 | tf_op jit(solution)/shard_map/add_pieces/pallas_call | solution.py:67
  133.4 2.9 %collective-permute-done.17.came_ref.small_came_ref = bf16[416,768]{1,0:T(8,128)(2,1)S(1)} collective-permute-done((bf16[416,768]{1,0:T(8,128)(2,1)}, bf16[416,768]{1,0:T(8,128)(2,1)S(1)}, u32[]{:S(2)}, u32[]{:S(2)}) %collective-permute-start.17) | collective-permute-done | bytes 639008 | tf_op jit(solution)/shard_map/ppermute | solution.py:156
  136.3 2.0 %fold_small.2 = (bf16[224,768]{1,0:T(8,128)(2,1)S(1)}, bf16[192,768]{1,0:T(8,128)(2,1)}, bf16[32,768]{1,0:T(8,128)(2,1)}) custom-call(s32[1]{0:T(128)} %bitcast.9.side_ref, bf16[384,768]{1,0:T(8,128)(2,1)} %get-tuple-element.155.kept_ref, bf16[416,768]{1,0:T(8,128)(2,1)S(1)} %collective-permute-done.17.came_ref.small_came_ref, ...), custom_call_target="tpu_custom_call" | custom-call | flops 1024 | bytes 1024 | tf_op jit(solution)/shard_map/fold_small/pallas_call | solution.py:67
  138.3 1.6 collective-permute-start.19
  139.9 5.8 %collective-permute-done.20.came_ref = bf16[192,768]{1,0:T(8,128)(2,1)S(1)} collective-permute-done((bf16[192,768]{1,0:T(8,128)(2,1)}, bf16[192,768]{1,0:T(8,128)(2,1)S(1)}, u32[]{:S(2)}, u32[]{:S(2)}) %collective-permute-start.20) | collective-permute-done | bytes 294944 | tf_op jit(solution)/shard_map/ppermute | solution.py:156
  145.7 1.8 join.4.own_ref
  147.5 0.9 collective-permute-start.26
  148.4 0.8 collective-permute-done.19.came_ref.small_came_ref
  149.1 1.8 fold_small.3
  150.9 1.1 collective-permute-start.21
  152.1 8.0 %collective-permute-done.23.came_ref = bf16[384,768]{1,0:T(8,128)(2,1)S(1)} collective-permute-done((bf16[384,768]{1,0:T(8,128)(2,1)}, bf16[384,768]{1,0:T(8,128)(2,1)S(1)}, u32[]{:S(2)}, u32[]{:S(2)}) %collective-permute-start.23) | collective-permute-done | bytes 589856 | tf_op jit(solution)/shard_map/ppermute | solution.py:156
  160.1 2.2 %join.5.own_ref = bf16[768,768]{1,0:T(8,128)(2,1)} custom-call(s32[1]{0:T(128)} %bitcast.9.side_ref, bf16[384,768]{1,0:T(8,128)(2,1)} %join.4.own_ref, bf16[384,768]{1,0:T(8,128)(2,1)S(1)} %collective-permute-done.23.came_ref), custom_call_target="tpu_custom_call" | custom-call | flops 1024 | bytes 1024 | tf_op jit(solution)/shard_map/join/pallas_call | solution.py:67
  162.3 1.7 collective-permute-start.30
  164.0 1.6 add_small.1
  165.6 0.7 slice.12.left_ref
  166.3 2.4 %finish_tokens.1 = f32[256,768]{1,0:T(8,128)} custom-call(f32[2,768]{1,0:T(2,128)} %pad_maximum_fusion.1.gain_ref, bf16[256,768]{1,0:T(8,128)(2,1)} %bitcast.34, bf16[256,768]{1,0:T(8,128)(2,1)} %get-tuple-element.160.own_ref, bf16[256,768]{1,0:T(8,128)(2,1)S(1)} %collective-permute-done.26.came_ref, bf16[256,768]{1,0:T(8,128)(2,1)} %get-tuple-element.150.dh_ref), custom_call_target="tpu_custom_call" | custom-call | flops 99999997952 | bytes 1024 | tf_op jit(solution)/shard_map/finish_tokens/pallas_call | solution.py:67
  168.7 1.4 add.38.left_ref
  170.1 3.0 %collective-permute-done.24.came_ref = bf16[96,768]{1,0:T(8,128)(2,1)S(1)} collective-permute-done((bf16[96,768]{1,0:T(8,128)(2,1)}, bf16[96,768]{1,0:T(8,128)(2,1)S(1)}, u32[]{:S(2)}, u32[]{:S(2)}) %collective-permute-start.24) | collective-permute-done | bytes 147488 | tf_op jit(solution)/shard_map/ppermute | solution.py:156
  173.1 1.6 join.6.own_ref
  174.8 0.6 collective-permute-start.27
  175.4 2.1 %finish_mixed.1 = bf16[256,768]{1,0:T(8,128)(2,1)} custom-call(f32[256,768]{1,0:T(8,128)} %get-tuple-element.121.hidden_ref, bf16[256,768]{1,0:T(8,128)(2,1)} %get-tuple-element.153.own_ref, bf16[256,768]{1,0:T(8,128)(2,1)S(1)} %collective-permute-done.21.came_ref), custom_call_target="tpu_custom_call" | custom-call | flops 1024 | bytes 1024 | tf_op jit(solution)/shard_map/finish_mixed/pallas_call | solution.py:67
  177.5 1.3 collective-permute-done.27.right_ref
  178.8 1.3 add.39
  180.2 1.5 collective-permute-done.28.came_ref
  181.7 1.8 join.7.own_ref
  183.8 1.3 slice_bitcast_fusion
  185.0 1.4 slice_reduce_fusion
  186.5 3.6 %finish_feed.1 = (f32[768,768]{1,0:T(8,128)}, f32[768,768]{1,0:T(8,128)}) custom-call(s32[1]{0:T(128)} %bitcast.side_ref, bf16[768,768]{1,0:T(8,128)(2,1)} %join.5.own_ref, bf16[768,768]{1,0:T(8,128)(2,1)S(1)} %collective-permute-done.30.came_ref), custom_call_target="tpu_custom_call" | custom-call | flops 1024 | bytes 1024 | tf_op jit(solution)/shard_map/finish_feed/pallas_call | solution.py:67
  190.1 3.5 %collective-permute-done.29.came_ref = bf16[384,768]{1,0:T(8,128)(2,1)S(1)} collective-permute-done((bf16[384,768]{1,0:T(8,128)(2,1)}, bf16[384,768]{1,0:T(8,128)(2,1)S(1)}, u32[]{:S(2)}, u32[]{:S(2)}) %collective-permute-start.29) | collective-permute-done | bytes 589856 | tf_op jit(solution)/shard_map/ppermute | solution.py:156
  193.6 2.7 %finish_heads.1 = (f32[192,768]{1,0:T(8,128)}, f32[192,768]{1,0:T(8,128)}, f32[192,768]{1,0:T(8,128)}, f32[192,768]{1,0:T(8,128)}) custom-call(s32[1]{0:T(128)} %bitcast.side_ref, bf16[384,768]{1,0:T(8,128)(2,1)} %join.7.own_ref, bf16[384,768]{1,0:T(8,128)(2,1)S(1)} %collective-permute-done.29.came_ref), custom_call_target="tpu_custom_call" | custom-call | flops 1024 | bytes 1024 | tf_op jit(solution)/shard_map/finish_heads/pallas_call | solution.py:67
  (71 shorter events, 2.9 us)
Async XLA Ops:
  0.6 9.4 %copy-start.16 = (s32[4]{0:T(128)S(1)}, s32[4]{0:T(128)}, u32[]{:S(2)}) copy-start(s32[4]{0:T(128)} %constant.56.clone) | copy-start | bytes 52
  0.7 14.8 %copy-start.8 = (f32[32,3]{0,1:T(4,128)S(1)}, f32[32,3]{0,1:T(4,128)}, u32[]{:S(2)}) copy-start(f32[32,3]{0,1:T(4,128)} %param.25) | copy-start | bytes 1156
  0.7 12.4 %collective-permute-start.1 = (bf16[256,768]{1,0:T(8,128)(2,1)}, bf16[256,768]{1,0:T(8,128)(2,1)S(1)}, u32[]{:S(2)}, u32[]{:S(2)}) collective-permute-start(bf16[256,768]{1,0:T(8,128)(2,1)} %bitcast.31), channel_id=1, source_target_pairs={{0,2},{1,3},{2,0},{3,1},{4,6},{5,7},{6,4},{7,5},{8,10},{9,11},{10,... | collective-permute-start | bytes 1179656 | tf_op jit(solution)/shard_map/ppermute | solution.py:120
  3.7 10.0 %collective-permute-start = (bf16[256,768]{1,0:T(8,128)(2,1)}, bf16[256,768]{1,0:T(8,128)(2,1)S(1)}, u32[]{:S(2)}, u32[]{:S(2)}) collective-permute-start(bf16[256,768]{1,0:T(8,128)(2,1)} %bitcast.32), channel_id=1, source_target_pairs={{0,1},{1,0},{2,3},{3,2},{4,5},{5,4},{6,7},{7,6},{8,9},{9,8},{10,11... | collective-permute-start | bytes 1179656 | tf_op jit(solution)/shard_map/ppermute | solution.py:120
  10.0 25.1 %copy-start.1 = (bf16[448,768]{1,0:T(8,128)(2,1)}, bf16[448,768]{1,0:T(8,128)(2,1)S(1)}, u32[]{:S(2)}) copy-start(bf16[448,768]{1,0:T(8,128)(2,1)S(1)} %pad_maximum_fusion.refs_7_.refs_4_) | copy-start | bytes 2064388
  13.0 4.2 %copy-start.12 = (bf16[256,768]{1,0:T(8,128)(2,1)}, bf16[256,768]{1,0:T(8,128)(2,1)S(1)}, u32[]{:S(2)}) copy-start(bf16[256,768]{1,0:T(8,128)(2,1)S(1)} %collective-permute-done.1.refs_1_) | copy-start | bytes 1179652
  13.7 1.7 collective-permute-start.2
  13.7 3.6 %copy-start.13 = (bf16[256,768]{1,0:T(8,128)(2,1)}, bf16[256,768]{1,0:T(8,128)(2,1)S(1)}, u32[]{:S(2)}) copy-start(bf16[256,768]{1,0:T(8,128)(2,1)S(1)} %collective-permute-done.refs_2_) | copy-start | bytes 1179652
  15.4 1.8 copy-start.15
  15.5 19.6 %collective-permute-start.6 = (bf16[448,768]{1,0:T(8,128)(2,1)S(1)}, bf16[448,768]{1,0:T(8,128)(2,1)S(1)}, u32[]{:S(2)}, u32[]{:S(2)}) collective-permute-start(bf16[448,768]{1,0:T(8,128)(2,1)S(1)} %pad_maximum_fusion.refs_7_.refs_4_), channel_id=1, source_target_pairs={{0,2},{1,3},{2,0},{3,1},{4,6},{5,7},{6,4},{7,5},{8,10},{9,11},{10,... | collective-permute-start | bytes 2064392 | tf_op jit(solution)/shard_map/ppermute | solution.py:120
  17.2 31.0 %copy-start = (s32[8]{0:T(128)S(1)}, s32[8]{0:T(128)}, u32[]{:S(2)}) copy-start(s32[8]{0:T(128)} %groups_ref.3) | copy-start | bytes 100
  34.4 11.1 %collective-permute-start.3 = (bf16[1536,128]{1,0:T(8,128)(2,1)}, bf16[1536,128]{1,0:T(8,128)(2,1)S(1)}, u32[]{:S(2)}, u32[]{:S(2)}) collective-permute-start(bf16[1536,128]{1,0:T(8,128)(2,1)} %get-tuple-element.116.refs_1_), channel_id=1, source_target_pairs={{0,2},{1,3},{2,0},{3,1},{4,6},{5,7},{6,4},{7,5},{8,10},{9,11},{10,... | collective-permute-start | bytes 1179656 | tf_op jit(solution)/shard_map/ppermute | solution.py:120
  35.1 10.5 %collective-permute-start.7 = (bf16[448,768]{1,0:T(8,128)(2,1)S(1)}, bf16[448,768]{1,0:T(8,128)(2,1)S(1)}, u32[]{:S(2)}, u32[]{:S(2)}) collective-permute-start(bf16[448,768]{1,0:T(8,128)(2,1)S(1)} %pad_maximum_fusion.refs_7_.refs_4_), channel_id=1, source_target_pairs={{0,1},{1,0},{2,3},{3,2},{4,5},{5,4},{6,7},{7,6},{8,9},{9,8},{10,11... | collective-permute-start | bytes 2064392 | tf_op jit(solution)/shard_map/ppermute | solution.py:120
  35.1 12.3 %copy-start.2 = (bf16[448,768]{1,0:T(8,128)(2,1)}, bf16[448,768]{1,0:T(8,128)(2,1)S(1)}, u32[]{:S(2)}) copy-start(bf16[448,768]{1,0:T(8,128)(2,1)S(1)} %collective-permute-done.6.refs_8_.refs_5_) | copy-start | bytes 2064388
  35.1 12.3 %collective-permute-start.8 = (bf16[448,768]{1,0:T(8,128)(2,1)S(1)}, bf16[448,768]{1,0:T(8,128)(2,1)S(1)}, u32[]{:S(2)}, u32[]{:S(2)}) collective-permute-start(bf16[448,768]{1,0:T(8,128)(2,1)S(1)} %collective-permute-done.6.refs_8_.refs_5_), channel_id=1, source_target_pairs={{0,1},{1,0},{2,3},{3,2},{4,5},{5,4},{6,7},{7,6},{8,9},{9,8},{10,11... | collective-permute-start | bytes 2064392 | tf_op jit(solution)/shard_map/ppermute | solution.py:120
  35.6 10.0 %collective-permute-start.4 = (bf16[1536,128]{1,0:T(8,128)(2,1)}, bf16[1536,128]{1,0:T(8,128)(2,1)S(1)}, u32[]{:S(2)}, u32[]{:S(2)}) collective-permute-start(bf16[1536,128]{1,0:T(8,128)(2,1)} %get-tuple-element.116.refs_1_), channel_id=1, source_target_pairs={{0,1},{1,0},{2,3},{3,2},{4,5},{5,4},{6,7},{7,6},{8,9},{9,8},{10,11... | collective-permute-start | bytes 1179656 | tf_op jit(solution)/shard_map/ppermute | solution.py:120
  45.6 1.9 copy-start.11
  45.6 1.9 collective-permute-start.5
  45.6 1.9 copy-start.14
  45.6 1.9 copy-start.3
  47.4 0.8 copy-start.4
  67.7 16.5 %collective-permute-start.10 = (bf16[768,768]{1,0:T(8,128)(2,1)}, bf16[768,768]{1,0:T(8,128)(2,1)S(1)}, u32[]{:S(2)}, u32[]{:S(2)}) collective-permute-start(bf16[768,768]{1,0:T(8,128)(2,1)} %get-tuple-element.125), channel_id=1, source_target_pairs={{0,4},{1,9},{2,6},{3,11},{4,0},{5,13},{6,2},{7,15},{8,12},{9,1},{1... | collective-permute-start | bytes 3538952 | tf_op jit(solution)/shard_map/ppermute | solution.py:156
  69.2 2.5 %collective-permute-start.11 = (bf16[512,768]{1,0:T(8,128)(2,1)}, bf16[512,768]{1,0:T(8,128)(2,1)S(1)}, u32[]{:S(2)}, u32[]{:S(2)}) collective-permute-start(bf16[512,768]{1,0:T(8,128)(2,1)} %get-tuple-element.127), channel_id=1, source_target_pairs={{0,1},{1,0},{2,3},{3,2},{4,5},{5,4},{6,7},{7,6},{8,9},{9,8},{10,11... | collective-permute-start | bytes 2359304 | tf_op jit(solution)/shard_map/ppermute | solution.py:120
  73.7 19.6 %collective-permute-start.13 = (bf16[512,768]{1,0:T(8,128)(2,1)S(1)}, bf16[512,768]{1,0:T(8,128)(2,1)S(1)}, u32[]{:S(2)}, u32[]{:S(2)}) collective-permute-start(bf16[512,768]{1,0:T(8,128)(2,1)S(1)} %get-tuple-element.133), channel_id=1, source_target_pairs={{0,2},{1,3},{2,0},{3,1},{4,6},{5,7},{6,4},{7,5},{8,10},{9,11},{10,... | collective-permute-start | bytes 2359304 | tf_op jit(solution)/shard_map/ppermute | solution.py:120
  86.9 10.1 %collective-permute-start.12 = (bf16[384,768]{1,0:T(8,128)(2,1)}, bf16[384,768]{1,0:T(8,128)(2,1)S(1)}, u32[]{:S(2)}, u32[]{:S(2)}) collective-permute-start(bf16[384,768]{1,0:T(8,128)(2,1)} %get-tuple-element.132), channel_id=1, source_target_pairs={{0,8},{1,5},{2,10},{3,7},{4,12},{5,1},{6,14},{7,3},{8,0},{9,13},{1... | collective-permute-start | bytes 1769480 | tf_op jit(solution)/shard_map/ppermute | solution.py:156
  88.4 40.8 %collective-permute-start.9 = (bf16[512,768]{1,0:T(8,128)(2,1)}, bf16[512,768]{1,0:T(8,128)(2,1)S(1)}, u32[]{:S(2)}, u32[]{:S(2)}) collective-permute-start(bf16[512,768]{1,0:T(8,128)(2,1)} %get-tuple-element.123), channel_id=1, source_target_pairs={{0,1},{1,0},{2,3},{3,2},{4,5},{5,4},{6,7},{7,6},{8,9},{9,8},{10,11... | collective-permute-start | bytes 2359304 | tf_op jit(solution)/shard_map/ppermute | solution.py:120
  95.4 6.1 %collective-permute-start.16 = (bf16[256,768]{1,0:T(8,128)(2,1)}, bf16[256,768]{1,0:T(8,128)(2,1)S(1)}, u32[]{:S(2)}, u32[]{:S(2)}) collective-permute-start(bf16[256,768]{1,0:T(8,128)(2,1)} %get-tuple-element.139.refs_1_), channel_id=1, source_target_pairs={{0,1},{1,0},{2,3},{3,2},{4,5},{5,4},{6,7},{7,6},{8,9},{9,8},{10,11... | collective-permute-start | bytes 1179656 | tf_op jit(solution)/shard_map/ppermute | solution.py:120
  95.4 6.1 %collective-permute-start.15 = (bf16[256,768]{1,0:T(8,128)(2,1)}, bf16[256,768]{1,0:T(8,128)(2,1)S(1)}, u32[]{:S(2)}, u32[]{:S(2)}) collective-permute-start(bf16[256,768]{1,0:T(8,128)(2,1)} %get-tuple-element.135.refs_0_), channel_id=1, source_target_pairs={{0,1},{1,0},{2,3},{3,2},{4,5},{5,4},{6,7},{7,6},{8,9},{9,8},{10,11... | collective-permute-start | bytes 1179656 | tf_op jit(solution)/shard_map/ppermute | solution.py:120
  98.9 28.3 %collective-permute-start.14 = (bf16[192,768]{1,0:T(8,128)(2,1)S(1)}, bf16[192,768]{1,0:T(8,128)(2,1)S(1)}, u32[]{:S(2)}, u32[]{:S(2)}) collective-permute-start(bf16[192,768]{1,0:T(8,128)(2,1)S(1)} %get-tuple-element.138), channel_id=1, source_target_pairs={{0,16},{1,17},{2,18},{3,19},{4,20},{5,21},{6,22},{7,23},{8,24},{9,... | collective-permute-start | bytes 884744 | tf_op jit(solution)/shard_map/ppermute | solution.py:156
  101.5 0.8 copy-start.5
  101.5 0.9 copy-start.6
  125.5 5.8 %collective-permute-start.18 = (bf16[512,768]{1,0:T(8,128)(2,1)}, bf16[512,768]{1,0:T(8,128)(2,1)S(1)}, u32[]{:S(2)}, u32[]{:S(2)}) collective-permute-start(bf16[512,768]{1,0:T(8,128)(2,1)} %get-tuple-element.158), channel_id=1, source_target_pairs={{0,1},{1,0},{2,3},{3,2},{4,5},{5,4},{6,7},{7,6},{8,9},{9,8},{10,11... | collective-permute-start | bytes 2359304 | tf_op jit(solution)/shard_map/ppermute | solution.py:120
  125.6 10.7 %collective-permute-start.17 = (bf16[416,768]{1,0:T(8,128)(2,1)}, bf16[416,768]{1,0:T(8,128)(2,1)S(1)}, u32[]{:S(2)}, u32[]{:S(2)}) collective-permute-start(bf16[416,768]{1,0:T(8,128)(2,1)} %get-tuple-element.156), channel_id=1, source_target_pairs={{0,4},{1,9},{2,6},{3,11},{4,0},{5,13},{6,2},{7,15},{8,12},{9,1},{1... | collective-permute-start | bytes 1916936 | tf_op jit(solution)/shard_map/ppermute | solution.py:156
  128.9 16.7 %collective-permute-start.20 = (bf16[192,768]{1,0:T(8,128)(2,1)}, bf16[192,768]{1,0:T(8,128)(2,1)S(1)}, u32[]{:S(2)}, u32[]{:S(2)}) collective-permute-start(bf16[192,768]{1,0:T(8,128)(2,1)} %add.37.own_ref), channel_id=1, source_target_pairs={{0,16},{1,17},{2,18},{3,19},{4,20},{5,21},{6,22},{7,23},{8,24},{9,... | collective-permute-start | bytes 884744 | tf_op jit(solution)/shard_map/ppermute | solution.py:156
  138.3 9.2 %copy-start.10 = (bf16[256,768]{1,0:T(8,128)(2,1)S(1)}, bf16[256,768]{1,0:T(8,128)(2,1)}, u32[]{:S(2)}) copy-start(bf16[256,768]{1,0:T(8,128)(2,1)} %get-tuple-element.176) | copy-start | bytes 1179652
  138.3 10.8 %collective-permute-start.19 = (bf16[224,768]{1,0:T(8,128)(2,1)S(1)}, bf16[224,768]{1,0:T(8,128)(2,1)S(1)}, u32[]{:S(2)}, u32[]{:S(2)}) collective-permute-start(bf16[224,768]{1,0:T(8,128)(2,1)S(1)} %get-tuple-element.164), channel_id=1, source_target_pairs={{0,8},{1,5},{2,10},{3,7},{4,12},{5,1},{6,14},{7,3},{8,0},{9,13},{1... | collective-permute-start | bytes 1032200 | tf_op jit(solution)/shard_map/ppermute | solution.py:156
  147.5 12.6 %collective-permute-start.23 = (bf16[384,768]{1,0:T(8,128)(2,1)}, bf16[384,768]{1,0:T(8,128)(2,1)S(1)}, u32[]{:S(2)}, u32[]{:S(2)}) collective-permute-start(bf16[384,768]{1,0:T(8,128)(2,1)} %join.4.own_ref), channel_id=1, source_target_pairs={{0,8},{1,5},{2,10},{3,7},{4,12},{5,1},{6,14},{7,3},{8,0},{9,13},{1... | collective-permute-start | bytes 1769480 | tf_op jit(solution)/shard_map/ppermute | solution.py:156
  147.5 18.1 %collective-permute-start.26 = (bf16[256,768]{1,0:T(8,128)(2,1)S(1)}, bf16[256,768]{1,0:T(8,128)(2,1)S(1)}, u32[]{:S(2)}, u32[]{:S(2)}) collective-permute-start(bf16[256,768]{1,0:T(8,128)(2,1)S(1)} %copy-done.10), channel_id=1, source_target_pairs={{0,2},{1,3},{2,0},{3,1},{4,6},{5,7},{6,4},{7,5},{8,10},{9,11},{10,... | collective-permute-start | bytes 1179656 | tf_op jit(solution)/shard_map/ppermute | solution.py:120
  149.1 1.8 copy-start.9
  150.9 13.0 %collective-permute-start.22 = (bf16[128,768]{1,0:T(8,128)(2,1)S(1)}, bf16[128,768]{1,0:T(8,128)(2,1)S(1)}, u32[]{:S(2)}, u32[]{:S(2)}) collective-permute-start(bf16[128,768]{1,0:T(8,128)(2,1)S(1)} %get-tuple-element.168), channel_id=1, source_target_pairs={{0,16},{1,17},{2,18},{3,19},{4,20},{5,21},{6,22},{7,23},{8,24},{9,... | collective-permute-start | bytes 589832 | tf_op jit(solution)/shard_map/ppermute | solution.py:156
  150.9 24.5 %collective-permute-start.21 = (bf16[256,768]{1,0:T(8,128)(2,1)S(1)}, bf16[256,768]{1,0:T(8,128)(2,1)S(1)}, u32[]{:S(2)}, u32[]{:S(2)}) collective-permute-start(bf16[256,768]{1,0:T(8,128)(2,1)S(1)} %copy-done.9), channel_id=1, source_target_pairs={{0,2},{1,3},{2,0},{3,1},{4,6},{5,7},{6,4},{7,5},{8,10},{9,11},{10,... | collective-permute-start | bytes 1179656 | tf_op jit(solution)/shard_map/ppermute | solution.py:120
  162.3 24.2 %collective-permute-start.30 = (bf16[768,768]{1,0:T(8,128)(2,1)}, bf16[768,768]{1,0:T(8,128)(2,1)S(1)}, u32[]{:S(2)}, u32[]{:S(2)}) collective-permute-start(bf16[768,768]{1,0:T(8,128)(2,1)} %join.5.own_ref), channel_id=1, source_target_pairs={{0,4},{1,9},{2,6},{3,11},{4,0},{5,13},{6,2},{7,15},{8,12},{9,1},{1... | collective-permute-start | bytes 3538952 | tf_op jit(solution)/shard_map/ppermute | solution.py:156
  165.6 7.5 %collective-permute-start.24 = (bf16[96,768]{1,0:T(8,128)(2,1)}, bf16[96,768]{1,0:T(8,128)(2,1)S(1)}, u32[]{:S(2)}, u32[]{:S(2)}) collective-permute-start(bf16[96,768]{1,0:T(8,128)(2,1)} %get-tuple-element.174.own_ref), channel_id=1, source_target_pairs={{0,16},{1,17},{2,18},{3,19},{4,20},{5,21},{6,22},{7,23},{8,24},{9,... | collective-permute-start | bytes 442376 | tf_op jit(solution)/shard_map/ppermute | solution.py:156
  166.3 2.4 %copy-start.7 = (f32[8,768]{1,0:T(8,128)}, f32[8,768]{1,0:T(8,128)S(1)}, u32[]{:S(2)}) copy-start(f32[8,768]{1,0:T(8,128)S(1)} %slice.12.left_ref) | copy-start | bytes 73732
  166.3 2.4 %collective-permute-start.25 = (f32[8,768]{1,0:T(8,128)S(1)}, f32[8,768]{1,0:T(8,128)S(1)}, u32[]{:S(2)}, u32[]{:S(2)}) collective-permute-start(f32[8,768]{1,0:T(8,128)S(1)} %slice.12.left_ref), channel_id=1, source_target_pairs={{0,1},{1,0},{2,3},{3,2},{4,5},{5,4},{6,7},{7,6},{8,9},{9,8},{10,11... | collective-permute-start | bytes 73736 | tf_op jit(solution)/shard_map/ppermute | solution.py:120
  174.7 6.9 %collective-permute-start.28 = (bf16[192,768]{1,0:T(8,128)(2,1)}, bf16[192,768]{1,0:T(8,128)(2,1)S(1)}, u32[]{:S(2)}, u32[]{:S(2)}) collective-permute-start(bf16[192,768]{1,0:T(8,128)(2,1)} %join.6.own_ref), channel_id=1, source_target_pairs={{0,8},{1,5},{2,10},{3,7},{4,12},{5,1},{6,14},{7,3},{8,0},{9,13},{1... | collective-permute-start | bytes 884744 | tf_op jit(solution)/shard_map/ppermute | solution.py:156
  174.8 4.0 %collective-permute-start.27 = (f32[8,768]{1,0:T(8,128)}, f32[8,768]{1,0:T(8,128)S(1)}, u32[]{:S(2)}, u32[]{:S(2)}) collective-permute-start(f32[8,768]{1,0:T(8,128)} %add.38.left_ref), channel_id=1, source_target_pairs={{0,2},{1,3},{2,0},{3,1},{4,6},{5,7},{6,4},{7,5},{8,10},{9,11},{10,... | collective-permute-start | bytes 73736 | tf_op jit(solution)/shard_map/ppermute | solution.py:120
  183.5 10.1 %collective-permute-start.29 = (bf16[384,768]{1,0:T(8,128)(2,1)}, bf16[384,768]{1,0:T(8,128)(2,1)S(1)}, u32[]{:S(2)}, u32[]{:S(2)}) collective-permute-start(bf16[384,768]{1,0:T(8,128)(2,1)} %join.7.own_ref), channel_id=1, source_target_pairs={{0,4},{1,9},{2,6},{3,11},{4,0},{5,13},{6,2},{7,15},{8,12},{9,1},{1... | collective-permute-start | bytes 1769480 | tf_op jit(solution)/shard_map/ppermute | solution.py:156

commit v2 on v1

--- a/solution.py
+++ b/solution.py
@@ -17,13 +17,13 @@
 HEAVY = pl.CostEstimate(flops=10**11, bytes_accessed=1024, transcendentals=0)
 LIGHT = pl.CostEstimate(flops=1024, bytes_accessed=1024, transcendentals=0)
 ORDER = (
-    "swap_dn", "feed1", "sum_dn", "feed2", "back", "feed3",
-    "swap_out", "swap_in", "two1", "feed4", "two2", "go_mixed",
+    "swap_dn", "out_part", "feed1", "swap_out", "sum_dn", "feed2", "back",
+    "feed3", "swap_in", "two1", "feed4", "two2", "go_mixed",
     "feed5", "two3", "end_tokens", "gains_a", "two4", "end_mixed",
     "gains_b", "two5", "end_feed", "end_heads",
 )
 LONG = (
-    "feed", "end_heads", "end_tokens", "feed4", "swap_out", "two2",
+    "feed", "end_tokens", "feed3", "feed4", "two2",
 )
 
 
@@ -479,6 +479,10 @@
     return lax.rsqrt(jnp.full((1, LANES), alike.astype(F32)))[:, 0:1]
 
 
+def row_of(ref):
+    return ref[...].reshape(1, ref.shape[0])
+
+
 def norm_rows(values):
     return lax.rsqrt(jnp.mean(values * values, axis=-1, keepdims=True) + NORM_EPS)
 
@@ -494,52 +498,73 @@
     return pl.multiple_of(start, LANES)
 
 
-def attend_kernel(
-    heads, count, length_ref, starts_ref, table_ref, buckets_ref, gain_ref, wq_ref, wk_ref, wv_ref, *refs
-):
-    tok_refs = refs[:count]
-    (ctx_ref, packed_ref, exps_ref, linv_ref, normed_ref, tok_all_ref) = refs[count : count + 6]
-    (q_ref, v_ref, k_turned_ref, k_ref, v_turned_ref, bias_ref, all_normed, scores_ref) = refs[count + 6 :]
+def bias_kernel(table_ref, buckets_ref, bias_ref):
+    which = buckets_ref[...]
+    heads, _, wide = bias_ref.shape
+    for h in range(heads):
+        rel = jnp.zeros((8, wide), F32)
+        for b in range(table_ref.shape[0]):
+            rel = jnp.where(which == b, table_ref[b, h], rel)
+        full = jnp.broadcast_to(rel[0:1], (LANES, wide))
+        bias_ref[h] = pltpu.roll(full, wide - (LANES - 1), 1, stride=1, stride_axis=0)
+
+
+def bias_tiles(table, buckets):
+    shape = (table.shape[1], LANES, buckets.shape[1])
+    return local_call(
+        bias_kernel,
+        grid=(1,),
+        in_specs=[pl.BlockSpec(memory_space=pltpu.SMEM), vmem_whole(buckets.shape)],
+        out_specs=vmem_whole(shape),
+        out_shape=FAR(shape, F32),
+        mib=16,
+        name="bias_tiles",
+        cost=HEAVY,
+    )(table, buckets)
+
+
+def attend_kernel(heads, count, length_ref, starts_ref, gain_ref, wq_ref, wk_ref, wv_ref, *refs):
+    tok_refs, bias_far, refs = refs[:count], refs[count], refs[count + 1 :]
+    (ctx_ref, packed_ref, exps_ref, linv_ref, normed_ref, tok_all_ref) = refs[:6]
+    (q_ref, v_ref, k_turned_ref, k_ref, v_turned_ref, bias_ref, all_normed, scores_ref, sem) = refs[6:]
     step = pl.program_id(0)
     blk = ctx_ref.shape[0]
     seq = blk * count
     head_cols = wq_ref.shape[0]
     width = head_cols // heads
-    wide = 2 * seq
 
     @pl.when(step == 0)
     def _():
-        which = buckets_ref[...]
-        for h in range(heads):
-            rel = jnp.zeros((8, wide), F32)
-            for b in range(table_ref.shape[0]):
-                rel = jnp.where(which == b, table_ref[b, h], rel)
-            full = jnp.broadcast_to(rel[0:1], (LANES, wide))
-            bias_ref[h] = pltpu.roll(full, wide - (LANES - 1), 1, stride=1, stride_axis=0)
+        bias_copy = pltpu.make_async_copy(bias_far, bias_ref, sem)
+        bias_copy.start()
         lane = lax.broadcasted_iota(jnp.int32, (blk, LANES - width), 1)
         row = lax.broadcasted_iota(jnp.int32, (blk, LANES - width), 0)
-        first = lane == 0
-        ones_q = jnp.where(first, 1.0, 0.0)
+        line = lax.broadcasted_iota(jnp.int32, (LANES - width, blk), 0)
+        place = lax.broadcasted_iota(jnp.int32, (LANES - width, blk), 1)
+        ones_q = jnp.where(lane == 0, 1.0, 0.0)
         ones_v = jnp.where(lane < 2, 1.0, 0.0)
+        ones_turned = jnp.where(line < 2, 1.0, 0.0)
         for b in range(count):
             values = tok_refs[b][...].astype(F32)
-            normed = (values * norm_rows(values) * gain_ref[0:1]).astype(BF16)
+            normed = (values * norm_rows(values) * row_of(gain_ref)).astype(BF16)
             rows = slice(b * blk, (b + 1) * blk)
             all_normed[rows] = normed
-            masked = first & (row + starts_ref[b] >= length_ref[0])
-            fill = jnp.where(masked, MASK_FILL, 0.0)
+            used = length_ref[0] - starts_ref[b]
+            fill = jnp.where((lane == 0) & (row >= used), MASK_FILL, 0.0)
+            fill_turned = jnp.where((line == 0) & (place >= used), MASK_FILL, 0.0)
             query = dot_nt(normed, wq_ref[...])
             keys = dot_nt(normed, wk_ref[...])
             values = dot_nt(normed, wv_ref[...])
+            keys_turned = dot_nt(wk_ref[...], normed)
+            values_turned = dot_nt(wv_ref[...], normed)
             for h in range(heads):
                 cols = slice(h * width, (h + 1) * width)
                 q_ref[h, rows] = jnp.concatenate((query[:, cols], ones_q), axis=1).astype(BF16)
-                own_k = jnp.concatenate((keys[:, cols], fill), axis=1)
-                own_v = jnp.concatenate((values[:, cols], ones_v), axis=1)
-                k_ref[h, rows] = own_k.astype(BF16)
-                v_ref[h, rows] = own_v.astype(BF16)
-                k_turned_ref[h, :, rows] = own_k.T.astype(BF16)
-                v_turned_ref[h, :, rows] = own_v.T.astype(BF16)
+                k_ref[h, rows] = jnp.concatenate((keys[:, cols], fill), axis=1).astype(BF16)
+                v_ref[h, rows] = jnp.concatenate((values[:, cols], ones_v), axis=1).astype(BF16)
+                k_turned_ref[h, :, rows] = jnp.concatenate((keys_turned[cols], fill_turned), axis=0).astype(BF16)
+                v_turned_ref[h, :, rows] = jnp.concatenate((values_turned[cols], ones_turned), axis=0).astype(BF16)
+        bias_copy.wait()
 
     row0 = pl.multiple_of(step * blk, blk)
     first_query = starts_ref[step]
@@ -585,20 +610,21 @@
             packed_ref[place : place + blk, lanes : lanes + rest] = ctx[:, LANES:]
 
 
-def attend(length, starts, table, buckets, gain, w_query, w_key, w_value, tok):
+def attend(length, starts, bias, gain, w_query, w_key, w_value, tok):
     count = len(tok)
     blk, model = tok[0].shape
     seq = blk * count
-    heads = table.shape[1]
+    heads = bias.shape[0]
     head_cols = w_query.shape[0]
     smem = pl.BlockSpec(memory_space=pltpu.SMEM)
     assert 2 * (head_cols - LANES) == LANES
     return local_call(
         functools.partial(attend_kernel, heads, count),
         grid=(count,),
-        in_specs=[smem, smem, smem, vmem_whole((8, 2 * seq)), vmem_whole((2, model))]
+        in_specs=[smem, smem, vmem_whole((model,))]
         + [vmem_whole((head_cols, model))] * 3
-        + [vmem_whole((blk, model))] * count,
+        + [vmem_whole((blk, model))] * count
+        + [pl.BlockSpec(memory_space=pl.ANY)],
         out_specs=[
             pl.BlockSpec((blk, head_cols), lambda i: (i, 0)),
             vmem_whole((seq * 3 // 2, LANES)),
@@ -627,19 +653,20 @@
             pltpu.VMEM((heads, LANES, 2 * seq), F32),
             pltpu.VMEM((seq, model), BF16),
             pltpu.VMEM((seq, blk), F32),
+            pltpu.SemaphoreType.DMA,
         ],
         mib=28,
         name="attend",
         cost=HEAVY,
-    )(length, starts, table, buckets, gain, w_query, w_key, w_value, tok[0], *tok[1:])
+    )(length, starts, gain, w_query, w_key, w_value, *[Came(piece) for piece in tok], bias)
 
 
 def feed_kernel(count, side_ref, groups_ref, own_ref, gain_ref, *refs):
     tok_far, ctx_far, refs = refs[0], refs[1 : 1 + count], refs[1 + count :]
     w_in_far, w_back_far, joined_far, refs = refs[0], refs[1], refs[2 : 2 + count], refs[2 + count :]
-    hidden_ref, unit_ref, spread_ref, dn_low_ref, dn_high_ref, out_low_ref, out_high_ref, send_far, keep_far = refs[:9]
-    tok_all, ctx_all, w_in_ref, w_back_ref, w_out_ref, grad_all, active_now, dup_all, active_turned = refs[9:18]
-    normed_turned, hidden_now, halves, sems, out_sems = refs[18:]
+    hidden_ref, unit_ref, spread_ref, active_ref, dn_low_ref, dn_high_ref, send_far, keep_far = refs[:8]
+    tok_all, ctx_all, w_in_ref, w_back_ref, w_out_ref, grad_all, normed_now, dup_all, active_turned = refs[8:17]
+    normed_turned, hidden_now, halves, sems, out_sems = refs[17:]
     step = pl.program_id(0)
     blk = hidden_ref.shape[0]
     half = count // 2
@@ -660,16 +687,17 @@
         found = [copy(tok_far.at[rows], tok_all.at[rows])]
         for k in range(count):
             c = b ^ k
-            found.append(copy(ctx_far[k].at[pl.ds(c * blk, blk)], ctx_all.at[k, rows, pl.ds(0, LANES)]))
+            lanes = 2 * k * LANES
+            found.append(copy(ctx_far[k].at[pl.ds(c * blk, blk)], ctx_all.at[rows, pl.ds(lanes, LANES)]))
             place = pl.ds(count * blk + (c % half) * blk, blk)
-            found.append(copy(ctx_far[k].at[place], ctx_all.at[k, rows, pl.ds(LANES, LANES)]))
+            found.append(copy(ctx_far[k].at[place], ctx_all.at[rows, pl.ds(lanes + LANES, LANES)]))
         row_copies.append(found)
         grad_copies.append(copy(joined_far[b].at[pl.ds(0, blk)], grad_all.at[rows]))
     for k in range(count):
-        for side in range(2):
-            place = w_out_ref.at[side, k, pl.ds(0, LANES)]
-            out_copies.append(copy(joined_far[k].at[pl.ds(blk, LANES)], place))
-            place = w_out_ref.at[side, k, pl.ds(LANES + side * rest, rest)]
+        for part in range(2):
+            top = 2 * k * LANES
+            out_copies.append(copy(joined_far[k].at[pl.ds(blk, LANES)], w_out_ref.at[part, pl.ds(top, LANES)]))
+            place = w_out_ref.at[part, pl.ds(top + LANES + (part ^ (k // half)) * rest, rest)]
             out_copies.append(copy(joined_far[k].at[pl.ds(blk + LANES, rest)], place))
     in_copy = copy(w_in_far, w_in_ref)
     back_copy = copy(w_back_far, w_back_ref)
@@ -680,10 +708,10 @@
         late = [one for b in range(half, count) for one in row_copies[b]]
         for one in [*out_copies, *early, in_copy, *grad_copies[:half], back_copy, *late, *grad_copies[half:]]:
             one.start()
-        for side in range(2):
+        for part in range(2):
             for k in range(count):
-                other = LANES + (1 - side) * rest
-                w_out_ref[side, k, other : other + rest] = jnp.zeros((rest, model), BF16)
+                other = 2 * k * LANES + LANES + (1 - (part ^ (k // half))) * rest
+                w_out_ref[part, other : other + rest] = jnp.zeros((rest, model), BF16)
         for one in out_copies:
             one.wait()
 
@@ -697,14 +725,8 @@
 
     rows = pl.ds(pl.multiple_of(step * span, span), span)
     for b in range(half):
-        now = slice(b * blk, (b + 1) * blk)
-        block = step * half + b
-        there = pl.ds(pl.multiple_of(block * blk, blk), blk)
-        hidden = tok_all[there].astype(F32)
-        for k in range(count):
-            side = (block ^ k) // half
-            hidden = hidden + dot_nn(ctx_all[k, there], w_out_ref[side, k])
-        hidden_now[now] = hidden
+        there = pl.ds(pl.multiple_of(step * span + b * blk, blk), blk)
+        hidden_now[b * blk : (b + 1) * blk] = tok_all[there].astype(F32) + dot_nn(ctx_all[there], w_out_ref[step])
     strip = 32 if blk % 32 == 0 else blk
     for r in range(0, span, strip):
         some = slice(r, r + strip)
@@ -713,8 +735,8 @@
         unit = hidden * spread
         unit_ref[some] = unit.astype(BF16)
         spread_ref[some] = jnp.broadcast_to(spread, (strip, LANES))
-        active_now[some, :model] = (unit * gain_ref[1:2]).astype(BF16)
-    normed = active_now[:, :model]
+        normed_now[some] = (unit * row_of(gain_ref)).astype(BF16)
+    normed = normed_now[...]
     normed_turned[:, rows] = normed.T
 
     @pl.when(step == 0)
@@ -733,31 +755,36 @@
     grad = grad_all[rows]
     scale = group_scale(groups_ref, own_ref)
     part = 256 if units % 256 == 0 else units
-    ups = [dot_nn(normed, w_in_ref[:, c : c + part]) for c in range(0, units, part)]
-    for c, up in zip(range(0, units, part), ups, strict=True):
-        cols = slice(c, c + part)
-        dactive = dot_nt(grad, w_back_ref[cols])
-        square = up * up
-        bend = jnp.tanh(up * (GELU_SCALE + GELU_SCALE * GELU_CUBE * square))
-        bell = 0.5 + 0.5 * bend
-        active = (up * bell).astype(BF16)
-        steep = GELU_SCALE + 3.0 * GELU_SCALE * GELU_CUBE * square
-        slope = (bell + (0.5 * up) * (1.0 - bend * bend) * steep) * scale
-        active_now[:, cols] = active
-        active_turned[cols, rows] = active.T
-        dup_all[rows, cols] = (dactive * slope).astype(BF16)
-    dnormed = dot_nt(dup_all[rows], w_in_ref[...]).astype(BF16)
-    out = dot_nn(active_now[:, :units], w_back_ref[...]).astype(BF16)
+    for b in range(0, span, 256):
+        near = slice(b, b + 256)
+        there = pl.ds(pl.multiple_of(step * span + b, 256), 256)
+        for c in range(0, units, part):
+            cols = slice(c, c + part)
+            up = dot_nn(normed[near], w_in_ref[:, cols])
+            dactive = dot_nt(grad[near], w_back_ref[cols])
+            square = up * up
+            bend = jnp.tanh(up * (GELU_SCALE + GELU_SCALE * GELU_CUBE * square))
+            bell = 0.5 + 0.5 * bend
+            active = (up * bell).astype(BF16)
+            steep = GELU_SCALE + 3.0 * GELU_SCALE * GELU_CUBE * square
+            slope = (bell + (0.5 * up) * (1.0 - bend * bend) * steep) * scale
+            active_ref[near, cols] = active
+            active_turned[cols, there] = active.T
+            dup_all[there, cols] = (dactive * slope).astype(BF16)
+
+    def put(dn_ref):
+        for b in range(0, span, 256):
+            near = slice(b, b + 256)
+            there = pl.ds(pl.multiple_of(step * span + b, 256), 256)
+            dn_ref[near] = dot_nt(dup_all[there], w_in_ref[...]).astype(BF16)
 
     @pl.when(step == 0)
     def _():
-        dn_low_ref[...] = dnormed
-        out_low_ref[...] = out
+        put(dn_low_ref)
 
     @pl.when(step == 1)
     def _():
-        dn_high_ref[...] = dnormed
-        out_high_ref[...] = out
+        put(dn_high_ref)
         going = []
         for k, (far, side) in enumerate(((send_far, 1 - side_ref[0]), (keep_far, side_ref[0]))):
             back = dot_nn(active_turned[pl.ds(side * many, many)], grad_all[...]) * scale
@@ -787,26 +814,27 @@
     return local_call(
         functools.partial(feed_kernel, count),
         grid=(2,),
-        in_specs=[smem, smem, whole((2, model))] + [anywhere] * (3 + 2 * count),
+        in_specs=[smem, smem, pl.BlockSpec((model,), lambda i, side: (0,))] + [anywhere] * (3 + 2 * count),
         out_specs=[
             whole((blk, model)),
             by_row,
             pl.BlockSpec((span, LANES), lambda i, side: (i, 0)),
-            *[whole((span, model))] * 4,
+            pl.BlockSpec((span, units), lambda i, side: (i, 0)),
+            *[whole((span, model))] * 2,
             anywhere,
             anywhere,
         ],
-        out_shape=[FAR((blk, model), F32), FAR((rows, model), BF16), FAR((rows, LANES), F32)]
-        + [FAR((span, model), BF16)] * 4
+        out_shape=[FAR((blk, model), F32), FAR((rows, model), BF16), FAR((rows, LANES), F32), FAR((rows, units), BF16)]
+        + [FAR((span, model), BF16)] * 2
         + [FAR(grads, BF16)] * 2,
         scratch_shapes=[
             pltpu.VMEM((rows, model), BF16),
-            pltpu.VMEM((count, rows, 2 * LANES), BF16),
+            pltpu.VMEM((rows, 2 * count * LANES), BF16),
             pltpu.VMEM((model, units), BF16),
             pltpu.VMEM((units, model), BF16),
-            pltpu.VMEM((2, count, 2 * LANES, model), BF16),
+            pltpu.VMEM((2, 2 * count * LANES, model), BF16),
             pltpu.VMEM((rows, model), BF16),
-            pltpu.VMEM((span, max(units, model)), BF16),
+            pltpu.VMEM((span, model), BF16),
             pltpu.VMEM((rows, units), BF16),
             pltpu.VMEM((units, rows), BF16),
             pltpu.VMEM((model, rows), BF16),
@@ -819,7 +847,31 @@
         mib=52,
         name="feed",
         cost=cost_of("feed"),
-    )(side, groups, own, gain, tok, *ctx, w_in, w_back, *joined)
+    )(side, groups, own, gain, tok, ctx[0], *[Came(a) for a in ctx[1:]], w_in, w_back, *joined)
+
+
+def feed_out_kernel(active_ref, w_back_ref, *out_refs):
+    for k, ref in enumerate(out_refs):
+
+        @pl.when(pl.program_id(0) == k)
+        def _():
+            ref[...] = dot_nn(active_ref[...], w_back_ref[...]).astype(BF16)
+
+
+def feed_out(active, w_back, count, cost):
+    rows, units = active.shape
+    model = w_back.shape[1]
+    blk = rows // count
+    return local_call(
+        feed_out_kernel,
+        grid=(count,),
+        in_specs=[pl.BlockSpec((blk, units), lambda i: (i, 0)), vmem_whole(w_back.shape)],
+        out_specs=[vmem_whole((blk, model))] * count,
+        out_shape=[FAR((blk, model), BF16)] * count,
+        mib=16,
+        name="feed_out",
+        cost=cost,
+    )(active, w_back)
 
 
 def finish_mixed_kernel(hidden_ref, own_ref, came_ref, out_ref):
@@ -846,7 +898,7 @@
     dnormed = own_ref[...].astype(F32) + came_ref[...].astype(F32)
     values = tok_ref[...].astype(F32)
     spread = norm_rows(values)
-    out_ref[...] = dh_ref[...].astype(F32) + norm_back(dnormed, values * spread, spread, gain_ref[0:1])[0]
+    out_ref[...] = dh_ref[...].astype(F32) + norm_back(dnormed, values * spread, spread, row_of(gain_ref))[0]
 
 
 def finish_tokens(gain, tok, own, came, dh_own, cost=LIGHT):
@@ -856,7 +908,7 @@
     return local_call(
         finish_tokens_kernel,
         grid=(steps,),
-        in_specs=[vmem_whole((2, model))] + [place] * 4,
+        in_specs=[vmem_whole((model,))] + [place] * 4,
         out_specs=place,
         out_shape=jax.ShapeDtypeStruct((blk, model), F32),
         mib=10,
@@ -933,7 +985,7 @@
     for r in range(0, blk, strip):
         there = pl.ds(pl.multiple_of(row0 + r, strip), strip)
         unit = unit_all[there].astype(F32)
-        scaled = gain_ref[1:2] * dn_all[there].astype(F32)
+        scaled = row_of(gain_ref) * dn_all[there].astype(F32)
         inner = jnp.mean(scaled * unit, axis=-1, keepdims=True)
         dhidden = spread_all[there, 0:1] * (scaled - unit * inner)
         dh_all[there] = (dhidden + grad_all[there].astype(F32) * scale).astype(BF16)
@@ -1073,7 +1125,7 @@
     return local_call(
         functools.partial(attend_back_kernel, heads, count),
         grid=(count,),
-        in_specs=[smem, smem, smem, whole((2, model)), whole((8, 2 * seq))] + [anywhere] * (2 * count + 6 + len(late)),
+        in_specs=[smem, smem, smem, whole((model,)), whole((8, 2 * seq))] + [anywhere] * (2 * count + 6 + len(late)),
         out_specs=[anywhere] * len(outs),
         out_shape=[FAR(shape, BF16) for shape in outs],
         scratch_shapes=[pltpu.VMEM((seq, model), BF16), pltpu.VMEM((seq, model), BF16)]
@@ -1098,7 +1150,7 @@
         mib=52,
         name="attend_back",
         cost=cost,
-    )(side, starts, groups, own, gain, buckets, *dn, *joined, *first, exps, w_out, *late)
+    )(side, starts, groups, own, gain, buckets, *[Came(a) for a in dn], *joined, *first, exps, w_out, *late)
 
 
 def shards(
@@ -1129,7 +1181,6 @@
     here = lax.axis_index("tensor")
     starts = (here ^ jnp.array(block_order(count), jnp.int32)) * blk
     weights = (w_query.T, w_key.T, w_value.T)
-    gains = jnp.stack((gain_attn, gain_ffn))
     own_row = lax.axis_index("dp")[None]
     turned = jnp.pad(rel_buckets[::-1], (0, 1), constant_values=-1)
     buckets = jnp.broadcast_to(turned[None], (8, 2 * seq))
@@ -1154,23 +1205,25 @@
 
     own_tok = tokens[0]
     joined = jnp.concatenate((masked_grad, w_out))
-    ready = (joined, starts, buckets, gains, own_row, rel_table)
-    tok, ready = gather_tensor(own_tok, count, ready)
-    joined, starts, buckets, both_gains, own_row, rel_table = ready
-    joined = [joined]
-    for bit in low_bits:
-        joined = joined + [swap_tensor(piece, bit) for piece in joined]
+    bias = bias_tiles(rel_table, buckets)
+    ready = (joined, starts, own_row, bias)
+    assert count == 4
+    far_tok = swap_tensor(own_tok, 2)
+    near_tok = swap_tensor(own_tok, 1)
+    far_tok, ready = lax.optimization_barrier((far_tok, ready))
+    joined, starts, own_row, bias = ready
+    tok = [own_tok, far_tok, near_tok, swap_tensor(far_tok, 1)]
+    joined = [joined, swap_tensor(joined, 2)]
     ctx, packed, exps, linv, normed, tok_all, q, v, k_turned = turn.done(
-        attend(row_lengths, starts, rel_table, buckets, both_gains, *weights, tok)
+        attend(row_lengths, starts, bias, gain_attn, *weights, tok)
     )
     contexts, _ = gather_tensor(packed, count)
     joined = [turn(piece) for piece in joined]
     joined = joined + [swap_tensor(piece, bits[-1]) for piece in joined]
-    hidden, unit, spread, dn_low, dn_high, out_low, out_high, feed_send, feed_keep = turn.done(
-        feed(first_side, task_groups, own_row, both_gains, w_in, w_back, tok_all, contexts, joined)
+    hidden, unit, spread, active, dn_low, dn_high, feed_send, feed_keep = turn.done(
+        feed(first_side, task_groups, own_row, gain_ffn, w_in, w_back, tok_all, contexts, joined)
     )
     dn_came = swap_tensor(dn_high, bits[-1])
-    out_came = swap_tensor(out_high, bits[-1])
     sum_feed = DpSum(turn, feed_send, feed_keep, finish_feed)
     assert half == 2 and len(low_bits) == 1
     flip = block_order(count).index(low_bits[0])
@@ -1193,7 +1246,7 @@
             starts,
             task_groups,
             own_row,
-            both_gains,
+            gain_ffn,
             w_out,
             buckets,
             dn,
@@ -1219,11 +1272,17 @@
         got["in_own"], got["in_came"] = own, swap_tensor(other, low_bits[0])
 
     def end_tokens(cost):
-        args = (both_gains, own_tok, got["in_own"], turn(got["in_came"]), got["dh"], cost)
+        args = (gain_attn, own_tok, got["in_own"], turn(got["in_came"]), got["dh"], cost)
         got["tokens"] = turn.done(finish_tokens(*args))[None]
 
+    def out_part(cost):
+        parts = turn.done(feed_out(turn(active), w_back, count, cost))
+        got["out_low"] = parts[:half]
+        got["out_came"] = [swap_tensor(part, bits[-1]) for part in parts[half:]]
+
     def swap_out(cost):
-        got["out_own"], got["out_other"] = turn.done(add_pieces(out_low, turn(out_came), half, cost))
+        pairs = zip(got["out_low"], got["out_came"], strict=True)
+        got["out_own"], got["out_other"] = [turn.done(add(own, turn(came), cost)) for own, came in pairs]
 
     def go_mixed(cost):
         got["out_came"] = swap_tensor(turn(got["out_other"]), low_bits[0])
@@ -1250,6 +1309,7 @@
         back=back,
         swap_in=swap_in,
         end_tokens=end_tokens,
+        out_part=out_part,
         swap_out=swap_out,
         go_mixed=go_mixed,
         end_mixed=end_mixed,

time: 197 us -> 190 us (0.964)
  waiting for transfers between devices: 61.1 us -> 46.2 us
  Pallas kernels: 101 us -> 108 us
  starting transfers between devices: 21.5 us -> 26.7 us
  other arithmetic: 3.42 us -> 0.86 us
    ppermute x19 -> x20, waiting for transfers between devices: 25.1 us -> 15.9 us  [swap_tensor(): return lax.ppermute(value, 'tensor', [(i, i ^ bit) for i in range(size)])]
    pallas_call x23 -> x26, Pallas kernels: 101 us -> 108 us  [run(): return call(*args[:prefetch], *given)]
    ppermute x12, waiting for transfers between devices: 36 us -> 30.2 us  [swap_dp(): return lax.ppermute(value, ('dp', 'tensor'), route)]
    ppermute x19 -> x20, starting transfers between devices: 10.2 us -> 14.5 us  [swap_tensor(): return lax.ppermute(value, 'tensor', [(i, i ^ bit) for i in range(size)])]
  transfers between devices with their start and end apart: 31 -> 32, of which waited for: 16 -> 14; matrix products, arithmetic and copies ran while one was open for 5% -> 3% of each run, Pallas kernels for 40% -> 47%
where the time goes in v2:
time: 190 us; the launch traced here: 189 us
  Pallas kernels  108 us (57%)
  waiting for transfers between devices  46.2 us (24%)
  starting transfers between devices  26.7 us (14%)
  local copies, waits for them, and re-layouts  6.2 us (3%)
    pallas_call x26, Pallas kernels, run(): return call(*args[:prefetch], *given)  108 us
    ppermute x12, waiting for transfers between devices, swap_dp(): return lax.ppermute(value, ('dp', 'tensor'), route)  30.2 us
    ppermute x20, waiting for transfers between devices, swap_tensor(): return lax.ppermute(value, 'tensor', [(i, i ^ bit) for i in range(size)])  15.9 us
    ppermute x20, starting transfers between devices, swap_tensor(): return lax.ppermute(value, 'tensor', [(i, i ^ bit) for i in range(size)])  14.5 us
    ppermute x12, starting transfers between devices, swap_dp(): return lax.ppermute(value, ('dp', 'tensor'), route)  12.2 us
  transfers between devices with their start and end apart: 32, of which 14 were waited for; matrix products, arithmetic and copies ran while one was open for 3% of the time, Pallas kernels for 47%

profile of v2, /device:TPU:0, one launch (start us, length us, event | category | flops | bytes accessed | tf_op | source)
XLA Modules:
  0.0 189.1 jit_solution(975978520107894838)
XLA Ops:
  0.6 3.0 %collective-permute-start = (bf16[256,768]{1,0:T(8,128)(2,1)}, bf16[256,768]{1,0:T(8,128)(2,1)S(1)}, u32[]{:S(2)}, u32[]{:S(2)}) collective-permute-start(bf16[256,768]{1,0:T(8,128)(2,1)} %bitcast.20), channel_id=1, source_target_pairs={{0,2},{1,3},{2,0},{3,1},{4,6},{5,7},{6,4},{7,5},{8,10},{9,11},{10,... | collective-permute-start | bytes 1179656 | tf_op jit(solution)/shard_map/ppermute | solution.py:120
  4.3 0.7 compare_reduce_fusion
  5.0 0.8 reverse
  5.9 0.8 copy.27.table_ref
  6.6 0.6 broadcast_in_dim.56.buckets_ref
  7.3 3.7 %bias_tiles.1.refs_4_ = f32[3,128,2048]{2,1,0:T(8,128)} custom-call(f32[32,3]{1,0:T(8,128)S(1)} %copy.27.table_ref, s32[8,2048]{1,0:T(8,128)} %broadcast_in_dim.56.buckets_ref), custom_call_target="tpu_custom_call" | custom-call | flops 99999997952 | bytes 1024 | tf_op jit(solution)/shard_map/bias_tiles/pallas_call | solution.py:67
  11.2 0.5 copy-done.17
  11.7 1.3 collective-permute-done.refs_1_
  13.0 1.7 collective-permute-start.6
  14.8 16.7 %attend.1 = (bf16[1024,192]{1,0:T(8,128)(2,1)}, bf16[1536,128]{1,0:T(8,128)(2,1)}, bf16[3,1024,1024]{2,1,0:T(8,128)(2,1)}, f32[1024,128]{1,0:T(8,128)}, bf16[102...) custom-call(s32[1]{0:T(128)} %copy.28.length_ref, ...), custom_call_target="tpu_custom_call" | custom-call | flops 99999997952 | bytes 1024 | tf_op jit(solution)/shard_map/attend/pallas_call | solution.py:67
  31.5 1.8 collective-permute-start.3
  33.3 0.5 collective-permute-start.8
  33.9 9.2 %collective-permute-done.3.refs_2_ = bf16[1536,128]{1,0:T(8,128)(2,1)S(1)} collective-permute-done((bf16[1536,128]{1,0:T(8,128)(2,1)}, bf16[1536,128]{1,0:T(8,128)(2,1)S(1)}, u32[]{:S(2)}, u32[]{:S(2)}) %collective-permute-start.3) | collective-permute-done | bytes 393248 | tf_op jit(solution)/shard_map/ppermute | solution.py:120
  43.0 1.7 collective-permute-done.5.refs_4_
  44.8 16.4 %feed.1 = (f32[256,768]{1,0:T(8,128)}, bf16[1024,768]{1,0:T(8,128)(2,1)}, f32[1024,128]{1,0:T(8,128)}, bf16[1024,768]{1,0:T(8,128)(2,1)}, bf16[512,768]{1,0:T(8,...) custom-call(s32[1]{0:T(128)} %bitcast.side_ref, s32[8]{0:T(128)S(1)} %copy-done.3, ...), custom_call_target="tpu_custom_call" | custom-call | flops 99999997952 | bytes 1024 | tf_op jit(solution)/shard_map/feed/pallas_call | solution.py:67
  61.2 1.6 collective-permute-start.11
  62.8 2.5 %collective-permute-done.9.right_ref = bf16[512,768]{1,0:T(8,128)(2,1)S(1)} collective-permute-done((bf16[512,768]{1,0:T(8,128)(2,1)}, bf16[512,768]{1,0:T(8,128)(2,1)S(1)}, u32[]{:S(2)}, u32[]{:S(2)}) %collective-permute-start.9) | collective-permute-done | bytes 786464 | tf_op jit(solution)/shard_map/ppermute | solution.py:120
  65.3 2.0 %add_swap.1 = (bf16[512,768]{1,0:T(8,128)(2,1)}, bf16[512,768]{1,0:T(8,128)(2,1)S(1)}) custom-call(bf16[512,768]{1,0:T(8,128)(2,1)} %get-tuple-element.106.left_ref, bf16[512,768]{1,0:T(8,128)(2,1)S(1)} %collective-permute-done.9.right_ref), custom_call_target="tpu_custom_call" | custom-call | flops 1024 | bytes 1024 | tf_op jit(solution)/shard_map/add_swap/pallas_call | solution.py:67
  67.3 1.5 collective-permute-start.13
  68.8 5.1 %feed_out.1 = (bf16[256,768]{1,0:T(8,128)(2,1)}, bf16[256,768]{1,0:T(8,128)(2,1)}, bf16[256,768]{1,0:T(8,128)(2,1)}, bf16[256,768]{1,0:T(8,128)(2,1)}) custom-call(bf16[1024,768]{1,0:T(8,128)(2,1)} %get-tuple-element.110.active_ref, bf16[768,768]{1,0:T(8,128)(2,1)} %w_back_ref.1), custom_call_target="tpu_custom_call" | custom-call | flops 1024 | bytes 1024 | tf_op jit(solution)/shard_map/feed_out/pallas_call | solution.py:67
  73.9 3.8 %collective-permute-done.11.came_ref = bf16[768,768]{1,0:T(8,128)(2,1)S(1)} collective-permute-done((bf16[768,768]{1,0:T(8,128)(2,1)}, bf16[768,768]{1,0:T(8,128)(2,1)S(1)}, u32[]{:S(2)}, u32[]{:S(2)}) %collective-permute-start.11) | collective-permute-done | bytes 1179680 | tf_op jit(solution)/shard_map/ppermute | solution.py:156
  77.7 2.5 %fold.2 = (bf16[384,768]{1,0:T(8,128)(2,1)S(1)}, bf16[384,768]{1,0:T(8,128)(2,1)}) custom-call(s32[1]{0:T(128)} %bitcast.8.side_ref, bf16[768,768]{1,0:T(8,128)(2,1)} %get-tuple-element.113.kept_ref, bf16[768,768]{1,0:T(8,128)(2,1)S(1)} %collective-permute-done.11.came_ref), custom_call_target="tpu_custom_call" | custom-call | flops 1024 | bytes 1024 | tf_op jit(solution)/shard_map/fold/pallas_call | solution.py:67
  80.2 1.7 collective-permute-start.15
  81.8 0.5 collective-permute-start.12
  82.3 1.2 collective-permute-done.10.right_ref
  83.5 1.8 add.39.own_ref
  85.4 1.8 add.40
  87.2 2.2 %add_pieces.2 = (bf16[256,768]{1,0:T(8,128)(2,1)}, bf16[256,768]{1,0:T(8,128)(2,1)}) custom-call(bf16[512,768]{1,0:T(8,128)(2,1)} %get-tuple-element.109.refs_0_, bf16[512,768]{1,0:T(8,128)(2,1)S(1)} %collective-permute-done.13.refs_1_), custom_call_target="tpu_custom_call" | custom-call | flops 1024 | bytes 1024 | tf_op jit(solution)/shard_map/add_pieces/pallas_call | solution.py:67
  89.5 0.4 collective-permute-start.14
  90.0 2.0 %fold.3 = (bf16[192,768]{1,0:T(8,128)(2,1)S(1)}, bf16[192,768]{1,0:T(8,128)(2,1)}) custom-call(s32[1]{0:T(128)} %bitcast.9.side_ref, bf16[384,768]{1,0:T(8,128)(2,1)} %get-tuple-element.125.kept_ref, bf16[384,768]{1,0:T(8,128)(2,1)S(1)} %collective-permute-done.15.came_ref), custom_call_target="tpu_custom_call" | custom-call | flops 1024 | bytes 1024 | tf_op jit(solution)/shard_map/fold/pallas_call | solution.py:67
  92.0 2.7 %collective-permute-start.19 = (bf16[192,768]{1,0:T(8,128)(2,1)S(1)}, bf16[192,768]{1,0:T(8,128)(2,1)S(1)}, u32[]{:S(2)}, u32[]{:S(2)}) collective-permute-start(bf16[192,768]{1,0:T(8,128)(2,1)S(1)} %get-tuple-element.127), channel_id=1, source_target_pairs={{0,16},{1,17},{2,18},{3,19},{4,20},{5,21},{6,22},{7,23},{8,24},{9,... | collective-permute-start | bytes 884744 | tf_op jit(solution)/shard_map/ppermute | solution.py:156
  94.7 23.3 %attend_back.1 = (bf16[256,768]{1,0:T(8,128)(2,1)}, bf16[32,768]{1,0:T(8,128)(2,1)}, bf16[416,768]{1,0:T(8,128)(2,1)}, bf16[384,768]{1,0:T(8,128)(2,1)}, bf16[51...) custom-call(s32[1]{0:T(128)} %bitcast.side_ref, s32[4]{0:T(128)S(1)} %xor_multiply_fusion.starts_ref, s32[8]{0:T(128)S(1)} %copy-done.3, ...), custom_call_target="tpu_custom_call" | custom-call | flops 1024 | bytes 1024 | tf_op jit(solution)/shard_map/attend_back/pallas_call | solution.py:67
  118.1 1.5 collective-permute-start.17
  119.6 1.7 add.41.own_ref
  121.7 2.1 %add_pieces.3 = (bf16[256,768]{1,0:T(8,128)(2,1)}, bf16[256,768]{1,0:T(8,128)(2,1)}) custom-call(bf16[512,768]{1,0:T(8,128)(2,1)} %get-tuple-element.140.refs_0_, bf16[512,768]{1,0:T(8,128)(2,1)S(1)} %collective-permute-done.18.refs_1_), custom_call_target="tpu_custom_call" | custom-call | flops 1024 | bytes 1024 | tf_op jit(solution)/shard_map/add_pieces/pallas_call | solution.py:67
  123.8 4.9 %collective-permute-done.17.came_ref.small_came_ref = bf16[416,768]{1,0:T(8,128)(2,1)S(1)} collective-permute-done((bf16[416,768]{1,0:T(8,128)(2,1)}, bf16[416,768]{1,0:T(8,128)(2,1)S(1)}, u32[]{:S(2)}, u32[]{:S(2)}) %collective-permute-start.17) | collective-permute-done | bytes 639008 | tf_op jit(solution)/shard_map/ppermute | solution.py:156
  128.8 2.0 %fold_small.2 = (bf16[224,768]{1,0:T(8,128)(2,1)S(1)}, bf16[192,768]{1,0:T(8,128)(2,1)}, bf16[32,768]{1,0:T(8,128)(2,1)}) custom-call(s32[1]{0:T(128)} %bitcast.8.side_ref, bf16[384,768]{1,0:T(8,128)(2,1)} %get-tuple-element.138.kept_ref, bf16[416,768]{1,0:T(8,128)(2,1)S(1)} %collective-permute-done.17.came_ref.small_came_ref, ...), custom_call_target="tpu_custom_call" | custom-call | flops 1024 | bytes 1024 | tf_op jit(solution)/shard_map/fold_small/pallas_call | solution.py:67
  130.8 1.5 collective-permute-start.20
  132.3 5.8 %collective-permute-done.21.came_ref = bf16[192,768]{1,0:T(8,128)(2,1)S(1)} collective-permute-done((bf16[192,768]{1,0:T(8,128)(2,1)}, bf16[192,768]{1,0:T(8,128)(2,1)S(1)}, u32[]{:S(2)}, u32[]{:S(2)}) %collective-permute-start.21) | collective-permute-done | bytes 294944 | tf_op jit(solution)/shard_map/ppermute | solution.py:156
  138.1 1.8 join.4.own_ref
  139.9 1.6 collective-permute-start.27
  141.6 1.8 fold_small.3
  143.4 0.6 collective-permute-start.23
  144.0 1.0 collective-permute-start.22
  145.0 7.0 %collective-permute-done.24.came_ref = bf16[384,768]{1,0:T(8,128)(2,1)S(1)} collective-permute-done((bf16[384,768]{1,0:T(8,128)(2,1)}, bf16[384,768]{1,0:T(8,128)(2,1)S(1)}, u32[]{:S(2)}, u32[]{:S(2)}) %collective-permute-start.24) | collective-permute-done | bytes 589856 | tf_op jit(solution)/shard_map/ppermute | solution.py:156
  152.0 2.2 %join.5.own_ref = bf16[768,768]{1,0:T(8,128)(2,1)} custom-call(s32[1]{0:T(128)} %bitcast.8.side_ref, bf16[384,768]{1,0:T(8,128)(2,1)} %join.4.own_ref, bf16[384,768]{1,0:T(8,128)(2,1)S(1)} %collective-permute-done.24.came_ref), custom_call_target="tpu_custom_call" | custom-call | flops 1024 | bytes 1024 | tf_op jit(solution)/shard_map/join/pallas_call | solution.py:67
  154.2 1.7 collective-permute-start.31
  155.9 1.6 add_small.1
  157.5 0.7 slice.12.left_ref
  158.2 2.4 %finish_tokens.1 = f32[256,768]{1,0:T(8,128)} custom-call(f32[768]{0:T(1024)S(1)} %copy-done.6, bf16[256,768]{1,0:T(8,128)(2,1)} %bitcast.22, bf16[256,768]{1,0:T(8,128)(2,1)} %get-tuple-element.146.own_ref, bf16[256,768]{1,0:T(8,128)(2,1)S(1)} %collective-permute-done.27.came_ref, bf16[256,768]{1,0:T(8,128)(2,1)} %get-tuple-element.143.dh_ref), custom_call_target="tpu_custom_call" | custom-call | flops 99999997952 | bytes 1024 | tf_op jit(solution)/shard_map/finish_tokens/pallas_call | solution.py:67
  160.7 1.4 add.42.left_ref
  162.0 3.5 %collective-permute-done.25.came_ref = bf16[96,768]{1,0:T(8,128)(2,1)S(1)} collective-permute-done((bf16[96,768]{1,0:T(8,128)(2,1)}, bf16[96,768]{1,0:T(8,128)(2,1)S(1)}, u32[]{:S(2)}, u32[]{:S(2)}) %collective-permute-start.25) | collective-permute-done | bytes 147488 | tf_op jit(solution)/shard_map/ppermute | solution.py:156
  165.5 1.6 join.6.own_ref
  167.1 2.3 %collective-permute-start.28 = (f32[8,768]{1,0:T(8,128)}, f32[8,768]{1,0:T(8,128)S(1)}, u32[]{:S(2)}, u32[]{:S(2)}) collective-permute-start(f32[8,768]{1,0:T(8,128)} %add.42.left_ref), channel_id=1, source_target_pairs={{0,2},{1,3},{2,0},{3,1},{4,6},{5,7},{6,4},{7,5},{8,10},{9,11},{10,... | collective-permute-start | bytes 73736 | tf_op jit(solution)/shard_map/ppermute | solution.py:120
  169.4 2.1 %finish_mixed.1 = bf16[256,768]{1,0:T(8,128)(2,1)} custom-call(f32[256,768]{1,0:T(8,128)} %get-tuple-element.104.hidden_ref, bf16[256,768]{1,0:T(8,128)(2,1)} %add.39.own_ref, bf16[256,768]{1,0:T(8,128)(2,1)S(1)} %collective-permute-done.22.came_ref), custom_call_target="tpu_custom_call" | custom-call | flops 1024 | bytes 1024 | tf_op jit(solution)/shard_map/finish_mixed/pallas_call | solution.py:67
  171.5 1.3 add.43
  172.9 1.6 collective-permute-done.29.came_ref
  174.5 1.8 join.7.own_ref
  176.3 0.5 collective-permute-start.30
  176.8 1.3 slice_bitcast_fusion
  178.0 1.4 slice_reduce_fusion
  179.5 3.6 %finish_feed.1 = (f32[768,768]{1,0:T(8,128)}, f32[768,768]{1,0:T(8,128)}) custom-call(s32[1]{0:T(128)} %bitcast.side_ref, bf16[768,768]{1,0:T(8,128)(2,1)} %join.5.own_ref, bf16[768,768]{1,0:T(8,128)(2,1)S(1)} %collective-permute-done.31.came_ref), custom_call_target="tpu_custom_call" | custom-call | flops 1024 | bytes 1024 | tf_op jit(solution)/shard_map/finish_feed/pallas_call | solution.py:67
  183.1 3.3 %collective-permute-done.30.came_ref = bf16[384,768]{1,0:T(8,128)(2,1)S(1)} collective-permute-done((bf16[384,768]{1,0:T(8,128)(2,1)}, bf16[384,768]{1,0:T(8,128)(2,1)S(1)}, u32[]{:S(2)}, u32[]{:S(2)}) %collective-permute-start.30) | collective-permute-done | bytes 589856 | tf_op jit(solution)/shard_map/ppermute | solution.py:156
  186.4 2.7 %finish_heads.1 = (f32[192,768]{1,0:T(8,128)}, f32[192,768]{1,0:T(8,128)}, f32[192,768]{1,0:T(8,128)}, f32[192,768]{1,0:T(8,128)}) custom-call(s32[1]{0:T(128)} %bitcast.side_ref, bf16[384,768]{1,0:T(8,128)(2,1)} %join.7.own_ref, bf16[384,768]{1,0:T(8,128)(2,1)S(1)} %collective-permute-done.30.came_ref), custom_call_target="tpu_custom_call" | custom-call | flops 1024 | bytes 1024 | tf_op jit(solution)/shard_map/finish_heads/pallas_call | solution.py:67
  (75 shorter events, 1.3 us)
Async XLA Ops:
  0.6 12.4 %collective-permute-start = (bf16[256,768]{1,0:T(8,128)(2,1)}, bf16[256,768]{1,0:T(8,128)(2,1)S(1)}, u32[]{:S(2)}, u32[]{:S(2)}) collective-permute-start(bf16[256,768]{1,0:T(8,128)(2,1)} %bitcast.20), channel_id=1, source_target_pairs={{0,2},{1,3},{2,0},{3,1},{4,6},{5,7},{6,4},{7,5},{8,10},{9,11},{10,... | collective-permute-start | bytes 1179656 | tf_op jit(solution)/shard_map/ppermute | solution.py:120
  3.7 11.1 %collective-permute-start.1 = (bf16[256,768]{1,0:T(8,128)(2,1)}, bf16[256,768]{1,0:T(8,128)(2,1)S(1)}, u32[]{:S(2)}, u32[]{:S(2)}) collective-permute-start(bf16[256,768]{1,0:T(8,128)(2,1)} %bitcast.21), channel_id=1, source_target_pairs={{0,1},{1,0},{2,3},{3,2},{4,5},{5,4},{6,7},{7,6},{8,9},{9,8},{10,11... | collective-permute-start | bytes 1179656 | tf_op jit(solution)/shard_map/ppermute | solution.py:120
  7.3 3.8 %copy-start.11 = (bf16[1,256,768]{2,1,0:T(8,128)(2,1)S(1)}, bf16[1,256,768]{2,1,0:T(8,128)(2,1)}, u32[]{:S(2)}) copy-start(bf16[1,256,768]{2,1,0:T(8,128)(2,1)} %param.30) | copy-start | bytes 1179652
  7.3 3.9 %copy-start.8 = (bf16[192,768]{1,0:T(8,128)(2,1)S(1)}, bf16[192,768]{1,0:T(8,128)(2,1)}, u32[]{:S(2)}) copy-start(bf16[192,768]{1,0:T(8,128)(2,1)} %refs_13_.1) | copy-start | bytes 884740
  11.0 0.7 copy-start.17
  11.0 3.7 %copy-start.4 = (bf16[1,256,768]{2,1,0:T(8,128)(2,1)S(1)}, bf16[1,256,768]{2,1,0:T(8,128)(2,1)}, u32[]{:S(2)}) copy-start(bf16[1,256,768]{2,1,0:T(8,128)(2,1)} %param.16) | copy-start | bytes 1179652
  11.0 3.7 %copy-start.5 = (f32[768]{0:T(1024)S(1)}, f32[768]{0:T(1024)}, u32[]{:S(2)}) copy-start(f32[768]{0:T(1024)} %gain_ref.7) | copy-start | bytes 9220
  11.7 21.6 %copy-start.7 = (bf16[448,768]{1,0:T(8,128)(2,1)}, bf16[448,768]{1,0:T(8,128)(2,1)S(1)}, u32[]{:S(2)}) copy-start(bf16[448,768]{1,0:T(8,128)(2,1)S(1)} %pad_maximum_fusion.refs_7_.refs_4_) | copy-start | bytes 2064388
  13.0 1.7 collective-permute-start.2
  13.0 20.3 %collective-permute-start.6 = (bf16[448,768]{1,0:T(8,128)(2,1)S(1)}, bf16[448,768]{1,0:T(8,128)(2,1)S(1)}, u32[]{:S(2)}, u32[]{:S(2)}) collective-permute-start(bf16[448,768]{1,0:T(8,128)(2,1)S(1)} %pad_maximum_fusion.refs_7_.refs_4_), channel_id=1, source_target_pairs={{0,2},{1,3},{2,0},{3,1},{4,6},{5,7},{6,4},{7,5},{8,10},{9,11},{10,... | collective-permute-start | bytes 2064392 | tf_op jit(solution)/shard_map/ppermute | solution.py:120
  14.8 30.0 %copy-start.2 = (f32[768]{0:T(1024)S(1)}, f32[768]{0:T(1024)}, u32[]{:S(2)}) copy-start(f32[768]{0:T(1024)} %gain_ref.6) | copy-start | bytes 9220
  14.8 30.0 %copy-start.3 = (s32[8]{0:T(128)S(1)}, s32[8]{0:T(128)}, u32[]{:S(2)}) copy-start(s32[8]{0:T(128)} %groups_ref.3) | copy-start | bytes 100
  31.5 11.5 %collective-permute-start.3 = (bf16[1536,128]{1,0:T(8,128)(2,1)}, bf16[1536,128]{1,0:T(8,128)(2,1)S(1)}, u32[]{:S(2)}, u32[]{:S(2)}) collective-permute-start(bf16[1536,128]{1,0:T(8,128)(2,1)} %get-tuple-element.99.refs_1_), channel_id=1, source_target_pairs={{0,2},{1,3},{2,0},{3,1},{4,6},{5,7},{6,4},{7,5},{8,10},{9,11},{10,... | collective-permute-start | bytes 1179656 | tf_op jit(solution)/shard_map/ppermute | solution.py:120
  33.3 9.8 %collective-permute-start.7 = (bf16[448,768]{1,0:T(8,128)(2,1)S(1)}, bf16[448,768]{1,0:T(8,128)(2,1)S(1)}, u32[]{:S(2)}, u32[]{:S(2)}) collective-permute-start(bf16[448,768]{1,0:T(8,128)(2,1)S(1)} %pad_maximum_fusion.refs_7_.refs_4_), channel_id=1, source_target_pairs={{0,1},{1,0},{2,3},{3,2},{4,5},{5,4},{6,7},{7,6},{8,9},{9,8},{10,11... | collective-permute-start | bytes 2064392 | tf_op jit(solution)/shard_map/ppermute | solution.py:120
  33.3 11.5 %copy-start.9 = (bf16[448,768]{1,0:T(8,128)(2,1)}, bf16[448,768]{1,0:T(8,128)(2,1)S(1)}, u32[]{:S(2)}) copy-start(bf16[448,768]{1,0:T(8,128)(2,1)S(1)} %collective-permute-done.6.refs_8_.refs_5_) | copy-start | bytes 2064388
  33.3 11.5 %collective-permute-start.8 = (bf16[448,768]{1,0:T(8,128)(2,1)S(1)}, bf16[448,768]{1,0:T(8,128)(2,1)}, u32[]{:S(2)}, u32[]{:S(2)}) collective-permute-start(bf16[448,768]{1,0:T(8,128)(2,1)S(1)} %collective-permute-done.6.refs_8_.refs_5_), channel_id=1, source_target_pairs={{0,1},{1,0},{2,3},{3,2},{4,5},{5,4},{6,7},{7,6},{8,9},{9,8},{10,11... | collective-permute-start | bytes 2064392 | tf_op jit(solution)/shard_map/ppermute | solution.py:120
  33.8 9.3 %collective-permute-start.4 = (bf16[1536,128]{1,0:T(8,128)(2,1)}, bf16[1536,128]{1,0:T(8,128)(2,1)S(1)}, u32[]{:S(2)}, u32[]{:S(2)}) collective-permute-start(bf16[1536,128]{1,0:T(8,128)(2,1)} %get-tuple-element.99.refs_1_), channel_id=1, source_target_pairs={{0,1},{1,0},{2,3},{3,2},{4,5},{5,4},{6,7},{7,6},{8,9},{9,8},{10,11... | collective-permute-start | bytes 1179656 | tf_op jit(solution)/shard_map/ppermute | solution.py:120
  43.0 1.7 collective-permute-start.5
  43.0 1.7 copy-start.10
  61.2 16.5 %collective-permute-start.11 = (bf16[768,768]{1,0:T(8,128)(2,1)}, bf16[768,768]{1,0:T(8,128)(2,1)S(1)}, u32[]{:S(2)}, u32[]{:S(2)}) collective-permute-start(bf16[768,768]{1,0:T(8,128)(2,1)} %get-tuple-element.114), channel_id=1, source_target_pairs={{0,4},{1,9},{2,6},{3,11},{4,0},{5,13},{6,2},{7,15},{8,12},{9,1},{1... | collective-permute-start | bytes 3538952 | tf_op jit(solution)/shard_map/ppermute | solution.py:156
  62.8 2.5 %collective-permute-start.9 = (bf16[512,768]{1,0:T(8,128)(2,1)}, bf16[512,768]{1,0:T(8,128)(2,1)S(1)}, u32[]{:S(2)}, u32[]{:S(2)}) collective-permute-start(bf16[512,768]{1,0:T(8,128)(2,1)} %get-tuple-element.107), channel_id=1, source_target_pairs={{0,1},{1,0},{2,3},{3,2},{4,5},{5,4},{6,7},{7,6},{8,9},{9,8},{10,11... | collective-permute-start | bytes 2359304 | tf_op jit(solution)/shard_map/ppermute | solution.py:120
  67.3 19.9 %collective-permute-start.13 = (bf16[512,768]{1,0:T(8,128)(2,1)S(1)}, bf16[512,768]{1,0:T(8,128)(2,1)S(1)}, u32[]{:S(2)}, u32[]{:S(2)}) collective-permute-start(bf16[512,768]{1,0:T(8,128)(2,1)S(1)} %get-tuple-element.121), channel_id=1, source_target_pairs={{0,2},{1,3},{2,0},{3,1},{4,6},{5,7},{6,4},{7,5},{8,10},{9,11},{10,... | collective-permute-start | bytes 2359304 | tf_op jit(solution)/shard_map/ppermute | solution.py:120
  73.9 7.9 %copy-start.16 = (bf16[256,768]{1,0:T(8,128)(2,1)S(1)}, bf16[256,768]{1,0:T(8,128)(2,1)}, u32[]{:S(2)}) copy-start(bf16[256,768]{1,0:T(8,128)(2,1)} %get-tuple-element.112) | copy-start | bytes 1179652
  73.9 7.9 %copy-start.15 = (bf16[256,768]{1,0:T(8,128)(2,1)S(1)}, bf16[256,768]{1,0:T(8,128)(2,1)}, u32[]{:S(2)}) copy-start(bf16[256,768]{1,0:T(8,128)(2,1)} %get-tuple-element.119) | copy-start | bytes 1179652
  80.2 9.9 %collective-permute-start.15 = (bf16[384,768]{1,0:T(8,128)(2,1)S(1)}, bf16[384,768]{1,0:T(8,128)(2,1)S(1)}, u32[]{:S(2)}, u32[]{:S(2)}) collective-permute-start(bf16[384,768]{1,0:T(8,128)(2,1)S(1)} %get-tuple-element.116), channel_id=1, source_target_pairs={{0,8},{1,5},{2,10},{3,7},{4,12},{5,1},{6,14},{7,3},{8,0},{9,13},{1... | collective-permute-start | bytes 1769480 | tf_op jit(solution)/shard_map/ppermute | solution.py:156
  81.8 1.7 collective-permute-start.10
  81.8 3.6 %collective-permute-start.12 = (bf16[256,768]{1,0:T(8,128)(2,1)S(1)}, bf16[256,768]{1,0:T(8,128)(2,1)S(1)}, u32[]{:S(2)}, u32[]{:S(2)}) collective-permute-start(bf16[256,768]{1,0:T(8,128)(2,1)S(1)} %copy-done.15), channel_id=1, source_target_pairs={{0,1},{1,0},{2,3},{3,2},{4,5},{5,4},{6,7},{7,6},{8,9},{9,8},{10,11... | collective-permute-start | bytes 1179656 | tf_op jit(solution)/shard_map/ppermute | solution.py:120
  89.4 5.3 %copy-start = (bf16[256,768]{1,0:T(8,128)(2,1)S(1)}, bf16[256,768]{1,0:T(8,128)(2,1)}, u32[]{:S(2)}) copy-start(bf16[256,768]{1,0:T(8,128)(2,1)} %get-tuple-element.123.refs_0_) | copy-start | bytes 1179652
  89.4 5.4 %copy-start.1 = (bf16[256,768]{1,0:T(8,128)(2,1)S(1)}, bf16[256,768]{1,0:T(8,128)(2,1)}, u32[]{:S(2)}) copy-start(bf16[256,768]{1,0:T(8,128)(2,1)} %get-tuple-element.124.refs_1_) | copy-start | bytes 1179652
  89.4 5.3 %collective-permute-start.16 = (bf16[256,768]{1,0:T(8,128)(2,1)}, bf16[256,768]{1,0:T(8,128)(2,1)S(1)}, u32[]{:S(2)}, u32[]{:S(2)}) collective-permute-start(bf16[256,768]{1,0:T(8,128)(2,1)} %get-tuple-element.124.refs_1_), channel_id=1, source_target_pairs={{0,1},{1,0},{2,3},{3,2},{4,5},{5,4},{6,7},{7,6},{8,9},{9,8},{10,11... | collective-permute-start | bytes 1179656 | tf_op jit(solution)/shard_map/ppermute | solution.py:120
  89.5 5.2 %collective-permute-start.14 = (bf16[256,768]{1,0:T(8,128)(2,1)}, bf16[256,768]{1,0:T(8,128)(2,1)S(1)}, u32[]{:S(2)}, u32[]{:S(2)}) collective-permute-start(bf16[256,768]{1,0:T(8,128)(2,1)} %get-tuple-element.123.refs_0_), channel_id=1, source_target_pairs={{0,1},{1,0},{2,3},{3,2},{4,5},{5,4},{6,7},{7,6},{8,9},{9,8},{10,11... | collective-permute-start | bytes 1179656 | tf_op jit(solution)/shard_map/ppermute | solution.py:120
  92.0 27.6 %collective-permute-start.19 = (bf16[192,768]{1,0:T(8,128)(2,1)S(1)}, bf16[192,768]{1,0:T(8,128)(2,1)S(1)}, u32[]{:S(2)}, u32[]{:S(2)}) collective-permute-start(bf16[192,768]{1,0:T(8,128)(2,1)S(1)} %get-tuple-element.127), channel_id=1, source_target_pairs={{0,16},{1,17},{2,18},{3,19},{4,20},{5,21},{6,22},{7,23},{8,24},{9,... | collective-permute-start | bytes 884744 | tf_op jit(solution)/shard_map/ppermute | solution.py:156
  118.0 3.7 %collective-permute-start.18 = (bf16[512,768]{1,0:T(8,128)(2,1)}, bf16[512,768]{1,0:T(8,128)(2,1)S(1)}, u32[]{:S(2)}, u32[]{:S(2)}) collective-permute-start(bf16[512,768]{1,0:T(8,128)(2,1)} %get-tuple-element.141), channel_id=1, source_target_pairs={{0,1},{1,0},{2,3},{3,2},{4,5},{5,4},{6,7},{7,6},{8,9},{9,8},{10,11... | collective-permute-start | bytes 2359304 | tf_op jit(solution)/shard_map/ppermute | solution.py:120
  118.1 10.7 %collective-permute-start.17 = (bf16[416,768]{1,0:T(8,128)(2,1)}, bf16[416,768]{1,0:T(8,128)(2,1)S(1)}, u32[]{:S(2)}, u32[]{:S(2)}) collective-permute-start(bf16[416,768]{1,0:T(8,128)(2,1)} %get-tuple-element.139), channel_id=1, source_target_pairs={{0,4},{1,9},{2,6},{3,11},{4,0},{5,13},{6,2},{7,15},{8,12},{9,1},{1... | collective-permute-start | bytes 1916936 | tf_op jit(solution)/shard_map/ppermute | solution.py:156
  121.4 16.7 %collective-permute-start.21 = (bf16[192,768]{1,0:T(8,128)(2,1)}, bf16[192,768]{1,0:T(8,128)(2,1)S(1)}, u32[]{:S(2)}, u32[]{:S(2)}) collective-permute-start(bf16[192,768]{1,0:T(8,128)(2,1)} %add.41.own_ref), channel_id=1, source_target_pairs={{0,16},{1,17},{2,18},{3,19},{4,20},{5,21},{6,22},{7,23},{8,24},{9,... | collective-permute-start | bytes 884744 | tf_op jit(solution)/shard_map/ppermute | solution.py:156
  130.8 9.1 %copy-start.14 = (bf16[256,768]{1,0:T(8,128)(2,1)S(1)}, bf16[256,768]{1,0:T(8,128)(2,1)}, u32[]{:S(2)}) copy-start(bf16[256,768]{1,0:T(8,128)(2,1)} %get-tuple-element.162) | copy-start | bytes 1179652
  130.8 10.8 %collective-permute-start.20 = (bf16[224,768]{1,0:T(8,128)(2,1)S(1)}, bf16[224,768]{1,0:T(8,128)(2,1)S(1)}, u32[]{:S(2)}, u32[]{:S(2)}) collective-permute-start(bf16[224,768]{1,0:T(8,128)(2,1)S(1)} %get-tuple-element.150), channel_id=1, source_target_pairs={{0,8},{1,5},{2,10},{3,7},{4,12},{5,1},{6,14},{7,3},{8,0},{9,13},{1... | collective-permute-start | bytes 1032200 | tf_op jit(solution)/shard_map/ppermute | solution.py:156
  139.9 12.1 %collective-permute-start.24 = (bf16[384,768]{1,0:T(8,128)(2,1)}, bf16[384,768]{1,0:T(8,128)(2,1)S(1)}, u32[]{:S(2)}, u32[]{:S(2)}) collective-permute-start(bf16[384,768]{1,0:T(8,128)(2,1)} %join.4.own_ref), channel_id=1, source_target_pairs={{0,8},{1,5},{2,10},{3,7},{4,12},{5,1},{6,14},{7,3},{8,0},{9,13},{1... | collective-permute-start | bytes 1769480 | tf_op jit(solution)/shard_map/ppermute | solution.py:156
  139.9 17.6 %collective-permute-start.27 = (bf16[256,768]{1,0:T(8,128)(2,1)S(1)}, bf16[256,768]{1,0:T(8,128)(2,1)S(1)}, u32[]{:S(2)}, u32[]{:S(2)}) collective-permute-start(bf16[256,768]{1,0:T(8,128)(2,1)S(1)} %copy-done.14), channel_id=1, source_target_pairs={{0,2},{1,3},{2,0},{3,1},{4,6},{5,7},{6,4},{7,5},{8,10},{9,11},{10,... | collective-permute-start | bytes 1179656 | tf_op jit(solution)/shard_map/ppermute | solution.py:120
  141.6 2.4 %copy-start.12 = (bf16[256,768]{1,0:T(8,128)(2,1)S(1)}, bf16[256,768]{1,0:T(8,128)(2,1)}, u32[]{:S(2)}) copy-start(bf16[256,768]{1,0:T(8,128)(2,1)} %add.40) | copy-start | bytes 1179652
  143.4 14.8 %copy-start.6 = (f32[768]{0:T(1024)S(1)}, f32[768]{0:T(1024)}, u32[]{:S(2)}) copy-start(f32[768]{0:T(1024)} %gain_ref.7) | copy-start | bytes 9220
  143.4 12.5 %collective-permute-start.23 = (bf16[128,768]{1,0:T(8,128)(2,1)S(1)}, bf16[128,768]{1,0:T(8,128)(2,1)S(1)}, u32[]{:S(2)}, u32[]{:S(2)}) collective-permute-start(bf16[128,768]{1,0:T(8,128)(2,1)S(1)} %get-tuple-element.154), channel_id=1, source_target_pairs={{0,16},{1,17},{2,18},{3,19},{4,20},{5,21},{6,22},{7,23},{8,24},{9,... | collective-permute-start | bytes 589832 | tf_op jit(solution)/shard_map/ppermute | solution.py:156
  144.0 25.4 %collective-permute-start.22 = (bf16[256,768]{1,0:T(8,128)(2,1)S(1)}, bf16[256,768]{1,0:T(8,128)(2,1)S(1)}, u32[]{:S(2)}, u32[]{:S(2)}) collective-permute-start(bf16[256,768]{1,0:T(8,128)(2,1)S(1)} %copy-done.12), channel_id=1, source_target_pairs={{0,2},{1,3},{2,0},{3,1},{4,6},{5,7},{6,4},{7,5},{8,10},{9,11},{10,... | collective-permute-start | bytes 1179656 | tf_op jit(solution)/shard_map/ppermute | solution.py:120
  154.2 25.3 %collective-permute-start.31 = (bf16[768,768]{1,0:T(8,128)(2,1)}, bf16[768,768]{1,0:T(8,128)(2,1)S(1)}, u32[]{:S(2)}, u32[]{:S(2)}) collective-permute-start(bf16[768,768]{1,0:T(8,128)(2,1)} %join.5.own_ref), channel_id=1, source_target_pairs={{0,4},{1,9},{2,6},{3,11},{4,0},{5,13},{6,2},{7,15},{8,12},{9,1},{1... | collective-permute-start | bytes 3538952 | tf_op jit(solution)/shard_map/ppermute | solution.py:156
  157.5 8.0 %collective-permute-start.25 = (bf16[96,768]{1,0:T(8,128)(2,1)}, bf16[96,768]{1,0:T(8,128)(2,1)S(1)}, u32[]{:S(2)}, u32[]{:S(2)}) collective-permute-start(bf16[96,768]{1,0:T(8,128)(2,1)} %get-tuple-element.160.own_ref), channel_id=1, source_target_pairs={{0,16},{1,17},{2,18},{3,19},{4,20},{5,21},{6,22},{7,23},{8,24},{9,... | collective-permute-start | bytes 442376 | tf_op jit(solution)/shard_map/ppermute | solution.py:156
  158.2 2.4 %copy-start.13 = (f32[8,768]{1,0:T(8,128)}, f32[8,768]{1,0:T(8,128)S(1)}, u32[]{:S(2)}) copy-start(f32[8,768]{1,0:T(8,128)S(1)} %slice.12.left_ref) | copy-start | bytes 73732
  158.2 2.4 %collective-permute-start.26 = (f32[8,768]{1,0:T(8,128)S(1)}, f32[8,768]{1,0:T(8,128)S(1)}, u32[]{:S(2)}, u32[]{:S(2)}) collective-permute-start(f32[8,768]{1,0:T(8,128)S(1)} %slice.12.left_ref), channel_id=1, source_target_pairs={{0,1},{1,0},{2,3},{3,2},{4,5},{5,4},{6,7},{7,6},{8,9},{9,8},{10,11... | collective-permute-start | bytes 73736 | tf_op jit(solution)/shard_map/ppermute | solution.py:120
  167.1 7.4 %collective-permute-start.29 = (bf16[192,768]{1,0:T(8,128)(2,1)}, bf16[192,768]{1,0:T(8,128)(2,1)S(1)}, u32[]{:S(2)}, u32[]{:S(2)}) collective-permute-start(bf16[192,768]{1,0:T(8,128)(2,1)} %join.6.own_ref), channel_id=1, source_target_pairs={{0,8},{1,5},{2,10},{3,7},{4,12},{5,1},{6,14},{7,3},{8,0},{9,13},{1... | collective-permute-start | bytes 884744 | tf_op jit(solution)/shard_map/ppermute | solution.py:156
  167.1 4.4 %collective-permute-start.28 = (f32[8,768]{1,0:T(8,128)}, f32[8,768]{1,0:T(8,128)S(1)}, u32[]{:S(2)}, u32[]{:S(2)}) collective-permute-start(f32[8,768]{1,0:T(8,128)} %add.42.left_ref), channel_id=1, source_target_pairs={{0,2},{1,3},{2,0},{3,1},{4,6},{5,7},{6,4},{7,5},{8,10},{9,11},{10,... | collective-permute-start | bytes 73736 | tf_op jit(solution)/shard_map/ppermute | solution.py:120
  176.3 10.1 %collective-permute-start.30 = (bf16[384,768]{1,0:T(8,128)(2,1)}, bf16[384,768]{1,0:T(8,128)(2,1)S(1)}, u32[]{:S(2)}, u32[]{:S(2)}) collective-permute-start(bf16[384,768]{1,0:T(8,128)(2,1)} %join.7.own_ref), channel_id=1, source_target_pairs={{0,4},{1,9},{2,6},{3,11},{4,0},{5,13},{6,2},{7,15},{8,12},{9,1},{1... | collective-permute-start | bytes 1769480 | tf_op jit(solution)/shard_map/ppermute | solution.py:156

commit v3 on v2

--- a/solution.py
+++ b/solution.py
@@ -978,6 +978,9 @@
                 copy.wait()
             if b == 0:
                 out_copy.wait()
+                for copy in late[:3]:
+                    copy.wait()
+            exps_copy(b).wait()
 
     row0 = pl.multiple_of(block * blk, blk)
     now = pl.ds(row0, blk)
@@ -1000,24 +1003,6 @@
         coarse = inner.astype(BF16).astype(F32)
         extra = jnp.where(lane == 0, coarse, jnp.where(lane == 1, inner - coarse, 0.0))
         given_ref[h] = jnp.concatenate((dctx[:, cols] * inverse, extra), axis=1).astype(BF16)
-
-    @pl.when(block == 0)
-    def _():
-        total = jnp.zeros((1, model), F32)
-        for r in range(0, blk, strip):
-            product = unit_all[r : r + strip].astype(F32) * dn_all[r : r + strip].astype(F32)
-            total += jnp.sum(product, axis=0, keepdims=True)
-        sums_ref[...] = jnp.zeros_like(sums_ref)
-        sums_ref[12:16] = jnp.broadcast_to(total, (4, model))
-        pltpu.make_async_copy(dh_all.at[pl.ds(0, blk)], dh_own_far, out_sems.at[0]).start()
-        for copy in late[:3]:
-            copy.wait()
-
-    for b in range(count):
-
-        @pl.when(block == b)
-        def _():
-            exps_copy(b).wait()
 
     slot = lax.rem(block, 2)
     first_query = starts_ref[block]
@@ -1035,6 +1020,16 @@
         dv_ref[h] += dot_nn(exps_all[slot, h], given)
         dquery.append(dot_nn(k_turned_ref[h], ds_ref[h]).T[:, :width])
     dj_ref[0, now] = jnp.concatenate(dquery, axis=1).astype(BF16)
+
+    @pl.when(block == 0)
+    def _():
+        total = jnp.zeros((1, model), F32)
+        for r in range(0, blk, strip):
+            product = unit_all[r : r + strip].astype(F32) * dn_all[r : r + strip].astype(F32)
+            total += jnp.sum(product, axis=0, keepdims=True)
+        sums_ref[...] = jnp.zeros_like(sums_ref)
+        sums_ref[12:16] = jnp.broadcast_to(total, (4, model))
+        pltpu.make_async_copy(dh_all.at[pl.ds(0, blk)], dh_own_far, out_sems.at[0]).start()
 
     @pl.when(block == count - 1)
     def _():

time: 190 us -> 188 us (0.989)
  Pallas kernels: 108 us -> 105 us
    pallas_call x26, Pallas kernels: 108 us -> 105 us  [run(): return call(*args[:prefetch], *given)]
  transfers between devices with their start and end apart: 32 -> 32, of which waited for: 14 -> 14; matrix products, arithmetic and copies ran while one was open for 3% -> 4% of each run, Pallas kernels for 47% -> 46%
where the time goes in v3:
time: 188 us; the launch traced here: 186 us
  Pallas kernels  105 us (56%)
  waiting for transfers between devices  46.2 us (25%)
  starting transfers between devices  26.7 us (14%)
  local copies, waits for them, and re-layouts  6.2 us (3%)
    pallas_call x26, Pallas kernels, run(): return call(*args[:prefetch], *given)  105 us
    ppermute x12, waiting for transfers between devices, swap_dp(): return lax.ppermute(value, ('dp', 'tensor'), route)  30.3 us
    ppermute x20, waiting for transfers between devices, swap_tensor(): return lax.ppermute(value, 'tensor', [(i, i ^ bit) for i in range(size)])  15.9 us
    ppermute x20, starting transfers between devices, swap_tensor(): return lax.ppermute(value, 'tensor', [(i, i ^ bit) for i in range(size)])  14.5 us
    ppermute x12, starting transfers between devices, swap_dp(): return lax.ppermute(value, ('dp', 'tensor'), route)  12.2 us
  transfers between devices with their start and end apart: 32, of which 14 were waited for; matrix products, arithmetic and copies ran while one was open for 4% of the time, Pallas kernels for 46%

profile of v3, /device:TPU:0, one launch (start us, length us, event | category | flops | bytes accessed | tf_op | source)
XLA Modules:
  0.0 186.5 jit_solution(2078537382118250441)
XLA Ops:
  0.6 3.0 %collective-permute-start = (bf16[256,768]{1,0:T(8,128)(2,1)}, bf16[256,768]{1,0:T(8,128)(2,1)S(1)}, u32[]{:S(2)}, u32[]{:S(2)}) collective-permute-start(bf16[256,768]{1,0:T(8,128)(2,1)} %bitcast.20), channel_id=1, source_target_pairs={{0,2},{1,3},{2,0},{3,1},{4,6},{5,7},{6,4},{7,5},{8,10},{9,11},{10,... | collective-permute-start | bytes 1179656 | tf_op jit(solution)/shard_map/ppermute | solution.py:120
  4.3 0.7 compare_reduce_fusion
  5.0 0.8 reverse
  5.9 0.8 copy.27.table_ref
  6.6 0.6 broadcast_in_dim.56.buckets_ref
  7.3 3.7 %bias_tiles.1.refs_4_ = f32[3,128,2048]{2,1,0:T(8,128)} custom-call(f32[32,3]{1,0:T(8,128)S(1)} %copy.27.table_ref, s32[8,2048]{1,0:T(8,128)} %broadcast_in_dim.56.buckets_ref), custom_call_target="tpu_custom_call" | custom-call | flops 99999997952 | bytes 1024 | tf_op jit(solution)/shard_map/bias_tiles/pallas_call | solution.py:67
  11.2 0.5 copy-done.17
  11.7 1.3 collective-permute-done.refs_1_
  13.0 1.7 collective-permute-start.6
  14.8 16.7 %attend.1 = (bf16[1024,192]{1,0:T(8,128)(2,1)}, bf16[1536,128]{1,0:T(8,128)(2,1)}, bf16[3,1024,1024]{2,1,0:T(8,128)(2,1)}, f32[1024,128]{1,0:T(8,128)}, bf16[102...) custom-call(s32[1]{0:T(128)} %copy.28.length_ref, ...), custom_call_target="tpu_custom_call" | custom-call | flops 99999997952 | bytes 1024 | tf_op jit(solution)/shard_map/attend/pallas_call | solution.py:67
  31.5 1.8 collective-permute-start.3
  33.3 0.5 collective-permute-start.8
  33.9 9.2 %collective-permute-done.3.refs_2_ = bf16[1536,128]{1,0:T(8,128)(2,1)S(1)} collective-permute-done((bf16[1536,128]{1,0:T(8,128)(2,1)}, bf16[1536,128]{1,0:T(8,128)(2,1)S(1)}, u32[]{:S(2)}, u32[]{:S(2)}) %collective-permute-start.3) | collective-permute-done | bytes 393248 | tf_op jit(solution)/shard_map/ppermute | solution.py:120
  43.0 1.7 collective-permute-done.5.refs_4_
  44.8 16.4 %feed.1 = (f32[256,768]{1,0:T(8,128)}, bf16[1024,768]{1,0:T(8,128)(2,1)}, f32[1024,128]{1,0:T(8,128)}, bf16[1024,768]{1,0:T(8,128)(2,1)}, bf16[512,768]{1,0:T(8,...) custom-call(s32[1]{0:T(128)} %bitcast.side_ref, s32[8]{0:T(128)S(1)} %copy-done.3, ...), custom_call_target="tpu_custom_call" | custom-call | flops 99999997952 | bytes 1024 | tf_op jit(solution)/shard_map/feed/pallas_call | solution.py:67
  61.2 1.6 collective-permute-start.11
  62.8 2.5 %collective-permute-done.9.right_ref = bf16[512,768]{1,0:T(8,128)(2,1)S(1)} collective-permute-done((bf16[512,768]{1,0:T(8,128)(2,1)}, bf16[512,768]{1,0:T(8,128)(2,1)S(1)}, u32[]{:S(2)}, u32[]{:S(2)}) %collective-permute-start.9) | collective-permute-done | bytes 786464 | tf_op jit(solution)/shard_map/ppermute | solution.py:120
  65.3 2.0 %add_swap.1 = (bf16[512,768]{1,0:T(8,128)(2,1)}, bf16[512,768]{1,0:T(8,128)(2,1)S(1)}) custom-call(bf16[512,768]{1,0:T(8,128)(2,1)} %get-tuple-element.106.left_ref, bf16[512,768]{1,0:T(8,128)(2,1)S(1)} %collective-permute-done.9.right_ref), custom_call_target="tpu_custom_call" | custom-call | flops 1024 | bytes 1024 | tf_op jit(solution)/shard_map/add_swap/pallas_call | solution.py:67
  67.3 1.5 collective-permute-start.13
  68.8 5.1 %feed_out.1 = (bf16[256,768]{1,0:T(8,128)(2,1)}, bf16[256,768]{1,0:T(8,128)(2,1)}, bf16[256,768]{1,0:T(8,128)(2,1)}, bf16[256,768]{1,0:T(8,128)(2,1)}) custom-call(bf16[1024,768]{1,0:T(8,128)(2,1)} %get-tuple-element.110.active_ref, bf16[768,768]{1,0:T(8,128)(2,1)} %w_back_ref.1), custom_call_target="tpu_custom_call" | custom-call | flops 1024 | bytes 1024 | tf_op jit(solution)/shard_map/feed_out/pallas_call | solution.py:67
  73.9 3.8 %collective-permute-done.11.came_ref = bf16[768,768]{1,0:T(8,128)(2,1)S(1)} collective-permute-done((bf16[768,768]{1,0:T(8,128)(2,1)}, bf16[768,768]{1,0:T(8,128)(2,1)S(1)}, u32[]{:S(2)}, u32[]{:S(2)}) %collective-permute-start.11) | collective-permute-done | bytes 1179680 | tf_op jit(solution)/shard_map/ppermute | solution.py:156
  77.7 2.5 %fold.2 = (bf16[384,768]{1,0:T(8,128)(2,1)S(1)}, bf16[384,768]{1,0:T(8,128)(2,1)}) custom-call(s32[1]{0:T(128)} %bitcast.8.side_ref, bf16[768,768]{1,0:T(8,128)(2,1)} %get-tuple-element.113.kept_ref, bf16[768,768]{1,0:T(8,128)(2,1)S(1)} %collective-permute-done.11.came_ref), custom_call_target="tpu_custom_call" | custom-call | flops 1024 | bytes 1024 | tf_op jit(solution)/shard_map/fold/pallas_call | solution.py:67
  80.2 1.7 collective-permute-start.15
  81.8 0.5 collective-permute-start.12
  82.3 1.2 collective-permute-done.10.right_ref
  83.5 1.8 add.39.own_ref
  85.4 1.8 add.40
  87.2 2.2 %add_pieces.2 = (bf16[256,768]{1,0:T(8,128)(2,1)}, bf16[256,768]{1,0:T(8,128)(2,1)}) custom-call(bf16[512,768]{1,0:T(8,128)(2,1)} %get-tuple-element.109.refs_0_, bf16[512,768]{1,0:T(8,128)(2,1)S(1)} %collective-permute-done.13.refs_1_), custom_call_target="tpu_custom_call" | custom-call | flops 1024 | bytes 1024 | tf_op jit(solution)/shard_map/add_pieces/pallas_call | solution.py:67
  89.5 0.4 collective-permute-start.14
  90.0 2.0 %fold.3 = (bf16[192,768]{1,0:T(8,128)(2,1)S(1)}, bf16[192,768]{1,0:T(8,128)(2,1)}) custom-call(s32[1]{0:T(128)} %bitcast.9.side_ref, bf16[384,768]{1,0:T(8,128)(2,1)} %get-tuple-element.125.kept_ref, bf16[384,768]{1,0:T(8,128)(2,1)S(1)} %collective-permute-done.15.came_ref), custom_call_target="tpu_custom_call" | custom-call | flops 1024 | bytes 1024 | tf_op jit(solution)/shard_map/fold/pallas_call | solution.py:67
  92.0 2.7 %collective-permute-start.19 = (bf16[192,768]{1,0:T(8,128)(2,1)S(1)}, bf16[192,768]{1,0:T(8,128)(2,1)S(1)}, u32[]{:S(2)}, u32[]{:S(2)}) collective-permute-start(bf16[192,768]{1,0:T(8,128)(2,1)S(1)} %get-tuple-element.127), channel_id=1, source_target_pairs={{0,16},{1,17},{2,18},{3,19},{4,20},{5,21},{6,22},{7,23},{8,24},{9,... | collective-permute-start | bytes 884744 | tf_op jit(solution)/shard_map/ppermute | solution.py:156
  94.7 20.7 %attend_back.1 = (bf16[256,768]{1,0:T(8,128)(2,1)}, bf16[32,768]{1,0:T(8,128)(2,1)}, bf16[416,768]{1,0:T(8,128)(2,1)}, bf16[384,768]{1,0:T(8,128)(2,1)}, bf16[51...) custom-call(s32[1]{0:T(128)} %bitcast.side_ref, s32[4]{0:T(128)S(1)} %xor_multiply_fusion.starts_ref, s32[8]{0:T(128)S(1)} %copy-done.3, ...), custom_call_target="tpu_custom_call" | custom-call | flops 1024 | bytes 1024 | tf_op jit(solution)/shard_map/attend_back/pallas_call | solution.py:67
  115.5 1.6 collective-permute-start.17
  117.1 1.7 add.41.own_ref
  119.1 2.1 %add_pieces.3 = (bf16[256,768]{1,0:T(8,128)(2,1)}, bf16[256,768]{1,0:T(8,128)(2,1)}) custom-call(bf16[512,768]{1,0:T(8,128)(2,1)} %get-tuple-element.140.refs_0_, bf16[512,768]{1,0:T(8,128)(2,1)S(1)} %collective-permute-done.18.refs_1_), custom_call_target="tpu_custom_call" | custom-call | flops 1024 | bytes 1024 | tf_op jit(solution)/shard_map/add_pieces/pallas_call | solution.py:67
  121.2 5.0 %collective-permute-done.17.came_ref.small_came_ref = bf16[416,768]{1,0:T(8,128)(2,1)S(1)} collective-permute-done((bf16[416,768]{1,0:T(8,128)(2,1)}, bf16[416,768]{1,0:T(8,128)(2,1)S(1)}, u32[]{:S(2)}, u32[]{:S(2)}) %collective-permute-start.17) | collective-permute-done | bytes 639008 | tf_op jit(solution)/shard_map/ppermute | solution.py:156
  126.2 2.0 %fold_small.2 = (bf16[224,768]{1,0:T(8,128)(2,1)S(1)}, bf16[192,768]{1,0:T(8,128)(2,1)}, bf16[32,768]{1,0:T(8,128)(2,1)}) custom-call(s32[1]{0:T(128)} %bitcast.8.side_ref, bf16[384,768]{1,0:T(8,128)(2,1)} %get-tuple-element.138.kept_ref, bf16[416,768]{1,0:T(8,128)(2,1)S(1)} %collective-permute-done.17.came_ref.small_came_ref, ...), custom_call_target="tpu_custom_call" | custom-call | flops 1024 | bytes 1024 | tf_op jit(solution)/shard_map/fold_small/pallas_call | solution.py:67
  128.2 1.6 collective-permute-start.20
  129.7 5.8 %collective-permute-done.21.came_ref = bf16[192,768]{1,0:T(8,128)(2,1)S(1)} collective-permute-done((bf16[192,768]{1,0:T(8,128)(2,1)}, bf16[192,768]{1,0:T(8,128)(2,1)S(1)}, u32[]{:S(2)}, u32[]{:S(2)}) %collective-permute-start.21) | collective-permute-done | bytes 294944 | tf_op jit(solution)/shard_map/ppermute | solution.py:156
  135.5 1.8 join.4.own_ref
  137.3 1.6 collective-permute-start.27
  139.0 1.8 fold_small.3
  140.8 0.6 collective-permute-start.23
  141.4 1.0 collective-permute-start.22
  142.4 7.0 %collective-permute-done.24.came_ref = bf16[384,768]{1,0:T(8,128)(2,1)S(1)} collective-permute-done((bf16[384,768]{1,0:T(8,128)(2,1)}, bf16[384,768]{1,0:T(8,128)(2,1)S(1)}, u32[]{:S(2)}, u32[]{:S(2)}) %collective-permute-start.24) | collective-permute-done | bytes 589856 | tf_op jit(solution)/shard_map/ppermute | solution.py:156
  149.4 2.2 %join.5.own_ref = bf16[768,768]{1,0:T(8,128)(2,1)} custom-call(s32[1]{0:T(128)} %bitcast.8.side_ref, bf16[384,768]{1,0:T(8,128)(2,1)} %join.4.own_ref, bf16[384,768]{1,0:T(8,128)(2,1)S(1)} %collective-permute-done.24.came_ref), custom_call_target="tpu_custom_call" | custom-call | flops 1024 | bytes 1024 | tf_op jit(solution)/shard_map/join/pallas_call | solution.py:67
  151.6 1.7 collective-permute-start.31
  153.2 1.6 add_small.1
  154.9 0.7 slice.12.left_ref
  155.6 2.4 %finish_tokens.1 = f32[256,768]{1,0:T(8,128)} custom-call(f32[768]{0:T(1024)S(1)} %copy-done.6, bf16[256,768]{1,0:T(8,128)(2,1)} %bitcast.22, bf16[256,768]{1,0:T(8,128)(2,1)} %get-tuple-element.146.own_ref, bf16[256,768]{1,0:T(8,128)(2,1)S(1)} %collective-permute-done.27.came_ref, bf16[256,768]{1,0:T(8,128)(2,1)} %get-tuple-element.143.dh_ref), custom_call_target="tpu_custom_call" | custom-call | flops 99999997952 | bytes 1024 | tf_op jit(solution)/shard_map/finish_tokens/pallas_call | solution.py:67
  158.0 1.4 add.42.left_ref
  159.4 3.5 %collective-permute-done.25.came_ref = bf16[96,768]{1,0:T(8,128)(2,1)S(1)} collective-permute-done((bf16[96,768]{1,0:T(8,128)(2,1)}, bf16[96,768]{1,0:T(8,128)(2,1)S(1)}, u32[]{:S(2)}, u32[]{:S(2)}) %collective-permute-start.25) | collective-permute-done | bytes 147488 | tf_op jit(solution)/shard_map/ppermute | solution.py:156
  162.9 1.6 join.6.own_ref
  164.6 2.3 %collective-permute-start.28 = (f32[8,768]{1,0:T(8,128)}, f32[8,768]{1,0:T(8,128)S(1)}, u32[]{:S(2)}, u32[]{:S(2)}) collective-permute-start(f32[8,768]{1,0:T(8,128)} %add.42.left_ref), channel_id=1, source_target_pairs={{0,2},{1,3},{2,0},{3,1},{4,6},{5,7},{6,4},{7,5},{8,10},{9,11},{10,... | collective-permute-start | bytes 73736 | tf_op jit(solution)/shard_map/ppermute | solution.py:120
  166.8 2.1 %finish_mixed.1 = bf16[256,768]{1,0:T(8,128)(2,1)} custom-call(f32[256,768]{1,0:T(8,128)} %get-tuple-element.104.hidden_ref, bf16[256,768]{1,0:T(8,128)(2,1)} %add.39.own_ref, bf16[256,768]{1,0:T(8,128)(2,1)S(1)} %collective-permute-done.22.came_ref), custom_call_target="tpu_custom_call" | custom-call | flops 1024 | bytes 1024 | tf_op jit(solution)/shard_map/finish_mixed/pallas_call | solution.py:67
  168.9 1.3 add.43
  170.3 1.6 collective-permute-done.29.came_ref
  171.9 1.8 join.7.own_ref
  173.7 0.5 collective-permute-start.30
  174.2 1.3 slice_bitcast_fusion
  175.5 1.4 slice_reduce_fusion
  176.9 3.6 %finish_feed.1 = (f32[768,768]{1,0:T(8,128)}, f32[768,768]{1,0:T(8,128)}) custom-call(s32[1]{0:T(128)} %bitcast.side_ref, bf16[768,768]{1,0:T(8,128)(2,1)} %join.5.own_ref, bf16[768,768]{1,0:T(8,128)(2,1)S(1)} %collective-permute-done.31.came_ref), custom_call_target="tpu_custom_call" | custom-call | flops 1024 | bytes 1024 | tf_op jit(solution)/shard_map/finish_feed/pallas_call | solution.py:67
  180.5 3.3 %collective-permute-done.30.came_ref = bf16[384,768]{1,0:T(8,128)(2,1)S(1)} collective-permute-done((bf16[384,768]{1,0:T(8,128)(2,1)}, bf16[384,768]{1,0:T(8,128)(2,1)S(1)}, u32[]{:S(2)}, u32[]{:S(2)}) %collective-permute-start.30) | collective-permute-done | bytes 589856 | tf_op jit(solution)/shard_map/ppermute | solution.py:156
  183.8 2.7 %finish_heads.1 = (f32[192,768]{1,0:T(8,128)}, f32[192,768]{1,0:T(8,128)}, f32[192,768]{1,0:T(8,128)}, f32[192,768]{1,0:T(8,128)}) custom-call(s32[1]{0:T(128)} %bitcast.side_ref, bf16[384,768]{1,0:T(8,128)(2,1)} %join.7.own_ref, bf16[384,768]{1,0:T(8,128)(2,1)S(1)} %collective-permute-done.30.came_ref), custom_call_target="tpu_custom_call" | custom-call | flops 1024 | bytes 1024 | tf_op jit(solution)/shard_map/finish_heads/pallas_call | solution.py:67
  (75 shorter events, 1.3 us)
Async XLA Ops:
  0.6 12.4 %collective-permute-start = (bf16[256,768]{1,0:T(8,128)(2,1)}, bf16[256,768]{1,0:T(8,128)(2,1)S(1)}, u32[]{:S(2)}, u32[]{:S(2)}) collective-permute-start(bf16[256,768]{1,0:T(8,128)(2,1)} %bitcast.20), channel_id=1, source_target_pairs={{0,2},{1,3},{2,0},{3,1},{4,6},{5,7},{6,4},{7,5},{8,10},{9,11},{10,... | collective-permute-start | bytes 1179656 | tf_op jit(solution)/shard_map/ppermute | solution.py:120
  3.7 11.1 %collective-permute-start.1 = (bf16[256,768]{1,0:T(8,128)(2,1)}, bf16[256,768]{1,0:T(8,128)(2,1)S(1)}, u32[]{:S(2)}, u32[]{:S(2)}) collective-permute-start(bf16[256,768]{1,0:T(8,128)(2,1)} %bitcast.21), channel_id=1, source_target_pairs={{0,1},{1,0},{2,3},{3,2},{4,5},{5,4},{6,7},{7,6},{8,9},{9,8},{10,11... | collective-permute-start | bytes 1179656 | tf_op jit(solution)/shard_map/ppermute | solution.py:120
  7.3 3.8 %copy-start.11 = (bf16[1,256,768]{2,1,0:T(8,128)(2,1)S(1)}, bf16[1,256,768]{2,1,0:T(8,128)(2,1)}, u32[]{:S(2)}) copy-start(bf16[1,256,768]{2,1,0:T(8,128)(2,1)} %param.30) | copy-start | bytes 1179652
  7.3 3.9 %copy-start.8 = (bf16[192,768]{1,0:T(8,128)(2,1)S(1)}, bf16[192,768]{1,0:T(8,128)(2,1)}, u32[]{:S(2)}) copy-start(bf16[192,768]{1,0:T(8,128)(2,1)} %refs_13_.1) | copy-start | bytes 884740
  11.0 0.7 copy-start.17
  11.0 3.7 %copy-start.4 = (bf16[1,256,768]{2,1,0:T(8,128)(2,1)S(1)}, bf16[1,256,768]{2,1,0:T(8,128)(2,1)}, u32[]{:S(2)}) copy-start(bf16[1,256,768]{2,1,0:T(8,128)(2,1)} %param.16) | copy-start | bytes 1179652
  11.0 3.7 %copy-start.5 = (f32[768]{0:T(1024)S(1)}, f32[768]{0:T(1024)}, u32[]{:S(2)}) copy-start(f32[768]{0:T(1024)} %gain_ref.7) | copy-start | bytes 9220
  11.7 21.6 %copy-start.7 = (bf16[448,768]{1,0:T(8,128)(2,1)}, bf16[448,768]{1,0:T(8,128)(2,1)S(1)}, u32[]{:S(2)}) copy-start(bf16[448,768]{1,0:T(8,128)(2,1)S(1)} %pad_maximum_fusion.refs_7_.refs_4_) | copy-start | bytes 2064388
  13.0 1.7 collective-permute-start.2
  13.0 20.3 %collective-permute-start.6 = (bf16[448,768]{1,0:T(8,128)(2,1)S(1)}, bf16[448,768]{1,0:T(8,128)(2,1)S(1)}, u32[]{:S(2)}, u32[]{:S(2)}) collective-permute-start(bf16[448,768]{1,0:T(8,128)(2,1)S(1)} %pad_maximum_fusion.refs_7_.refs_4_), channel_id=1, source_target_pairs={{0,2},{1,3},{2,0},{3,1},{4,6},{5,7},{6,4},{7,5},{8,10},{9,11},{10,... | collective-permute-start | bytes 2064392 | tf_op jit(solution)/shard_map/ppermute | solution.py:120
  14.8 30.0 %copy-start.2 = (f32[768]{0:T(1024)S(1)}, f32[768]{0:T(1024)}, u32[]{:S(2)}) copy-start(f32[768]{0:T(1024)} %gain_ref.6) | copy-start | bytes 9220
  14.8 30.0 %copy-start.3 = (s32[8]{0:T(128)S(1)}, s32[8]{0:T(128)}, u32[]{:S(2)}) copy-start(s32[8]{0:T(128)} %groups_ref.3) | copy-start | bytes 100
  31.5 11.5 %collective-permute-start.3 = (bf16[1536,128]{1,0:T(8,128)(2,1)}, bf16[1536,128]{1,0:T(8,128)(2,1)S(1)}, u32[]{:S(2)}, u32[]{:S(2)}) collective-permute-start(bf16[1536,128]{1,0:T(8,128)(2,1)} %get-tuple-element.99.refs_1_), channel_id=1, source_target_pairs={{0,2},{1,3},{2,0},{3,1},{4,6},{5,7},{6,4},{7,5},{8,10},{9,11},{10,... | collective-permute-start | bytes 1179656 | tf_op jit(solution)/shard_map/ppermute | solution.py:120
  33.3 9.8 %collective-permute-start.7 = (bf16[448,768]{1,0:T(8,128)(2,1)S(1)}, bf16[448,768]{1,0:T(8,128)(2,1)S(1)}, u32[]{:S(2)}, u32[]{:S(2)}) collective-permute-start(bf16[448,768]{1,0:T(8,128)(2,1)S(1)} %pad_maximum_fusion.refs_7_.refs_4_), channel_id=1, source_target_pairs={{0,1},{1,0},{2,3},{3,2},{4,5},{5,4},{6,7},{7,6},{8,9},{9,8},{10,11... | collective-permute-start | bytes 2064392 | tf_op jit(solution)/shard_map/ppermute | solution.py:120
  33.3 11.5 %copy-start.9 = (bf16[448,768]{1,0:T(8,128)(2,1)}, bf16[448,768]{1,0:T(8,128)(2,1)S(1)}, u32[]{:S(2)}) copy-start(bf16[448,768]{1,0:T(8,128)(2,1)S(1)} %collective-permute-done.6.refs_8_.refs_5_) | copy-start | bytes 2064388
  33.3 11.5 %collective-permute-start.8 = (bf16[448,768]{1,0:T(8,128)(2,1)S(1)}, bf16[448,768]{1,0:T(8,128)(2,1)}, u32[]{:S(2)}, u32[]{:S(2)}) collective-permute-start(bf16[448,768]{1,0:T(8,128)(2,1)S(1)} %collective-permute-done.6.refs_8_.refs_5_), channel_id=1, source_target_pairs={{0,1},{1,0},{2,3},{3,2},{4,5},{5,4},{6,7},{7,6},{8,9},{9,8},{10,11... | collective-permute-start | bytes 2064392 | tf_op jit(solution)/shard_map/ppermute | solution.py:120
  33.8 9.3 %collective-permute-start.4 = (bf16[1536,128]{1,0:T(8,128)(2,1)}, bf16[1536,128]{1,0:T(8,128)(2,1)S(1)}, u32[]{:S(2)}, u32[]{:S(2)}) collective-permute-start(bf16[1536,128]{1,0:T(8,128)(2,1)} %get-tuple-element.99.refs_1_), channel_id=1, source_target_pairs={{0,1},{1,0},{2,3},{3,2},{4,5},{5,4},{6,7},{7,6},{8,9},{9,8},{10,11... | collective-permute-start | bytes 1179656 | tf_op jit(solution)/shard_map/ppermute | solution.py:120
  43.0 1.7 collective-permute-start.5
  43.0 1.7 copy-start.10
  61.2 16.5 %collective-permute-start.11 = (bf16[768,768]{1,0:T(8,128)(2,1)}, bf16[768,768]{1,0:T(8,128)(2,1)S(1)}, u32[]{:S(2)}, u32[]{:S(2)}) collective-permute-start(bf16[768,768]{1,0:T(8,128)(2,1)} %get-tuple-element.114), channel_id=1, source_target_pairs={{0,4},{1,9},{2,6},{3,11},{4,0},{5,13},{6,2},{7,15},{8,12},{9,1},{1... | collective-permute-start | bytes 3538952 | tf_op jit(solution)/shard_map/ppermute | solution.py:156
  62.8 2.5 %collective-permute-start.9 = (bf16[512,768]{1,0:T(8,128)(2,1)}, bf16[512,768]{1,0:T(8,128)(2,1)S(1)}, u32[]{:S(2)}, u32[]{:S(2)}) collective-permute-start(bf16[512,768]{1,0:T(8,128)(2,1)} %get-tuple-element.107), channel_id=1, source_target_pairs={{0,1},{1,0},{2,3},{3,2},{4,5},{5,4},{6,7},{7,6},{8,9},{9,8},{10,11... | collective-permute-start | bytes 2359304 | tf_op jit(solution)/shard_map/ppermute | solution.py:120
  67.3 19.9 %collective-permute-start.13 = (bf16[512,768]{1,0:T(8,128)(2,1)S(1)}, bf16[512,768]{1,0:T(8,128)(2,1)S(1)}, u32[]{:S(2)}, u32[]{:S(2)}) collective-permute-start(bf16[512,768]{1,0:T(8,128)(2,1)S(1)} %get-tuple-element.121), channel_id=1, source_target_pairs={{0,2},{1,3},{2,0},{3,1},{4,6},{5,7},{6,4},{7,5},{8,10},{9,11},{10,... | collective-permute-start | bytes 2359304 | tf_op jit(solution)/shard_map/ppermute | solution.py:120
  73.9 7.9 %copy-start.16 = (bf16[256,768]{1,0:T(8,128)(2,1)S(1)}, bf16[256,768]{1,0:T(8,128)(2,1)}, u32[]{:S(2)}) copy-start(bf16[256,768]{1,0:T(8,128)(2,1)} %get-tuple-element.112) | copy-start | bytes 1179652
  73.9 7.9 %copy-start.15 = (bf16[256,768]{1,0:T(8,128)(2,1)S(1)}, bf16[256,768]{1,0:T(8,128)(2,1)}, u32[]{:S(2)}) copy-start(bf16[256,768]{1,0:T(8,128)(2,1)} %get-tuple-element.119) | copy-start | bytes 1179652
  80.2 9.9 %collective-permute-start.15 = (bf16[384,768]{1,0:T(8,128)(2,1)S(1)}, bf16[384,768]{1,0:T(8,128)(2,1)S(1)}, u32[]{:S(2)}, u32[]{:S(2)}) collective-permute-start(bf16[384,768]{1,0:T(8,128)(2,1)S(1)} %get-tuple-element.116), channel_id=1, source_target_pairs={{0,8},{1,5},{2,10},{3,7},{4,12},{5,1},{6,14},{7,3},{8,0},{9,13},{1... | collective-permute-start | bytes 1769480 | tf_op jit(solution)/shard_map/ppermute | solution.py:156
  81.8 1.7 collective-permute-start.10
  81.8 3.6 %collective-permute-start.12 = (bf16[256,768]{1,0:T(8,128)(2,1)S(1)}, bf16[256,768]{1,0:T(8,128)(2,1)S(1)}, u32[]{:S(2)}, u32[]{:S(2)}) collective-permute-start(bf16[256,768]{1,0:T(8,128)(2,1)S(1)} %copy-done.15), channel_id=1, source_target_pairs={{0,1},{1,0},{2,3},{3,2},{4,5},{5,4},{6,7},{7,6},{8,9},{9,8},{10,11... | collective-permute-start | bytes 1179656 | tf_op jit(solution)/shard_map/ppermute | solution.py:120
  89.4 5.3 %copy-start = (bf16[256,768]{1,0:T(8,128)(2,1)S(1)}, bf16[256,768]{1,0:T(8,128)(2,1)}, u32[]{:S(2)}) copy-start(bf16[256,768]{1,0:T(8,128)(2,1)} %get-tuple-element.123.refs_0_) | copy-start | bytes 1179652
  89.4 5.4 %copy-start.1 = (bf16[256,768]{1,0:T(8,128)(2,1)S(1)}, bf16[256,768]{1,0:T(8,128)(2,1)}, u32[]{:S(2)}) copy-start(bf16[256,768]{1,0:T(8,128)(2,1)} %get-tuple-element.124.refs_1_) | copy-start | bytes 1179652
  89.4 5.3 %collective-permute-start.16 = (bf16[256,768]{1,0:T(8,128)(2,1)}, bf16[256,768]{1,0:T(8,128)(2,1)S(1)}, u32[]{:S(2)}, u32[]{:S(2)}) collective-permute-start(bf16[256,768]{1,0:T(8,128)(2,1)} %get-tuple-element.124.refs_1_), channel_id=1, source_target_pairs={{0,1},{1,0},{2,3},{3,2},{4,5},{5,4},{6,7},{7,6},{8,9},{9,8},{10,11... | collective-permute-start | bytes 1179656 | tf_op jit(solution)/shard_map/ppermute | solution.py:120
  89.5 5.2 %collective-permute-start.14 = (bf16[256,768]{1,0:T(8,128)(2,1)}, bf16[256,768]{1,0:T(8,128)(2,1)S(1)}, u32[]{:S(2)}, u32[]{:S(2)}) collective-permute-start(bf16[256,768]{1,0:T(8,128)(2,1)} %get-tuple-element.123.refs_0_), channel_id=1, source_target_pairs={{0,1},{1,0},{2,3},{3,2},{4,5},{5,4},{6,7},{7,6},{8,9},{9,8},{10,11... | collective-permute-start | bytes 1179656 | tf_op jit(solution)/shard_map/ppermute | solution.py:120
  92.0 25.0 %collective-permute-start.19 = (bf16[192,768]{1,0:T(8,128)(2,1)S(1)}, bf16[192,768]{1,0:T(8,128)(2,1)S(1)}, u32[]{:S(2)}, u32[]{:S(2)}) collective-permute-start(bf16[192,768]{1,0:T(8,128)(2,1)S(1)} %get-tuple-element.127), channel_id=1, source_target_pairs={{0,16},{1,17},{2,18},{3,19},{4,20},{5,21},{6,22},{7,23},{8,24},{9,... | collective-permute-start | bytes 884744 | tf_op jit(solution)/shard_map/ppermute | solution.py:156
  115.4 3.7 %collective-permute-start.18 = (bf16[512,768]{1,0:T(8,128)(2,1)}, bf16[512,768]{1,0:T(8,128)(2,1)S(1)}, u32[]{:S(2)}, u32[]{:S(2)}) collective-permute-start(bf16[512,768]{1,0:T(8,128)(2,1)} %get-tuple-element.141), channel_id=1, source_target_pairs={{0,1},{1,0},{2,3},{3,2},{4,5},{5,4},{6,7},{7,6},{8,9},{9,8},{10,11... | collective-permute-start | bytes 2359304 | tf_op jit(solution)/shard_map/ppermute | solution.py:120
  115.5 10.7 %collective-permute-start.17 = (bf16[416,768]{1,0:T(8,128)(2,1)}, bf16[416,768]{1,0:T(8,128)(2,1)S(1)}, u32[]{:S(2)}, u32[]{:S(2)}) collective-permute-start(bf16[416,768]{1,0:T(8,128)(2,1)} %get-tuple-element.139), channel_id=1, source_target_pairs={{0,4},{1,9},{2,6},{3,11},{4,0},{5,13},{6,2},{7,15},{8,12},{9,1},{1... | collective-permute-start | bytes 1916936 | tf_op jit(solution)/shard_map/ppermute | solution.py:156
  118.8 16.7 %collective-permute-start.21 = (bf16[192,768]{1,0:T(8,128)(2,1)}, bf16[192,768]{1,0:T(8,128)(2,1)S(1)}, u32[]{:S(2)}, u32[]{:S(2)}) collective-permute-start(bf16[192,768]{1,0:T(8,128)(2,1)} %add.41.own_ref), channel_id=1, source_target_pairs={{0,16},{1,17},{2,18},{3,19},{4,20},{5,21},{6,22},{7,23},{8,24},{9,... | collective-permute-start | bytes 884744 | tf_op jit(solution)/shard_map/ppermute | solution.py:156
  128.2 9.1 %copy-start.14 = (bf16[256,768]{1,0:T(8,128)(2,1)S(1)}, bf16[256,768]{1,0:T(8,128)(2,1)}, u32[]{:S(2)}) copy-start(bf16[256,768]{1,0:T(8,128)(2,1)} %get-tuple-element.162) | copy-start | bytes 1179652
  128.2 10.8 %collective-permute-start.20 = (bf16[224,768]{1,0:T(8,128)(2,1)S(1)}, bf16[224,768]{1,0:T(8,128)(2,1)S(1)}, u32[]{:S(2)}, u32[]{:S(2)}) collective-permute-start(bf16[224,768]{1,0:T(8,128)(2,1)S(1)} %get-tuple-element.150), channel_id=1, source_target_pairs={{0,8},{1,5},{2,10},{3,7},{4,12},{5,1},{6,14},{7,3},{8,0},{9,13},{1... | collective-permute-start | bytes 1032200 | tf_op jit(solution)/shard_map/ppermute | solution.py:156
  137.3 12.1 %collective-permute-start.24 = (bf16[384,768]{1,0:T(8,128)(2,1)}, bf16[384,768]{1,0:T(8,128)(2,1)S(1)}, u32[]{:S(2)}, u32[]{:S(2)}) collective-permute-start(bf16[384,768]{1,0:T(8,128)(2,1)} %join.4.own_ref), channel_id=1, source_target_pairs={{0,8},{1,5},{2,10},{3,7},{4,12},{5,1},{6,14},{7,3},{8,0},{9,13},{1... | collective-permute-start | bytes 1769480 | tf_op jit(solution)/shard_map/ppermute | solution.py:156
  137.3 17.6 %collective-permute-start.27 = (bf16[256,768]{1,0:T(8,128)(2,1)S(1)}, bf16[256,768]{1,0:T(8,128)(2,1)S(1)}, u32[]{:S(2)}, u32[]{:S(2)}) collective-permute-start(bf16[256,768]{1,0:T(8,128)(2,1)S(1)} %copy-done.14), channel_id=1, source_target_pairs={{0,2},{1,3},{2,0},{3,1},{4,6},{5,7},{6,4},{7,5},{8,10},{9,11},{10,... | collective-permute-start | bytes 1179656 | tf_op jit(solution)/shard_map/ppermute | solution.py:120
  139.0 2.4 %copy-start.12 = (bf16[256,768]{1,0:T(8,128)(2,1)S(1)}, bf16[256,768]{1,0:T(8,128)(2,1)}, u32[]{:S(2)}) copy-start(bf16[256,768]{1,0:T(8,128)(2,1)} %add.40) | copy-start | bytes 1179652
  140.8 14.8 %copy-start.6 = (f32[768]{0:T(1024)S(1)}, f32[768]{0:T(1024)}, u32[]{:S(2)}) copy-start(f32[768]{0:T(1024)} %gain_ref.7) | copy-start | bytes 9220
  140.8 12.4 %collective-permute-start.23 = (bf16[128,768]{1,0:T(8,128)(2,1)S(1)}, bf16[128,768]{1,0:T(8,128)(2,1)S(1)}, u32[]{:S(2)}, u32[]{:S(2)}) collective-permute-start(bf16[128,768]{1,0:T(8,128)(2,1)S(1)} %get-tuple-element.154), channel_id=1, source_target_pairs={{0,16},{1,17},{2,18},{3,19},{4,20},{5,21},{6,22},{7,23},{8,24},{9,... | collective-permute-start | bytes 589832 | tf_op jit(solution)/shard_map/ppermute | solution.py:156
  141.4 25.4 %collective-permute-start.22 = (bf16[256,768]{1,0:T(8,128)(2,1)S(1)}, bf16[256,768]{1,0:T(8,128)(2,1)S(1)}, u32[]{:S(2)}, u32[]{:S(2)}) collective-permute-start(bf16[256,768]{1,0:T(8,128)(2,1)S(1)} %copy-done.12), channel_id=1, source_target_pairs={{0,2},{1,3},{2,0},{3,1},{4,6},{5,7},{6,4},{7,5},{8,10},{9,11},{10,... | collective-permute-start | bytes 1179656 | tf_op jit(solution)/shard_map/ppermute | solution.py:120
  151.6 25.3 %collective-permute-start.31 = (bf16[768,768]{1,0:T(8,128)(2,1)}, bf16[768,768]{1,0:T(8,128)(2,1)S(1)}, u32[]{:S(2)}, u32[]{:S(2)}) collective-permute-start(bf16[768,768]{1,0:T(8,128)(2,1)} %join.5.own_ref), channel_id=1, source_target_pairs={{0,4},{1,9},{2,6},{3,11},{4,0},{5,13},{6,2},{7,15},{8,12},{9,1},{1... | collective-permute-start | bytes 3538952 | tf_op jit(solution)/shard_map/ppermute | solution.py:156
  154.9 8.1 %collective-permute-start.25 = (bf16[96,768]{1,0:T(8,128)(2,1)}, bf16[96,768]{1,0:T(8,128)(2,1)S(1)}, u32[]{:S(2)}, u32[]{:S(2)}) collective-permute-start(bf16[96,768]{1,0:T(8,128)(2,1)} %get-tuple-element.160.own_ref), channel_id=1, source_target_pairs={{0,16},{1,17},{2,18},{3,19},{4,20},{5,21},{6,22},{7,23},{8,24},{9,... | collective-permute-start | bytes 442376 | tf_op jit(solution)/shard_map/ppermute | solution.py:156
  155.6 2.4 %copy-start.13 = (f32[8,768]{1,0:T(8,128)}, f32[8,768]{1,0:T(8,128)S(1)}, u32[]{:S(2)}) copy-start(f32[8,768]{1,0:T(8,128)S(1)} %slice.12.left_ref) | copy-start | bytes 73732
  155.6 2.4 %collective-permute-start.26 = (f32[8,768]{1,0:T(8,128)S(1)}, f32[8,768]{1,0:T(8,128)S(1)}, u32[]{:S(2)}, u32[]{:S(2)}) collective-permute-start(f32[8,768]{1,0:T(8,128)S(1)} %slice.12.left_ref), channel_id=1, source_target_pairs={{0,1},{1,0},{2,3},{3,2},{4,5},{5,4},{6,7},{7,6},{8,9},{9,8},{10,11... | collective-permute-start | bytes 73736 | tf_op jit(solution)/shard_map/ppermute | solution.py:120
  164.6 7.4 %collective-permute-start.29 = (bf16[192,768]{1,0:T(8,128)(2,1)}, bf16[192,768]{1,0:T(8,128)(2,1)S(1)}, u32[]{:S(2)}, u32[]{:S(2)}) collective-permute-start(bf16[192,768]{1,0:T(8,128)(2,1)} %join.6.own_ref), channel_id=1, source_target_pairs={{0,8},{1,5},{2,10},{3,7},{4,12},{5,1},{6,14},{7,3},{8,0},{9,13},{1... | collective-permute-start | bytes 884744 | tf_op jit(solution)/shard_map/ppermute | solution.py:156
  164.6 4.4 %collective-permute-start.28 = (f32[8,768]{1,0:T(8,128)}, f32[8,768]{1,0:T(8,128)S(1)}, u32[]{:S(2)}, u32[]{:S(2)}) collective-permute-start(f32[8,768]{1,0:T(8,128)} %add.42.left_ref), channel_id=1, source_target_pairs={{0,2},{1,3},{2,0},{3,1},{4,6},{5,7},{6,4},{7,5},{8,10},{9,11},{10,... | collective-permute-start | bytes 73736 | tf_op jit(solution)/shard_map/ppermute | solution.py:120
  173.7 10.1 %collective-permute-start.30 = (bf16[384,768]{1,0:T(8,128)(2,1)}, bf16[384,768]{1,0:T(8,128)(2,1)S(1)}, u32[]{:S(2)}, u32[]{:S(2)}) collective-permute-start(bf16[384,768]{1,0:T(8,128)(2,1)} %join.7.own_ref), channel_id=1, source_target_pairs={{0,4},{1,9},{2,6},{3,11},{4,0},{5,13},{6,2},{7,15},{8,12},{9,1},{1... | collective-permute-start | bytes 1769480 | tf_op jit(solution)/shard_map/ppermute | solution.py:156

commit v4 on v3

--- a/solution.py
+++ b/solution.py
@@ -17,10 +17,10 @@
 HEAVY = pl.CostEstimate(flops=10**11, bytes_accessed=1024, transcendentals=0)
 LIGHT = pl.CostEstimate(flops=1024, bytes_accessed=1024, transcendentals=0)
 ORDER = (
-    "swap_dn", "out_part", "feed1", "swap_out", "sum_dn", "feed2", "back",
-    "feed3", "swap_in", "two1", "feed4", "two2", "go_mixed",
-    "feed5", "two3", "end_tokens", "gains_a", "two4", "end_mixed",
-    "gains_b", "two5", "end_feed", "end_heads",
+    "swap_dn", "out_part", "feed1", "swap_out", "sum_dn", "feed2",
+    "back", "feed3", "swap_in", "two1", "feed4", "two2",
+    "go_mixed", "feed5", "two3", "end_tokens", "gains_a", "end_mixed",
+    "two4", "gains_b", "two5", "end_feed", "end_heads",
 )
 LONG = (
     "feed", "end_tokens", "feed3", "feed4", "two2",

time: 188 us -> 188 us (level)
    ppermute x12, waiting for transfers between devices: 30.3 us -> 28.2 us  [swap_dp(): return lax.ppermute(value, ('dp', 'tensor'), route)]
    ppermute x20, waiting for transfers between devices: 15.9 us -> 17.9 us  [swap_tensor(): return lax.ppermute(value, 'tensor', [(i, i ^ bit) for i in range(size)])]
  transfers between devices with their start and end apart: 32 -> 32, of which waited for: 14 -> 15; matrix products, arithmetic and copies ran while one was open for 4% -> 4% of each run, Pallas kernels for 46% -> 46%
where the time goes in v4:
time: 188 us; the launch traced here: 186 us
  Pallas kernels  105 us (56%)
  waiting for transfers between devices  46.1 us (25%)
  starting transfers between devices  26.8 us (14%)
  local copies, waits for them, and re-layouts  6.19 us (3%)
    pallas_call x26, Pallas kernels, run(): return call(*args[:prefetch], *given)  105 us
    ppermute x12, waiting for transfers between devices, swap_dp(): return lax.ppermute(value, ('dp', 'tensor'), route)  28.2 us
    ppermute x20, waiting for transfers between devices, swap_tensor(): return lax.ppermute(value, 'tensor', [(i, i ^ bit) for i in range(size)])  17.9 us
    ppermute x20, starting transfers between devices, swap_tensor(): return lax.ppermute(value, 'tensor', [(i, i ^ bit) for i in range(size)])  14.2 us
    ppermute x12, starting transfers between devices, swap_dp(): return lax.ppermute(value, ('dp', 'tensor'), route)  12.6 us
  transfers between devices with their start and end apart: 32, of which 15 were waited for; matrix products, arithmetic and copies ran while one was open for 4% of the time, Pallas kernels for 46%

profile of v4, /device:TPU:0, one launch (start us, length us, event | category | flops | bytes accessed | tf_op | source)
XLA Modules:
  0.0 186.4 jit_solution(8098753308277216949)
XLA Ops:
  0.6 3.0 %collective-permute-start = (bf16[256,768]{1,0:T(8,128)(2,1)}, bf16[256,768]{1,0:T(8,128)(2,1)S(1)}, u32[]{:S(2)}, u32[]{:S(2)}) collective-permute-start(bf16[256,768]{1,0:T(8,128)(2,1)} %bitcast.20), channel_id=1, source_target_pairs={{0,2},{1,3},{2,0},{3,1},{4,6},{5,7},{6,4},{7,5},{8,10},{9,11},{10,... | collective-permute-start | bytes 1179656 | tf_op jit(solution)/shard_map/ppermute | solution.py:120
  4.3 0.7 compare_reduce_fusion
  5.0 0.8 reverse
  5.9 0.8 copy.27.table_ref
  6.6 0.6 broadcast_in_dim.56.buckets_ref
  7.3 3.7 %bias_tiles.1.refs_4_ = f32[3,128,2048]{2,1,0:T(8,128)} custom-call(f32[32,3]{1,0:T(8,128)S(1)} %copy.27.table_ref, s32[8,2048]{1,0:T(8,128)} %broadcast_in_dim.56.buckets_ref), custom_call_target="tpu_custom_call" | custom-call | flops 99999997952 | bytes 1024 | tf_op jit(solution)/shard_map/bias_tiles/pallas_call | solution.py:67
  11.7 1.3 collective-permute-done.refs_1_
  13.0 1.7 collective-permute-start.6
  14.8 16.7 %attend.1 = (bf16[1024,192]{1,0:T(8,128)(2,1)}, bf16[1536,128]{1,0:T(8,128)(2,1)}, bf16[3,1024,1024]{2,1,0:T(8,128)(2,1)}, f32[1024,128]{1,0:T(8,128)}, bf16[102...) custom-call(s32[1]{0:T(128)} %copy.28.length_ref, ...), custom_call_target="tpu_custom_call" | custom-call | flops 99999997952 | bytes 1024 | tf_op jit(solution)/shard_map/attend/pallas_call | solution.py:67
  31.5 1.8 collective-permute-start.3
  33.3 0.5 collective-permute-start.8
  33.8 9.2 %collective-permute-done.3.refs_2_ = bf16[1536,128]{1,0:T(8,128)(2,1)S(1)} collective-permute-done((bf16[1536,128]{1,0:T(8,128)(2,1)}, bf16[1536,128]{1,0:T(8,128)(2,1)S(1)}, u32[]{:S(2)}, u32[]{:S(2)}) %collective-permute-start.3) | collective-permute-done | bytes 393248 | tf_op jit(solution)/shard_map/ppermute | solution.py:120
  43.0 1.7 collective-permute-done.5.refs_4_
  44.8 16.3 %feed.1 = (f32[256,768]{1,0:T(8,128)}, bf16[1024,768]{1,0:T(8,128)(2,1)}, f32[1024,128]{1,0:T(8,128)}, bf16[1024,768]{1,0:T(8,128)(2,1)}, bf16[512,768]{1,0:T(8,...) custom-call(s32[1]{0:T(128)} %bitcast.side_ref, s32[8]{0:T(128)S(1)} %copy-done.3, ...), custom_call_target="tpu_custom_call" | custom-call | flops 99999997952 | bytes 1024 | tf_op jit(solution)/shard_map/feed/pallas_call | solution.py:67
  61.1 1.6 collective-permute-start.11
  62.7 2.5 %collective-permute-done.9.right_ref = bf16[512,768]{1,0:T(8,128)(2,1)S(1)} collective-permute-done((bf16[512,768]{1,0:T(8,128)(2,1)}, bf16[512,768]{1,0:T(8,128)(2,1)S(1)}, u32[]{:S(2)}, u32[]{:S(2)}) %collective-permute-start.9) | collective-permute-done | bytes 786464 | tf_op jit(solution)/shard_map/ppermute | solution.py:120
  65.2 2.0 %add_swap.1 = (bf16[512,768]{1,0:T(8,128)(2,1)}, bf16[512,768]{1,0:T(8,128)(2,1)S(1)}) custom-call(bf16[512,768]{1,0:T(8,128)(2,1)} %get-tuple-element.106.left_ref, bf16[512,768]{1,0:T(8,128)(2,1)S(1)} %collective-permute-done.9.right_ref), custom_call_target="tpu_custom_call" | custom-call | flops 1024 | bytes 1024 | tf_op jit(solution)/shard_map/add_swap/pallas_call | solution.py:67
  67.2 1.5 collective-permute-start.13
  68.7 5.1 %feed_out.1 = (bf16[256,768]{1,0:T(8,128)(2,1)}, bf16[256,768]{1,0:T(8,128)(2,1)}, bf16[256,768]{1,0:T(8,128)(2,1)}, bf16[256,768]{1,0:T(8,128)(2,1)}) custom-call(bf16[1024,768]{1,0:T(8,128)(2,1)} %get-tuple-element.110.active_ref, bf16[768,768]{1,0:T(8,128)(2,1)} %w_back_ref.1), custom_call_target="tpu_custom_call" | custom-call | flops 1024 | bytes 1024 | tf_op jit(solution)/shard_map/feed_out/pallas_call | solution.py:67
  73.8 3.8 %collective-permute-done.11.came_ref = bf16[768,768]{1,0:T(8,128)(2,1)S(1)} collective-permute-done((bf16[768,768]{1,0:T(8,128)(2,1)}, bf16[768,768]{1,0:T(8,128)(2,1)S(1)}, u32[]{:S(2)}, u32[]{:S(2)}) %collective-permute-start.11) | collective-permute-done | bytes 1179680 | tf_op jit(solution)/shard_map/ppermute | solution.py:156
  77.6 2.5 %fold.2 = (bf16[384,768]{1,0:T(8,128)(2,1)S(1)}, bf16[384,768]{1,0:T(8,128)(2,1)}) custom-call(s32[1]{0:T(128)} %bitcast.8.side_ref, bf16[768,768]{1,0:T(8,128)(2,1)} %get-tuple-element.113.kept_ref, bf16[768,768]{1,0:T(8,128)(2,1)S(1)} %collective-permute-done.11.came_ref), custom_call_target="tpu_custom_call" | custom-call | flops 1024 | bytes 1024 | tf_op jit(solution)/shard_map/fold/pallas_call | solution.py:67
  80.1 1.7 collective-permute-start.15
  81.7 0.5 collective-permute-start.12
  82.2 1.2 collective-permute-done.10.right_ref
  83.5 1.8 add.39.own_ref
  85.3 1.8 add.40
  87.1 2.1 %add_pieces.2 = (bf16[256,768]{1,0:T(8,128)(2,1)}, bf16[256,768]{1,0:T(8,128)(2,1)}) custom-call(bf16[512,768]{1,0:T(8,128)(2,1)} %get-tuple-element.109.refs_0_, bf16[512,768]{1,0:T(8,128)(2,1)S(1)} %collective-permute-done.13.refs_1_), custom_call_target="tpu_custom_call" | custom-call | flops 1024 | bytes 1024 | tf_op jit(solution)/shard_map/add_pieces/pallas_call | solution.py:67
  90.0 2.0 %fold.3 = (bf16[192,768]{1,0:T(8,128)(2,1)S(1)}, bf16[192,768]{1,0:T(8,128)(2,1)}) custom-call(s32[1]{0:T(128)} %bitcast.9.side_ref, bf16[384,768]{1,0:T(8,128)(2,1)} %get-tuple-element.125.kept_ref, bf16[384,768]{1,0:T(8,128)(2,1)S(1)} %collective-permute-done.15.came_ref), custom_call_target="tpu_custom_call" | custom-call | flops 1024 | bytes 1024 | tf_op jit(solution)/shard_map/fold/pallas_call | solution.py:67
  91.9 2.7 %collective-permute-start.19 = (bf16[192,768]{1,0:T(8,128)(2,1)S(1)}, bf16[192,768]{1,0:T(8,128)(2,1)S(1)}, u32[]{:S(2)}, u32[]{:S(2)}) collective-permute-start(bf16[192,768]{1,0:T(8,128)(2,1)S(1)} %get-tuple-element.127), channel_id=1, source_target_pairs={{0,16},{1,17},{2,18},{3,19},{4,20},{5,21},{6,22},{7,23},{8,24},{9,... | collective-permute-start | bytes 884744 | tf_op jit(solution)/shard_map/ppermute | solution.py:156
  94.6 20.7 %attend_back.1 = (bf16[256,768]{1,0:T(8,128)(2,1)}, bf16[32,768]{1,0:T(8,128)(2,1)}, bf16[416,768]{1,0:T(8,128)(2,1)}, bf16[384,768]{1,0:T(8,128)(2,1)}, bf16[51...) custom-call(s32[1]{0:T(128)} %bitcast.side_ref, s32[4]{0:T(128)S(1)} %xor_multiply_fusion.starts_ref, s32[8]{0:T(128)S(1)} %copy-done.3, ...), custom_call_target="tpu_custom_call" | custom-call | flops 1024 | bytes 1024 | tf_op jit(solution)/shard_map/attend_back/pallas_call | solution.py:67
  115.4 1.6 collective-permute-start.17
  117.0 1.7 add.41.own_ref
  119.0 2.1 %add_pieces.3 = (bf16[256,768]{1,0:T(8,128)(2,1)}, bf16[256,768]{1,0:T(8,128)(2,1)}) custom-call(bf16[512,768]{1,0:T(8,128)(2,1)} %get-tuple-element.140.refs_0_, bf16[512,768]{1,0:T(8,128)(2,1)S(1)} %collective-permute-done.18.refs_1_), custom_call_target="tpu_custom_call" | custom-call | flops 1024 | bytes 1024 | tf_op jit(solution)/shard_map/add_pieces/pallas_call | solution.py:67
  121.1 4.9 %collective-permute-done.17.came_ref.small_came_ref = bf16[416,768]{1,0:T(8,128)(2,1)S(1)} collective-permute-done((bf16[416,768]{1,0:T(8,128)(2,1)}, bf16[416,768]{1,0:T(8,128)(2,1)S(1)}, u32[]{:S(2)}, u32[]{:S(2)}) %collective-permute-start.17) | collective-permute-done | bytes 639008 | tf_op jit(solution)/shard_map/ppermute | solution.py:156
  126.1 2.0 %fold_small.2 = (bf16[224,768]{1,0:T(8,128)(2,1)S(1)}, bf16[192,768]{1,0:T(8,128)(2,1)}, bf16[32,768]{1,0:T(8,128)(2,1)}) custom-call(s32[1]{0:T(128)} %bitcast.8.side_ref, bf16[384,768]{1,0:T(8,128)(2,1)} %get-tuple-element.138.kept_ref, bf16[416,768]{1,0:T(8,128)(2,1)S(1)} %collective-permute-done.17.came_ref.small_came_ref, ...), custom_call_target="tpu_custom_call" | custom-call | flops 1024 | bytes 1024 | tf_op jit(solution)/shard_map/fold_small/pallas_call | solution.py:67
  128.1 1.6 collective-permute-start.20
  129.7 5.8 %collective-permute-done.21.came_ref = bf16[192,768]{1,0:T(8,128)(2,1)S(1)} collective-permute-done((bf16[192,768]{1,0:T(8,128)(2,1)}, bf16[192,768]{1,0:T(8,128)(2,1)S(1)}, u32[]{:S(2)}, u32[]{:S(2)}) %collective-permute-start.21) | collective-permute-done | bytes 294944 | tf_op jit(solution)/shard_map/ppermute | solution.py:156
  135.4 1.8 join.4.own_ref
  137.2 1.6 collective-permute-start.26
  138.9 1.8 fold_small.3
  140.7 0.6 collective-permute-start.23
  141.3 1.0 collective-permute-start.22
  142.3 7.0 %collective-permute-done.24.came_ref = bf16[384,768]{1,0:T(8,128)(2,1)S(1)} collective-permute-done((bf16[384,768]{1,0:T(8,128)(2,1)}, bf16[384,768]{1,0:T(8,128)(2,1)S(1)}, u32[]{:S(2)}, u32[]{:S(2)}) %collective-permute-start.24) | collective-permute-done | bytes 589856 | tf_op jit(solution)/shard_map/ppermute | solution.py:156
  149.3 2.2 %join.5.own_ref = bf16[768,768]{1,0:T(8,128)(2,1)} custom-call(s32[1]{0:T(128)} %bitcast.8.side_ref, bf16[384,768]{1,0:T(8,128)(2,1)} %join.4.own_ref, bf16[384,768]{1,0:T(8,128)(2,1)S(1)} %collective-permute-done.24.came_ref), custom_call_target="tpu_custom_call" | custom-call | flops 1024 | bytes 1024 | tf_op jit(solution)/shard_map/join/pallas_call | solution.py:67
  151.5 1.6 collective-permute-start.31
  153.1 1.6 add_small.1
  154.8 0.7 slice.12.left_ref
  155.5 2.4 %finish_tokens.1 = f32[256,768]{1,0:T(8,128)} custom-call(f32[768]{0:T(1024)S(1)} %copy-done.6, bf16[256,768]{1,0:T(8,128)(2,1)} %bitcast.22, bf16[256,768]{1,0:T(8,128)(2,1)} %get-tuple-element.146.own_ref, bf16[256,768]{1,0:T(8,128)(2,1)S(1)} %collective-permute-done.26.came_ref, bf16[256,768]{1,0:T(8,128)(2,1)} %get-tuple-element.143.dh_ref), custom_call_target="tpu_custom_call" | custom-call | flops 99999997952 | bytes 1024 | tf_op jit(solution)/shard_map/finish_tokens/pallas_call | solution.py:67
  157.9 1.4 add.42.left_ref
  159.3 2.1 %finish_mixed.1 = bf16[256,768]{1,0:T(8,128)(2,1)} custom-call(f32[256,768]{1,0:T(8,128)} %get-tuple-element.104.hidden_ref, bf16[256,768]{1,0:T(8,128)(2,1)} %add.39.own_ref, bf16[256,768]{1,0:T(8,128)(2,1)S(1)} %collective-permute-done.22.came_ref), custom_call_target="tpu_custom_call" | custom-call | flops 1024 | bytes 1024 | tf_op jit(solution)/shard_map/finish_mixed/pallas_call | solution.py:67
  161.4 1.4 collective-permute-done.28.came_ref
  162.8 1.6 join.6.own_ref
  164.5 0.5 collective-permute-start.29
  165.0 1.9 %collective-permute-start.27 = (f32[8,768]{1,0:T(8,128)S(1)}, f32[8,768]{1,0:T(8,128)S(1)}, u32[]{:S(2)}, u32[]{:S(2)}) collective-permute-start(f32[8,768]{1,0:T(8,128)S(1)} %copy-done.14), channel_id=1, source_target_pairs={{0,2},{1,3},{2,0},{3,1},{4,6},{5,7},{6,4},{7,5},{8,10},{9,11},{10,... | collective-permute-start | bytes 73736 | tf_op jit(solution)/shard_map/ppermute | solution.py:120
  166.9 1.9 %collective-permute-done.27.right_ref = f32[8,768]{1,0:T(8,128)S(1)} collective-permute-done((f32[8,768]{1,0:T(8,128)S(1)}, f32[8,768]{1,0:T(8,128)S(1)}, u32[]{:S(2)}, u32[]{:S(2)}) %collective-permute-start.27) | collective-permute-done | bytes 24608 | tf_op jit(solution)/shard_map/ppermute | solution.py:120
  168.8 1.4 add.43
  170.1 1.7 collective-permute-done.29.came_ref
  171.8 1.8 join.7.own_ref
  173.6 0.5 collective-permute-start.30
  174.1 1.3 slice_bitcast_fusion
  175.4 1.4 slice_reduce_fusion
  176.8 3.6 %finish_feed.1 = (f32[768,768]{1,0:T(8,128)}, f32[768,768]{1,0:T(8,128)}) custom-call(s32[1]{0:T(128)} %bitcast.side_ref, bf16[768,768]{1,0:T(8,128)(2,1)} %join.5.own_ref, bf16[768,768]{1,0:T(8,128)(2,1)S(1)} %collective-permute-done.31.came_ref), custom_call_target="tpu_custom_call" | custom-call | flops 1024 | bytes 1024 | tf_op jit(solution)/shard_map/finish_feed/pallas_call | solution.py:67
  180.4 3.3 %collective-permute-done.30.came_ref = bf16[384,768]{1,0:T(8,128)(2,1)S(1)} collective-permute-done((bf16[384,768]{1,0:T(8,128)(2,1)}, bf16[384,768]{1,0:T(8,128)(2,1)S(1)}, u32[]{:S(2)}, u32[]{:S(2)}) %collective-permute-start.30) | collective-permute-done | bytes 589856 | tf_op jit(solution)/shard_map/ppermute | solution.py:156
  183.7 2.7 %finish_heads.1 = (f32[192,768]{1,0:T(8,128)}, f32[192,768]{1,0:T(8,128)}, f32[192,768]{1,0:T(8,128)}, f32[192,768]{1,0:T(8,128)}) custom-call(s32[1]{0:T(128)} %bitcast.side_ref, bf16[384,768]{1,0:T(8,128)(2,1)} %join.7.own_ref, bf16[384,768]{1,0:T(8,128)(2,1)S(1)} %collective-permute-done.30.came_ref), custom_call_target="tpu_custom_call" | custom-call | flops 1024 | bytes 1024 | tf_op jit(solution)/shard_map/finish_heads/pallas_call | solution.py:67
  (77 shorter events, 2.1 us)
Async XLA Ops:
  0.6 12.4 %collective-permute-start = (bf16[256,768]{1,0:T(8,128)(2,1)}, bf16[256,768]{1,0:T(8,128)(2,1)S(1)}, u32[]{:S(2)}, u32[]{:S(2)}) collective-permute-start(bf16[256,768]{1,0:T(8,128)(2,1)} %bitcast.20), channel_id=1, source_target_pairs={{0,2},{1,3},{2,0},{3,1},{4,6},{5,7},{6,4},{7,5},{8,10},{9,11},{10,... | collective-permute-start | bytes 1179656 | tf_op jit(solution)/shard_map/ppermute | solution.py:120
  3.7 11.1 %collective-permute-start.1 = (bf16[256,768]{1,0:T(8,128)(2,1)}, bf16[256,768]{1,0:T(8,128)(2,1)S(1)}, u32[]{:S(2)}, u32[]{:S(2)}) collective-permute-start(bf16[256,768]{1,0:T(8,128)(2,1)} %bitcast.21), channel_id=1, source_target_pairs={{0,1},{1,0},{2,3},{3,2},{4,5},{5,4},{6,7},{7,6},{8,9},{9,8},{10,11... | collective-permute-start | bytes 1179656 | tf_op jit(solution)/shard_map/ppermute | solution.py:120
  7.3 3.8 %copy-start.11 = (bf16[1,256,768]{2,1,0:T(8,128)(2,1)S(1)}, bf16[1,256,768]{2,1,0:T(8,128)(2,1)}, u32[]{:S(2)}) copy-start(bf16[1,256,768]{2,1,0:T(8,128)(2,1)} %param.30) | copy-start | bytes 1179652
  7.3 3.9 %copy-start.8 = (bf16[192,768]{1,0:T(8,128)(2,1)S(1)}, bf16[192,768]{1,0:T(8,128)(2,1)}, u32[]{:S(2)}) copy-start(bf16[192,768]{1,0:T(8,128)(2,1)} %refs_13_.1) | copy-start | bytes 884740
  11.0 0.7 copy-start.18
  11.0 3.7 %copy-start.4 = (bf16[1,256,768]{2,1,0:T(8,128)(2,1)S(1)}, bf16[1,256,768]{2,1,0:T(8,128)(2,1)}, u32[]{:S(2)}) copy-start(bf16[1,256,768]{2,1,0:T(8,128)(2,1)} %param.16) | copy-start | bytes 1179652
  11.0 3.7 %copy-start.5 = (f32[768]{0:T(1024)S(1)}, f32[768]{0:T(1024)}, u32[]{:S(2)}) copy-start(f32[768]{0:T(1024)} %gain_ref.7) | copy-start | bytes 9220
  11.7 21.6 %copy-start.7 = (bf16[448,768]{1,0:T(8,128)(2,1)}, bf16[448,768]{1,0:T(8,128)(2,1)S(1)}, u32[]{:S(2)}) copy-start(bf16[448,768]{1,0:T(8,128)(2,1)S(1)} %pad_maximum_fusion.refs_7_.refs_4_) | copy-start | bytes 2064388
  13.0 1.7 collective-permute-start.2
  13.0 20.3 %collective-permute-start.6 = (bf16[448,768]{1,0:T(8,128)(2,1)S(1)}, bf16[448,768]{1,0:T(8,128)(2,1)S(1)}, u32[]{:S(2)}, u32[]{:S(2)}) collective-permute-start(bf16[448,768]{1,0:T(8,128)(2,1)S(1)} %pad_maximum_fusion.refs_7_.refs_4_), channel_id=1, source_target_pairs={{0,2},{1,3},{2,0},{3,1},{4,6},{5,7},{6,4},{7,5},{8,10},{9,11},{10,... | collective-permute-start | bytes 2064392 | tf_op jit(solution)/shard_map/ppermute | solution.py:120
  14.8 30.0 %copy-start.2 = (f32[768]{0:T(1024)S(1)}, f32[768]{0:T(1024)}, u32[]{:S(2)}) copy-start(f32[768]{0:T(1024)} %gain_ref.6) | copy-start | bytes 9220
  14.8 30.0 %copy-start.3 = (s32[8]{0:T(128)S(1)}, s32[8]{0:T(128)}, u32[]{:S(2)}) copy-start(s32[8]{0:T(128)} %groups_ref.3) | copy-start | bytes 100
  31.5 11.5 %collective-permute-start.3 = (bf16[1536,128]{1,0:T(8,128)(2,1)}, bf16[1536,128]{1,0:T(8,128)(2,1)S(1)}, u32[]{:S(2)}, u32[]{:S(2)}) collective-permute-start(bf16[1536,128]{1,0:T(8,128)(2,1)} %get-tuple-element.99.refs_1_), channel_id=1, source_target_pairs={{0,2},{1,3},{2,0},{3,1},{4,6},{5,7},{6,4},{7,5},{8,10},{9,11},{10,... | collective-permute-start | bytes 1179656 | tf_op jit(solution)/shard_map/ppermute | solution.py:120
  33.3 9.8 %collective-permute-start.7 = (bf16[448,768]{1,0:T(8,128)(2,1)S(1)}, bf16[448,768]{1,0:T(8,128)(2,1)S(1)}, u32[]{:S(2)}, u32[]{:S(2)}) collective-permute-start(bf16[448,768]{1,0:T(8,128)(2,1)S(1)} %pad_maximum_fusion.refs_7_.refs_4_), channel_id=1, source_target_pairs={{0,1},{1,0},{2,3},{3,2},{4,5},{5,4},{6,7},{7,6},{8,9},{9,8},{10,11... | collective-permute-start | bytes 2064392 | tf_op jit(solution)/shard_map/ppermute | solution.py:120
  33.3 11.5 %copy-start.9 = (bf16[448,768]{1,0:T(8,128)(2,1)}, bf16[448,768]{1,0:T(8,128)(2,1)S(1)}, u32[]{:S(2)}) copy-start(bf16[448,768]{1,0:T(8,128)(2,1)S(1)} %collective-permute-done.6.refs_8_.refs_5_) | copy-start | bytes 2064388
  33.3 11.5 %collective-permute-start.8 = (bf16[448,768]{1,0:T(8,128)(2,1)S(1)}, bf16[448,768]{1,0:T(8,128)(2,1)}, u32[]{:S(2)}, u32[]{:S(2)}) collective-permute-start(bf16[448,768]{1,0:T(8,128)(2,1)S(1)} %collective-permute-done.6.refs_8_.refs_5_), channel_id=1, source_target_pairs={{0,1},{1,0},{2,3},{3,2},{4,5},{5,4},{6,7},{7,6},{8,9},{9,8},{10,11... | collective-permute-start | bytes 2064392 | tf_op jit(solution)/shard_map/ppermute | solution.py:120
  33.8 9.3 %collective-permute-start.4 = (bf16[1536,128]{1,0:T(8,128)(2,1)}, bf16[1536,128]{1,0:T(8,128)(2,1)S(1)}, u32[]{:S(2)}, u32[]{:S(2)}) collective-permute-start(bf16[1536,128]{1,0:T(8,128)(2,1)} %get-tuple-element.99.refs_1_), channel_id=1, source_target_pairs={{0,1},{1,0},{2,3},{3,2},{4,5},{5,4},{6,7},{7,6},{8,9},{9,8},{10,11... | collective-permute-start | bytes 1179656 | tf_op jit(solution)/shard_map/ppermute | solution.py:120
  43.0 1.7 collective-permute-start.5
  43.0 1.7 copy-start.10
  61.1 16.5 %collective-permute-start.11 = (bf16[768,768]{1,0:T(8,128)(2,1)}, bf16[768,768]{1,0:T(8,128)(2,1)S(1)}, u32[]{:S(2)}, u32[]{:S(2)}) collective-permute-start(bf16[768,768]{1,0:T(8,128)(2,1)} %get-tuple-element.114), channel_id=1, source_target_pairs={{0,4},{1,9},{2,6},{3,11},{4,0},{5,13},{6,2},{7,15},{8,12},{9,1},{1... | collective-permute-start | bytes 3538952 | tf_op jit(solution)/shard_map/ppermute | solution.py:156
  62.7 2.5 %collective-permute-start.9 = (bf16[512,768]{1,0:T(8,128)(2,1)}, bf16[512,768]{1,0:T(8,128)(2,1)S(1)}, u32[]{:S(2)}, u32[]{:S(2)}) collective-permute-start(bf16[512,768]{1,0:T(8,128)(2,1)} %get-tuple-element.107), channel_id=1, source_target_pairs={{0,1},{1,0},{2,3},{3,2},{4,5},{5,4},{6,7},{7,6},{8,9},{9,8},{10,11... | collective-permute-start | bytes 2359304 | tf_op jit(solution)/shard_map/ppermute | solution.py:120
  67.2 19.9 %collective-permute-start.13 = (bf16[512,768]{1,0:T(8,128)(2,1)S(1)}, bf16[512,768]{1,0:T(8,128)(2,1)S(1)}, u32[]{:S(2)}, u32[]{:S(2)}) collective-permute-start(bf16[512,768]{1,0:T(8,128)(2,1)S(1)} %get-tuple-element.121), channel_id=1, source_target_pairs={{0,2},{1,3},{2,0},{3,1},{4,6},{5,7},{6,4},{7,5},{8,10},{9,11},{10,... | collective-permute-start | bytes 2359304 | tf_op jit(solution)/shard_map/ppermute | solution.py:120
  73.8 7.9 %copy-start.17 = (bf16[256,768]{1,0:T(8,128)(2,1)S(1)}, bf16[256,768]{1,0:T(8,128)(2,1)}, u32[]{:S(2)}) copy-start(bf16[256,768]{1,0:T(8,128)(2,1)} %get-tuple-element.112) | copy-start | bytes 1179652
  73.8 7.9 %copy-start.16 = (bf16[256,768]{1,0:T(8,128)(2,1)S(1)}, bf16[256,768]{1,0:T(8,128)(2,1)}, u32[]{:S(2)}) copy-start(bf16[256,768]{1,0:T(8,128)(2,1)} %get-tuple-element.119) | copy-start | bytes 1179652
  80.1 9.9 %collective-permute-start.15 = (bf16[384,768]{1,0:T(8,128)(2,1)S(1)}, bf16[384,768]{1,0:T(8,128)(2,1)S(1)}, u32[]{:S(2)}, u32[]{:S(2)}) collective-permute-start(bf16[384,768]{1,0:T(8,128)(2,1)S(1)} %get-tuple-element.116), channel_id=1, source_target_pairs={{0,8},{1,5},{2,10},{3,7},{4,12},{5,1},{6,14},{7,3},{8,0},{9,13},{1... | collective-permute-start | bytes 1769480 | tf_op jit(solution)/shard_map/ppermute | solution.py:156
  81.7 1.7 collective-permute-start.10
  81.7 3.6 %collective-permute-start.12 = (bf16[256,768]{1,0:T(8,128)(2,1)S(1)}, bf16[256,768]{1,0:T(8,128)(2,1)S(1)}, u32[]{:S(2)}, u32[]{:S(2)}) collective-permute-start(bf16[256,768]{1,0:T(8,128)(2,1)S(1)} %copy-done.16), channel_id=1, source_target_pairs={{0,1},{1,0},{2,3},{3,2},{4,5},{5,4},{6,7},{7,6},{8,9},{9,8},{10,11... | collective-permute-start | bytes 1179656 | tf_op jit(solution)/shard_map/ppermute | solution.py:120
  89.3 5.3 %copy-start = (bf16[256,768]{1,0:T(8,128)(2,1)S(1)}, bf16[256,768]{1,0:T(8,128)(2,1)}, u32[]{:S(2)}) copy-start(bf16[256,768]{1,0:T(8,128)(2,1)} %get-tuple-element.123.refs_0_) | copy-start | bytes 1179652
  89.3 5.3 %copy-start.1 = (bf16[256,768]{1,0:T(8,128)(2,1)S(1)}, bf16[256,768]{1,0:T(8,128)(2,1)}, u32[]{:S(2)}) copy-start(bf16[256,768]{1,0:T(8,128)(2,1)} %get-tuple-element.124.refs_1_) | copy-start | bytes 1179652
  89.3 5.3 %collective-permute-start.16 = (bf16[256,768]{1,0:T(8,128)(2,1)}, bf16[256,768]{1,0:T(8,128)(2,1)S(1)}, u32[]{:S(2)}, u32[]{:S(2)}) collective-permute-start(bf16[256,768]{1,0:T(8,128)(2,1)} %get-tuple-element.124.refs_1_), channel_id=1, source_target_pairs={{0,1},{1,0},{2,3},{3,2},{4,5},{5,4},{6,7},{7,6},{8,9},{9,8},{10,11... | collective-permute-start | bytes 1179656 | tf_op jit(solution)/shard_map/ppermute | solution.py:120
  89.4 5.2 %collective-permute-start.14 = (bf16[256,768]{1,0:T(8,128)(2,1)}, bf16[256,768]{1,0:T(8,128)(2,1)S(1)}, u32[]{:S(2)}, u32[]{:S(2)}) collective-permute-start(bf16[256,768]{1,0:T(8,128)(2,1)} %get-tuple-element.123.refs_0_), channel_id=1, source_target_pairs={{0,1},{1,0},{2,3},{3,2},{4,5},{5,4},{6,7},{7,6},{8,9},{9,8},{10,11... | collective-permute-start | bytes 1179656 | tf_op jit(solution)/shard_map/ppermute | solution.py:120
  91.9 25.0 %collective-permute-start.19 = (bf16[192,768]{1,0:T(8,128)(2,1)S(1)}, bf16[192,768]{1,0:T(8,128)(2,1)S(1)}, u32[]{:S(2)}, u32[]{:S(2)}) collective-permute-start(bf16[192,768]{1,0:T(8,128)(2,1)S(1)} %get-tuple-element.127), channel_id=1, source_target_pairs={{0,16},{1,17},{2,18},{3,19},{4,20},{5,21},{6,22},{7,23},{8,24},{9,... | collective-permute-start | bytes 884744 | tf_op jit(solution)/shard_map/ppermute | solution.py:156
  115.3 3.7 %collective-permute-start.18 = (bf16[512,768]{1,0:T(8,128)(2,1)}, bf16[512,768]{1,0:T(8,128)(2,1)S(1)}, u32[]{:S(2)}, u32[]{:S(2)}) collective-permute-start(bf16[512,768]{1,0:T(8,128)(2,1)} %get-tuple-element.141), channel_id=1, source_target_pairs={{0,1},{1,0},{2,3},{3,2},{4,5},{5,4},{6,7},{7,6},{8,9},{9,8},{10,11... | collective-permute-start | bytes 2359304 | tf_op jit(solution)/shard_map/ppermute | solution.py:120
  115.4 10.7 %collective-permute-start.17 = (bf16[416,768]{1,0:T(8,128)(2,1)}, bf16[416,768]{1,0:T(8,128)(2,1)S(1)}, u32[]{:S(2)}, u32[]{:S(2)}) collective-permute-start(bf16[416,768]{1,0:T(8,128)(2,1)} %get-tuple-element.139), channel_id=1, source_target_pairs={{0,4},{1,9},{2,6},{3,11},{4,0},{5,13},{6,2},{7,15},{8,12},{9,1},{1... | collective-permute-start | bytes 1916936 | tf_op jit(solution)/shard_map/ppermute | solution.py:156
  118.7 16.7 %collective-permute-start.21 = (bf16[192,768]{1,0:T(8,128)(2,1)}, bf16[192,768]{1,0:T(8,128)(2,1)S(1)}, u32[]{:S(2)}, u32[]{:S(2)}) collective-permute-start(bf16[192,768]{1,0:T(8,128)(2,1)} %add.41.own_ref), channel_id=1, source_target_pairs={{0,16},{1,17},{2,18},{3,19},{4,20},{5,21},{6,22},{7,23},{8,24},{9,... | collective-permute-start | bytes 884744 | tf_op jit(solution)/shard_map/ppermute | solution.py:156
  128.1 9.1 %copy-start.15 = (bf16[256,768]{1,0:T(8,128)(2,1)S(1)}, bf16[256,768]{1,0:T(8,128)(2,1)}, u32[]{:S(2)}) copy-start(bf16[256,768]{1,0:T(8,128)(2,1)} %get-tuple-element.161) | copy-start | bytes 1179652
  128.1 10.8 %collective-permute-start.20 = (bf16[224,768]{1,0:T(8,128)(2,1)S(1)}, bf16[224,768]{1,0:T(8,128)(2,1)S(1)}, u32[]{:S(2)}, u32[]{:S(2)}) collective-permute-start(bf16[224,768]{1,0:T(8,128)(2,1)S(1)} %get-tuple-element.150), channel_id=1, source_target_pairs={{0,8},{1,5},{2,10},{3,7},{4,12},{5,1},{6,14},{7,3},{8,0},{9,13},{1... | collective-permute-start | bytes 1032200 | tf_op jit(solution)/shard_map/ppermute | solution.py:156
  137.2 12.1 %collective-permute-start.24 = (bf16[384,768]{1,0:T(8,128)(2,1)}, bf16[384,768]{1,0:T(8,128)(2,1)S(1)}, u32[]{:S(2)}, u32[]{:S(2)}) collective-permute-start(bf16[384,768]{1,0:T(8,128)(2,1)} %join.4.own_ref), channel_id=1, source_target_pairs={{0,8},{1,5},{2,10},{3,7},{4,12},{5,1},{6,14},{7,3},{8,0},{9,13},{1... | collective-permute-start | bytes 1769480 | tf_op jit(solution)/shard_map/ppermute | solution.py:156
  137.2 17.5 %collective-permute-start.26 = (bf16[256,768]{1,0:T(8,128)(2,1)S(1)}, bf16[256,768]{1,0:T(8,128)(2,1)S(1)}, u32[]{:S(2)}, u32[]{:S(2)}) collective-permute-start(bf16[256,768]{1,0:T(8,128)(2,1)S(1)} %copy-done.15), channel_id=1, source_target_pairs={{0,2},{1,3},{2,0},{3,1},{4,6},{5,7},{6,4},{7,5},{8,10},{9,11},{10,... | collective-permute-start | bytes 1179656 | tf_op jit(solution)/shard_map/ppermute | solution.py:120
  138.9 2.4 %copy-start.12 = (bf16[256,768]{1,0:T(8,128)(2,1)S(1)}, bf16[256,768]{1,0:T(8,128)(2,1)}, u32[]{:S(2)}) copy-start(bf16[256,768]{1,0:T(8,128)(2,1)} %add.40) | copy-start | bytes 1179652
  140.7 14.8 %copy-start.6 = (f32[768]{0:T(1024)S(1)}, f32[768]{0:T(1024)}, u32[]{:S(2)}) copy-start(f32[768]{0:T(1024)} %gain_ref.7) | copy-start | bytes 9220
  140.7 12.4 %collective-permute-start.23 = (bf16[128,768]{1,0:T(8,128)(2,1)S(1)}, bf16[128,768]{1,0:T(8,128)(2,1)S(1)}, u32[]{:S(2)}, u32[]{:S(2)}) collective-permute-start(bf16[128,768]{1,0:T(8,128)(2,1)S(1)} %get-tuple-element.154), channel_id=1, source_target_pairs={{0,16},{1,17},{2,18},{3,19},{4,20},{5,21},{6,22},{7,23},{8,24},{9,... | collective-permute-start | bytes 589832 | tf_op jit(solution)/shard_map/ppermute | solution.py:156
  141.3 17.9 %collective-permute-start.22 = (bf16[256,768]{1,0:T(8,128)(2,1)S(1)}, bf16[256,768]{1,0:T(8,128)(2,1)S(1)}, u32[]{:S(2)}, u32[]{:S(2)}) collective-permute-start(bf16[256,768]{1,0:T(8,128)(2,1)S(1)} %copy-done.12), channel_id=1, source_target_pairs={{0,2},{1,3},{2,0},{3,1},{4,6},{5,7},{6,4},{7,5},{8,10},{9,11},{10,... | collective-permute-start | bytes 1179656 | tf_op jit(solution)/shard_map/ppermute | solution.py:120
  151.5 25.3 %collective-permute-start.31 = (bf16[768,768]{1,0:T(8,128)(2,1)}, bf16[768,768]{1,0:T(8,128)(2,1)S(1)}, u32[]{:S(2)}, u32[]{:S(2)}) collective-permute-start(bf16[768,768]{1,0:T(8,128)(2,1)} %join.5.own_ref), channel_id=1, source_target_pairs={{0,4},{1,9},{2,6},{3,11},{4,0},{5,13},{6,2},{7,15},{8,12},{9,1},{1... | collective-permute-start | bytes 3538952 | tf_op jit(solution)/shard_map/ppermute | solution.py:156
  154.8 8.1 %collective-permute-start.28 = (bf16[96,768]{1,0:T(8,128)(2,1)}, bf16[96,768]{1,0:T(8,128)(2,1)S(1)}, u32[]{:S(2)}, u32[]{:S(2)}) collective-permute-start(bf16[96,768]{1,0:T(8,128)(2,1)} %get-tuple-element.162.own_ref), channel_id=1, source_target_pairs={{0,16},{1,17},{2,18},{3,19},{4,20},{5,21},{6,22},{7,23},{8,24},{9,... | collective-permute-start | bytes 442376 | tf_op jit(solution)/shard_map/ppermute | solution.py:156
  155.5 2.4 %copy-start.13 = (f32[8,768]{1,0:T(8,128)}, f32[8,768]{1,0:T(8,128)S(1)}, u32[]{:S(2)}) copy-start(f32[8,768]{1,0:T(8,128)S(1)} %slice.12.left_ref) | copy-start | bytes 73732
  155.5 2.4 %collective-permute-start.25 = (f32[8,768]{1,0:T(8,128)S(1)}, f32[8,768]{1,0:T(8,128)S(1)}, u32[]{:S(2)}, u32[]{:S(2)}) collective-permute-start(f32[8,768]{1,0:T(8,128)S(1)} %slice.12.left_ref), channel_id=1, source_target_pairs={{0,1},{1,0},{2,3},{3,2},{4,5},{5,4},{6,7},{7,6},{8,9},{9,8},{10,11... | collective-permute-start | bytes 73736 | tf_op jit(solution)/shard_map/ppermute | solution.py:120
  159.3 5.7 %copy-start.14 = (f32[8,768]{1,0:T(8,128)S(1)}, f32[8,768]{1,0:T(8,128)}, u32[]{:S(2)}) copy-start(f32[8,768]{1,0:T(8,128)} %add.42.left_ref) | copy-start | bytes 73732
  164.5 7.4 %collective-permute-start.29 = (bf16[192,768]{1,0:T(8,128)(2,1)}, bf16[192,768]{1,0:T(8,128)(2,1)S(1)}, u32[]{:S(2)}, u32[]{:S(2)}) collective-permute-start(bf16[192,768]{1,0:T(8,128)(2,1)} %join.6.own_ref), channel_id=1, source_target_pairs={{0,8},{1,5},{2,10},{3,7},{4,12},{5,1},{6,14},{7,3},{8,0},{9,13},{1... | collective-permute-start | bytes 884744 | tf_op jit(solution)/shard_map/ppermute | solution.py:156
  165.0 3.8 %collective-permute-start.27 = (f32[8,768]{1,0:T(8,128)S(1)}, f32[8,768]{1,0:T(8,128)S(1)}, u32[]{:S(2)}, u32[]{:S(2)}) collective-permute-start(f32[8,768]{1,0:T(8,128)S(1)} %copy-done.14), channel_id=1, source_target_pairs={{0,2},{1,3},{2,0},{3,1},{4,6},{5,7},{6,4},{7,5},{8,10},{9,11},{10,... | collective-permute-start | bytes 73736 | tf_op jit(solution)/shard_map/ppermute | solution.py:120
  173.6 10.1 %collective-permute-start.30 = (bf16[384,768]{1,0:T(8,128)(2,1)}, bf16[384,768]{1,0:T(8,128)(2,1)S(1)}, u32[]{:S(2)}, u32[]{:S(2)}) collective-permute-start(bf16[384,768]{1,0:T(8,128)(2,1)} %join.7.own_ref), channel_id=1, source_target_pairs={{0,4},{1,9},{2,6},{3,11},{4,0},{5,13},{6,2},{7,15},{8,12},{9,1},{1... | collective-permute-start | bytes 1769480 | tf_op jit(solution)/shard_map/ppermute | solution.py:156
